TPU v7x, 32 devices: a whole 2x2x4 slice. The times are simulated.
32 devices in a mesh: dp: 4 (over y, x), context: 2 (over core), tensor: 4 (over z).
Axes of the slice: x: 2, y: 2, z: 4, core: 2. Of those that a mesh axis runs over, the one named last changes fastest.
Arguments:
- inputs: bfloat16 [4096, 2048], P(('dp', 'context')), may hold values from -6 to 6
- cotangent: bfloat16 [4096, 2048], P(('dp', 'context')), may hold values from -6 to 6
- doc_lengths: int32 [4, 8], P('dp'), may hold values from 1 to 512, 1024 in all within a row
- gain_attn: float32 [2048], P(('dp', 'context')), may hold values from 0.5 to 1.5
- w_query: float32 [2048, 2048], P(('dp', 'context'), 'tensor'), may hold values from -0.125 to 0.125
- w_key: float32 [2048, 512], P(('dp', 'context'), 'tensor'), may hold values from -0.125 to 0.125
- w_value: float32 [2048, 512], P(('dp', 'context'), 'tensor'), may hold values from -0.125 to 0.125
- w_out: float32 [2048, 2048], P('tensor', ('dp', 'context')), may hold values from -0.375 to 0.375
- gain_mlp: float32 [2048], P(('dp', 'context')), may hold values from 0.5 to 1.5
- w_gate: float32 [2048, 8192], P(('dp', 'context'), 'tensor'), may hold values from -0.125 to 0.125
- w_up: float32 [2048, 8192], P(('dp', 'context'), 'tensor'), may hold values from -0.125 to 0.125
- w_down: float32 [8192, 2048], P('tensor', ('dp', 'context')), may hold values from -0.0625 to 0.0625
Outputs:
- activations: bfloat16 [4096, 2048], P(('dp', 'context'))
- input_grad: float32 [4096, 2048], P(('dp', 'context'))
- grad_gain_attn: float32 [2048], P(('dp', 'context'))
- grad_query: float32 [2048, 2048], P(('dp', 'context'), 'tensor')
- grad_key: float32 [2048, 512], P(('dp', 'context'), 'tensor')
- grad_value: float32 [2048, 512], P(('dp', 'context'), 'tensor')
- grad_out: float32 [2048, 2048], P('tensor', ('dp', 'context'))
- grad_gain_mlp: float32 [2048], P(('dp', 'context'))
- grad_gate: float32 [2048, 8192], P(('dp', 'context'), 'tensor')
- grad_up: float32 [2048, 8192], P(('dp', 'context'), 'tensor')
- grad_down: float32 [8192, 2048], P('tensor', ('dp', 'context'))
Inputs may be any that keep to these rules, and one draw needn't show every extreme that they name: `doc_lengths`: each row lists the lengths of one sequence's 8 documents in order; they sum to 1024, and the longest is exactly 512.
All inputs are finite; a program needn't handle non-finite values.
Results may differ from a plain program's by a relative error of at most 0.014.
The roundings to bfloat16 on the way count: a program that leaves them out, or rounds other values in their place, can miss the bound.
Values may be sent and summed in bfloat16 or wider, within the bound.
A program may use at most 256 MiB of HBM per device.

v0:
```python
import math

import jax
import jax.numpy as jnp
from jax import lax
from jax.sharding import PartitionSpec as P

HD = 64


EPSILON = 1e-05
NEGATIVE = -1e30


def frequencies():
    exponent = jnp.arange(0, HD, 2).astype(jnp.float32) / HD
    initial = 1.0 / 500000.0**exponent
    wavelength = 2.0 * math.pi / initial
    smoothing = (8192.0 / wavelength - 1.0) / 3.0
    blended = (1.0 - smoothing) * initial / 32.0 + smoothing * initial
    return jnp.where(
        wavelength < 2048.0, initial, jnp.where(wavelength > 8192.0, initial / 32.0, blended)
    )


def rope_tables(position):
    angles = position.astype(jnp.float32)[:, None] * frequencies()[None, :]
    cosine = jnp.cos(angles)
    sine_part = jnp.sin(angles)
    return (jnp.concatenate([cosine, cosine], -1), jnp.concatenate([sine_part, sine_part], -1))


def rotate(values, cosine, sine_part):
    middle = values.shape[-1] // 2
    turned = jnp.concatenate([-values[..., middle:], values[..., :middle]], -1)
    return values * cosine[:, None, :] + turned * sine_part[:, None, :]


def unrotate(values, cosine, sine_part):
    middle = values.shape[-1] // 2
    scaled = values * sine_part[:, None, :]
    turned = jnp.concatenate([scaled[..., middle:], -scaled[..., :middle]], -1)
    return values * cosine[:, None, :] + turned


def documents(lengths_row, seq_total):
    doc_ends = jnp.cumsum(lengths_row)
    doc_starts = doc_ends - lengths_row
    token_index = jnp.arange(seq_total, dtype=jnp.int32)
    segment = jnp.sum((token_index[:, None] >= doc_ends[None, :]).astype(jnp.int32), 1)
    member = segment[:, None] == jnp.arange(lengths_row.shape[0], dtype=jnp.int32)[None, :]
    position = token_index - jnp.sum(jnp.where(member, doc_starts[None, :], 0), 1)
    return (segment, position)


def norm_forward(source, gain_vector):
    rscale = lax.rsqrt(jnp.mean(source * source, -1, keepdims=True) + EPSILON)
    scaled = source * rscale
    return ((scaled * gain_vector).astype(jnp.bfloat16), scaled, rscale)


def norm_backward(grad_normed, scaled, rscale, gain_vector):
    gain_grad = jnp.sum(grad_normed * scaled, 0)
    grad_scaled = grad_normed * gain_vector
    grad_source = rscale * (
        grad_scaled - scaled * jnp.mean(grad_scaled * scaled, -1, keepdims=True)
    )
    return (grad_source, gain_grad)


def block_scores(query_blk, first_row, keys_all, segment):
    length = query_blk.shape[0]
    row_ids = first_row + jnp.arange(length, dtype=jnp.int32)
    columns = jnp.arange(keys_all.shape[0], dtype=jnp.int32)
    seg_rows = lax.dynamic_slice_in_dim(segment, first_row, length, 0)
    allowed = (seg_rows[:, None] == segment[None, :]) & (columns[None, :] <= row_ids[:, None])
    scores = jnp.einsum(
        "bkgd,lkd->kgbl", query_blk, keys_all, preferred_element_type=jnp.float32
    ) * HD ** (-0.5)
    return jnp.where(allowed, scores, NEGATIVE)


def shards(
    inputs,
    cotangent,
    doc_lengths,
    gain_attn,
    w_query,
    w_key,
    w_value,
    w_out,
    gain_mlp,
    w_gate,
    w_up,
    w_down,
):
    tokens_here = inputs.shape[0]
    offset = lax.axis_index("context") * tokens_here
    segment, position = documents(doc_lengths[0], tokens_here * lax.axis_size("context"))
    cosine, sine_part = rope_tables(lax.dynamic_slice_in_dim(position, offset, tokens_here, 0))
    heads_here = w_query.shape[1] // HD
    groups_here = w_key.shape[1] // HD
    per_group = heads_here // groups_here
    block_rows = min(512, tokens_here)
    blocks = tokens_here // block_rows
    scale_factor = HD ** (-0.5)
    attention_copy = (
        gain_attn.astype(jnp.bfloat16),
        w_query.astype(jnp.bfloat16),
        w_key.astype(jnp.bfloat16),
        w_value.astype(jnp.bfloat16),
        w_out.astype(jnp.bfloat16),
    )
    mlp_copy = (
        gain_mlp.astype(jnp.bfloat16),
        w_gate.astype(jnp.bfloat16),
        w_up.astype(jnp.bfloat16),
        w_down.astype(jnp.bfloat16),
    )
    gain_one, query_full, key_full, value_full, out_full = (
        lax.all_gather(attention_copy[0], ("dp", "context"), axis=0, tiled=True),
        lax.all_gather(attention_copy[1], ("dp", "context"), axis=0, tiled=True),
        lax.all_gather(attention_copy[2], ("dp", "context"), axis=0, tiled=True),
        lax.all_gather(attention_copy[3], ("dp", "context"), axis=0, tiled=True),
        lax.all_gather(attention_copy[4], ("dp", "context"), axis=1, tiled=True),
    )
    gain_one_f = gain_one.astype(jnp.float32)
    source = inputs.astype(jnp.float32)
    grad_output = cotangent.astype(jnp.float32)
    normed, scaled_one, rscale_one = norm_forward(source, gain_one_f)
    queries = jnp.dot(normed, query_full, preferred_element_type=jnp.float32).reshape(
        tokens_here, heads_here, HD
    )
    queries = rotate(queries, cosine, sine_part).astype(jnp.bfloat16)
    keys_here = jnp.dot(normed, key_full, preferred_element_type=jnp.float32).reshape(
        tokens_here, groups_here, HD
    )
    keys_here = rotate(keys_here, cosine, sine_part).astype(jnp.bfloat16)
    values_here = (
        jnp.dot(normed, value_full, preferred_element_type=jnp.float32)
        .astype(jnp.bfloat16)
        .reshape(tokens_here, groups_here, HD)
    )
    keys_all, values_all = (
        lax.all_gather(keys_here, "context", axis=0, tiled=True),
        lax.all_gather(values_here, "context", axis=0, tiled=True),
    )
    query_blocks = queries.reshape(blocks, block_rows, groups_here, per_group, HD)
    block_starts = offset + jnp.arange(blocks, dtype=jnp.int32) * block_rows

    def forward_block(block_items):
        query_blk, first_row = block_items
        scores = block_scores(query_blk, first_row, keys_all, segment)
        highest = jnp.max(scores, -1, keepdims=True)
        raw_weights = jnp.exp(scores - highest)
        totals = jnp.sum(raw_weights, -1, keepdims=True)
        soft_weights = (raw_weights / totals).astype(jnp.bfloat16)
        mixed_blk = jnp.einsum(
            "kgbl,lkd->bkgd", soft_weights, values_all, preferred_element_type=jnp.float32
        )
        return (mixed_blk.astype(jnp.bfloat16), highest[..., 0] + jnp.log(totals[..., 0]))

    mixed_blocks, log_totals = lax.map(forward_block, (query_blocks, block_starts))
    mixed_heads = mixed_blocks.reshape(tokens_here, heads_here * HD)
    attention_terms = jnp.dot(mixed_heads, out_full, preferred_element_type=jnp.float32)
    gain_two, gate_full, up_full, down_full = (
        lax.all_gather(mlp_copy[0], ("dp", "context"), axis=0, tiled=True),
        lax.all_gather(mlp_copy[1], ("dp", "context"), axis=0, tiled=True),
        lax.all_gather(mlp_copy[2], ("dp", "context"), axis=0, tiled=True),
        lax.all_gather(mlp_copy[3], ("dp", "context"), axis=1, tiled=True),
    )
    gain_two_f = gain_two.astype(jnp.float32)
    branch = lax.psum(attention_terms, "tensor")
    hidden_state = source + branch
    normed_mlp, scaled_two, rscale_two = norm_forward(hidden_state, gain_two_f)
    gate_value = jnp.dot(normed_mlp, gate_full, preferred_element_type=jnp.float32)
    upward = jnp.dot(normed_mlp, up_full, preferred_element_type=jnp.float32)
    sigmoid_gate = jax.nn.sigmoid(gate_value)
    swish_gate = gate_value * sigmoid_gate
    activated = (swish_gate * upward).astype(jnp.bfloat16)
    mlp_terms = jnp.dot(activated, down_full, preferred_element_type=jnp.float32)
    mlp_branch = lax.psum(mlp_terms.astype(jnp.bfloat16), "tensor").astype(jnp.float32)
    activations = (hidden_state + mlp_branch).astype(jnp.bfloat16)
    grad_down = jnp.einsum("tf,td->fd", activated, cotangent, preferred_element_type=jnp.float32)
    grad_activated = jnp.einsum(
        "td,fd->tf", cotangent, down_full, preferred_element_type=jnp.float32
    )
    grad_gate_in = (
        grad_activated * upward * sigmoid_gate * (1.0 + gate_value * (1.0 - sigmoid_gate))
    ).astype(jnp.bfloat16)
    grad_upward = (grad_activated * swish_gate).astype(jnp.bfloat16)
    grad_gate = jnp.einsum(
        "td,tf->df", normed_mlp, grad_gate_in, preferred_element_type=jnp.float32
    )
    grad_up = jnp.einsum("td,tf->df", normed_mlp, grad_upward, preferred_element_type=jnp.float32)
    partial_two = jnp.einsum(
        "tf,df->td", grad_gate_in, gate_full, preferred_element_type=jnp.float32
    )
    partial_two = partial_two + jnp.einsum(
        "tf,df->td", grad_upward, up_full, preferred_element_type=jnp.float32
    )
    grad_normed_mlp = lax.psum(partial_two, "tensor")
    grad_hidden, gain_grad_two = norm_backward(grad_normed_mlp, scaled_two, rscale_two, gain_two_f)
    grad_hidden = grad_hidden + grad_output
    grad_branch = grad_hidden.astype(jnp.bfloat16)
    grad_gate_own, grad_up_own, grad_down_own = (
        lax.psum_scatter(grad_gate, ("dp", "context"), scatter_dimension=0, tiled=True),
        lax.psum_scatter(grad_up, ("dp", "context"), scatter_dimension=0, tiled=True),
        lax.psum_scatter(grad_down, ("dp", "context"), scatter_dimension=1, tiled=True),
    )
    grad_out = jnp.einsum("te,td->ed", mixed_heads, grad_branch, preferred_element_type=jnp.float32)
    grad_mixed = jnp.einsum(
        "td,ed->te", grad_branch, out_full, preferred_element_type=jnp.float32
    ).astype(jnp.bfloat16)
    grad_mixed_blocks = grad_mixed.reshape(blocks, block_rows, groups_here, per_group, HD)

    def backward_block(running, block_items):
        key_acc, value_acc = running
        query_blk, first_row, grad_blk, log_blk = block_items
        scores = block_scores(query_blk, first_row, keys_all, segment)
        soft_weights = jnp.exp(scores - log_blk[..., None])
        dprobs = jnp.einsum(
            "bkgd,lkd->kgbl", grad_blk, values_all, preferred_element_type=jnp.float32
        )
        row_delta = jnp.sum(soft_weights * dprobs, -1, keepdims=True)
        dscores = (soft_weights * (dprobs - row_delta)).astype(jnp.bfloat16)
        dquery = (
            jnp.einsum("kgbl,lkd->bkgd", dscores, keys_all, preferred_element_type=jnp.float32)
            * scale_factor
        )
        key_acc = (
            key_acc
            + jnp.einsum("kgbl,bkgd->lkd", dscores, query_blk, preferred_element_type=jnp.float32)
            * scale_factor
        )
        value_acc = value_acc + jnp.einsum(
            "kgbl,bkgd->lkd",
            soft_weights.astype(jnp.bfloat16),
            grad_blk,
            preferred_element_type=jnp.float32,
        )
        return ((key_acc, value_acc), dquery)

    zero_keys = jnp.zeros(keys_all.shape, jnp.float32)
    (key_acc, value_acc), dquery_blocks = lax.scan(
        backward_block,
        (zero_keys, zero_keys),
        (query_blocks, block_starts, grad_mixed_blocks, log_totals),
    )
    key_grad, value_grad = (
        lax.psum_scatter(key_acc, "context", scatter_dimension=0, tiled=True),
        lax.psum_scatter(value_acc, "context", scatter_dimension=0, tiled=True),
    )
    grad_key_in = (
        unrotate(key_grad, cosine, sine_part)
        .astype(jnp.bfloat16)
        .reshape(tokens_here, groups_here * HD)
    )
    grad_value_in = value_grad.astype(jnp.bfloat16).reshape(tokens_here, groups_here * HD)
    grad_query_in = (
        unrotate(dquery_blocks.reshape(tokens_here, heads_here, HD), cosine, sine_part)
        .astype(jnp.bfloat16)
        .reshape(tokens_here, heads_here * HD)
    )
    grad_query = jnp.einsum("td,te->de", normed, grad_query_in, preferred_element_type=jnp.float32)
    grad_key = jnp.einsum("td,te->de", normed, grad_key_in, preferred_element_type=jnp.float32)
    grad_value = jnp.einsum("td,te->de", normed, grad_value_in, preferred_element_type=jnp.float32)
    partial_one = jnp.einsum(
        "te,de->td", grad_query_in, query_full, preferred_element_type=jnp.float32
    )
    partial_one = partial_one + jnp.einsum(
        "te,de->td", grad_key_in, key_full, preferred_element_type=jnp.float32
    )
    partial_one = partial_one + jnp.einsum(
        "te,de->td", grad_value_in, value_full, preferred_element_type=jnp.float32
    )
    grad_normed = lax.psum(partial_one, "tensor")
    grad_source, gain_grad_one = norm_backward(grad_normed, scaled_one, rscale_one, gain_one_f)
    input_grad = grad_source + grad_hidden
    gain_total_one, gain_total_two = (gain_grad_one, gain_grad_two)
    grad_gain_attn, grad_gain_mlp, grad_query_own, grad_key_own, grad_value_own, grad_out_own = (
        lax.psum_scatter(gain_total_one, ("dp", "context"), scatter_dimension=0, tiled=True),
        lax.psum_scatter(gain_total_two, ("dp", "context"), scatter_dimension=0, tiled=True),
        lax.psum_scatter(grad_query, ("dp", "context"), scatter_dimension=0, tiled=True),
        lax.psum_scatter(grad_key, ("dp", "context"), scatter_dimension=0, tiled=True),
        lax.psum_scatter(grad_value, ("dp", "context"), scatter_dimension=0, tiled=True),
        lax.psum_scatter(grad_out, ("dp", "context"), scatter_dimension=1, tiled=True),
    )
    return (
        activations,
        input_grad,
        grad_gain_attn,
        grad_query_own,
        grad_key_own,
        grad_value_own,
        grad_out_own,
        grad_gain_mlp,
        grad_gate_own,
        grad_up_own,
        grad_down_own,
    )


def solution(mesh):
    return jax.shard_map(
        shards,
        mesh=mesh,
        in_specs=(
            P(("dp", "context"), None),
            P(("dp", "context"), None),
            P("dp", None),
            P(("dp", "context")),
            P(("dp", "context"), "tensor"),
            P(("dp", "context"), "tensor"),
            P(("dp", "context"), "tensor"),
            P("tensor", ("dp", "context")),
            P(("dp", "context")),
            P(("dp", "context"), "tensor"),
            P(("dp", "context"), "tensor"),
            P("tensor", ("dp", "context")),
        ),
        out_specs=(
            P(("dp", "context"), None),
            P(("dp", "context"), None),
            P(("dp", "context")),
            P(("dp", "context"), "tensor"),
            P(("dp", "context"), "tensor"),
            P(("dp", "context"), "tensor"),
            P("tensor", ("dp", "context")),
            P(("dp", "context")),
            P(("dp", "context"), "tensor"),
            P(("dp", "context"), "tensor"),
            P("tensor", ("dp", "context")),
        ),
        check_vma=False,
    )
```

profile of v0, /device:TPU:0, one launch (start us, length us, event | category | flops | bytes accessed | tf_op | source)
XLA Modules:
  0.0 1470.6 jit_solution(9530350730254042631)
XLA Ops:
  7.2 1.8 convert_element_type.132
  9.2 1.8 convert_element_type.137
  13.2 2.1 fusion.19
  15.7 10.3 all-gather
  26.1 11.0 all_gather.34
  37.1 8.7 all_gather.36
  45.8 2.3 fusion.13
  49.0 2.1 all_gather.35
  52.4 2.7 all_gather.37
  55.6 2.9 fusion.48
  59.4 7.5 fusion.46
  66.9 8.2 fusion.3
  75.1 7.4 fusion.22
  82.6 5.1 fusion.49
  89.0 2.9 convert_element_type.141
  91.9 2.7 convert_element_type.144
  94.7 9.1 all-gather.1
  103.8 139.4 %all-reduce.8.cloned.1.call-done = f32[512,2048]{1,0:T(8,128)} async-done(((f32[512,2048]{1,0:T(8,128)}), f32[512,2048]{1,0:T(8,128)}) %all-reduce.8.cloned.1.call-update) | async-done | bytes 4194320 | tf_op jit(solution)/shard_map/psum | solution.py:173
  243.2 2.8 multiply_reduce_fusion.2
  246.0 1.9 copy-done.3
  248.4 50.7 %all-gather.14.cloned.1.call-done = bf16[2048,2048]{1,0:T(8,128)(2,1)} async-done(((bf16[256,2048]{1,0:T(8,128)(2,1)}), bf16[2048,2048]{1,0:T(8,128)(2,1)}) %all-gather.14.cloned.1.call-update) | async-done | bytes 8388624 | tf_op jit(solution)/shard_map/all_gather | solution.py:169
  299.1 9.6 fusion.51
  308.7 47.3 %all-gather.12.cloned.1.call-done = bf16[2048,2048]{1,0:T(8,128)(2,1)} async-done(((bf16[256,2048]{1,0:T(8,128)(2,1)}), bf16[2048,2048]{1,0:T(8,128)(2,1)}) %all-gather.12.cloned.1.call-update) | async-done | bytes 8388624 | tf_op jit(solution)/shard_map/all_gather | solution.py:168
  356.0 10.5 fusion.50
  366.5 47.9 %all-gather.16.cloned.1.call-done = bf16[2048,2048]{1,0:T(8,128)(2,1)} async-done(((bf16[2048,256]{1,0:T(8,128)(2,1)}), bf16[2048,2048]{1,0:T(8,128)(2,1)}) %all-gather.16.cloned.1.call-update) | async-done | bytes 8388624 | tf_op jit(solution)/shard_map/all_gather | solution.py:170
  414.5 11.7 multiply_convert_fusion
  426.2 8.5 fusion.52
  434.7 9.5 convolution_add_fusion
  444.5 9.8 convolution_convert_fusion
  454.5 144.9 %all-reduce.12.cloned.1.call-done = f32[512,2048]{1,0:T(8,128)} async-done(((f32[512,2048]{1,0:T(8,128)}), f32[512,2048]{1,0:T(8,128)}) %all-reduce.12.cloned.1.call-update) | async-done | bytes 4194320 | tf_op jit(solution)/shard_map/psum | solution.py:202
  599.4 4.4 multiply_reduce_fusion
  603.8 84.0 %all-reduce.10.cloned.1.call-done = bf16[512,2048]{1,0:T(8,128)(2,1)} async-done(((bf16[512,2048]{1,0:T(8,128)(2,1)}), bf16[512,2048]{1,0:T(8,128)(2,1)}) %all-reduce.10.cloned.1.call-update) | async-done | bytes 2097168 | tf_op jit(solution)/shard_map/psum | solution.py:182
  687.9 6.1 convert_add_fusion.1
  696.0 15.1 %fusion = (f32[2,4,512]{2,1,0:T(4,128)S(1)}, f32[2,1024,512,4]{2,1,3,0:T(8,128)}) fusion(f32[2,4,512,1024]{2,3,1,0:T(8,128)} %get-tuple-element.92, f32[2,4,512]{2,1,0:T(4,128)S(1)} %bitcast.147, bf16[512,2,4,64]{0,3,2,1:T(8,128)(2,1)S(1)} %bitcast.138, bf16[1024,2,64]{0,2,1:T(8,128)(2,1)S(1)} %copy-done.24), kind=kOutput, calls=%fused_computation.2 | convolution fusion | flops 549449728 | bytes 34373632 | tf_op jit(solution)/shard_map/while/body/eval_jaxpr/bkgd,lkd->kgbl/dot_general | solution.py:222
  711.2 1.4 slice-done.3
  712.6 7.8 fusion.2
  720.5 3.3 copy-done.2
  723.7 3.4 fusion.27
  727.2 4.9 convolution_multiply_fusion
  733.3 9.5 fusion.23
  742.8 4.9 fusion.53
  749.8 2.7 fusion.54
  753.5 6.2 add_add_fusion
  759.7 1.5 copy-done.1
  761.2 1.7 fusion.57
  763.0 1.7 fusion.56
  764.8 5.7 fusion.32
  770.6 3.3 fusion.55
  774.0 1.5 copy-done.18
  775.6 9.7 fusion.60
  785.5 1.4 copy-done.20
  786.8 9.8 fusion.59
  796.7 9.8 fusion.58
  808.4 106.1 %all-reduce.14.cloned.1.call-done = f32[512,2048]{1,0:T(8,128)} async-done(((f32[512,2048]{1,0:T(8,128)}), f32[512,2048]{1,0:T(8,128)}) %all-reduce.14.cloned.1.call-update) | async-done | bytes 4194320 | tf_op jit(solution)/shard_map/psum | solution.py:277
  914.5 3.3 fusion.18
  917.8 24.2 %all-reduce.2 = (f32[2048]{0:T(1024)S(1)}, f32[2048]{0:T(1024)S(1)}) all-reduce(f32[2048]{0:T(1024)S(1)} %get-tuple-element.59, f32[2048]{0:T(1024)S(1)} %get-tuple-element.57), channel_id=4, replica_groups=mesh['dp'=4,'context'=2,'tensor'=4] {'dp','context'}, use_global_device_ids=true, to_apply=%region_17.18.clone | all-reduce | flops 4096 | bytes 32768
  943.3 6.6 fusion.17
  949.8 3.3 reduce-scatter.18.cloned.1.call-done
  953.2 39.8 %reduce-scatter.16.cloned.1.call-done = f32[256,128]{1,0:T(8,128)} async-done(((f32[2048,128]{1,0:T(8,128)}), f32[256,128]{1,0:T(8,128)}) %reduce-scatter.16.cloned.1.call-update) | async-done | bytes 131088 | tf_op jit(solution)/shard_map/reduce_scatter | solution.py:285
  992.9 55.1 %reduce-scatter.20.cloned.1.call-done = f32[512,256]{1,0:T(8,128)} async-done(((f32[512,2048]{1,0:T(8,128)}), f32[512,256]{1,0:T(8,128)}) %reduce-scatter.20.cloned.1.call-update) | async-done | bytes 524304 | tf_op jit(solution)/shard_map/reduce_scatter | solution.py:287
  1048.1 55.5 %reduce-scatter.14.cloned.1.call-done = f32[256,512]{1,0:T(8,128)} async-done(((f32[2048,512]{1,0:T(8,128)}), f32[256,512]{1,0:T(8,128)}) %reduce-scatter.14.cloned.1.call-update) | async-done | bytes 524304 | tf_op jit(solution)/shard_map/reduce_scatter | solution.py:284
  1103.6 120.0 %reduce-scatter.26.cloned.1.call-done = f32[2048,256]{1,0:T(8,128)} async-done(((f32[2048,2048]{1,0:T(8,128)}), f32[2048,256]{1,0:T(8,128)}) %reduce-scatter.26.cloned.1.call-update) | async-done | bytes 2097168 | tf_op jit(solution)/shard_map/reduce_scatter | solution.py:209
  1223.6 120.0 %reduce-scatter.24.cloned.1.call-done = f32[256,2048]{1,0:T(8,128)} async-done(((f32[2048,2048]{1,0:T(8,128)}), f32[256,2048]{1,0:T(8,128)}) %reduce-scatter.24.cloned.1.call-update) | async-done | bytes 2097168 | tf_op jit(solution)/shard_map/reduce_scatter | solution.py:208
  1343.5 120.0 %reduce-scatter.22.cloned.1.call-done = f32[256,2048]{1,0:T(8,128)} async-done(((f32[2048,2048]{1,0:T(8,128)}), f32[256,2048]{1,0:T(8,128)}) %reduce-scatter.22.cloned.1.call-update) | async-done | bytes 2097168 | tf_op jit(solution)/shard_map/reduce_scatter | solution.py:207
  (158 shorter events, 17.7 us)
Async XLA Ops:
  7.2 18.8 %copy-start.27 = (f32[256,128]{1,0:T(8,128)S(1)}, f32[256,128]{1,0:T(8,128)}, u32[]{:S(2)}) copy-start(f32[256,128]{1,0:T(8,128)} %param.17) | copy-start | bytes 393220
  7.2 18.9 %copy-start.28 = (f32[256,128]{1,0:T(8,128)S(1)}, f32[256,128]{1,0:T(8,128)}, u32[]{:S(2)}) copy-start(f32[256,128]{1,0:T(8,128)} %param.18) | copy-start | bytes 393220
  7.2 48.4 %all-gather.8.cloned.1.call-start = ((), (), s32[]{:S(2)}) async-start(), calls=%async_computation.9 | async-start | bytes 2359296 | tf_op jit(solution)/shard_map/all_gather | solution.py:122
  9.1 73.5 %all-gather.10.cloned.1.call-start = ((), (), s32[]{:S(2)}) async-start(), calls=%async_computation.10 | async-start | bytes 2359296 | tf_op jit(solution)/shard_map/all_gather | solution.py:125
  10.9 232.3 %all-reduce.8.cloned.1.call-start = ((), (), s32[]{:S(2)}) async-start(), calls=%async_computation.11 | async-start | bytes 8388608 | tf_op jit(solution)/shard_map/psum | solution.py:173
  15.3 33.7 %copy-start.29 = (f32[512]{0:T(512)}, f32[512]{0:T(512)S(1)}, u32[]{:S(2)}) copy-start(f32[512]{0:T(512)S(1)} %add_rsqrt_fusion.1) | copy-start | bytes 6148
  26.0 23.0 %copy-start.25 = (f32[8,1,256]{2,1,0:T(1,128)}, f32[8,1,256]{2,1,0:T(1,128)S(1)}, u32[]{:S(2)}) copy-start(f32[8,1,256]{2,1,0:T(1,128)S(1)} %convert_element_type.158) | copy-start | bytes 24580
  37.1 14.9 %copy-start.7 = (bf16[2048,128]{1,0:T(8,128)(2,1)}, bf16[2048,128]{1,0:T(8,128)(2,1)S(1)}, u32[]{:S(2)}) copy-start(bf16[2048,128]{1,0:T(8,128)(2,1)S(1)} %all_gather.34) | copy-start | bytes 1572868
  45.8 6.2 copy-start.9
  48.1 7.4 copy-start
  58.5 1.0 copy-start.13
  66.9 8.2 copy-start.23
  82.5 5.2 copy-start.11
  82.6 5.2 copy-start.21
  87.7 211.4 %all-gather.14.cloned.1.call-start = ((), (), s32[]{:S(2)}) async-start(), calls=%async_computation.13 | async-start | bytes 9437184 | tf_op jit(solution)/shard_map/all_gather | solution.py:169
  88.9 5.8 copy-start.31
  88.9 154.3 %copy-start.4 = (bf16[512,2048]{1,0:T(8,128)(2,1)S(1)}, bf16[512,2048]{1,0:T(8,128)(2,1)}, u32[]{:S(2)}) copy-start(bf16[512,2048]{1,0:T(8,128)(2,1)} %param.12) | copy-start | bytes 6291460
  88.9 267.1 %all-gather.12.cloned.1.call-start = ((), (), s32[]{:S(2)}) async-start(), calls=%async_computation.12 | async-start | bytes 9437184 | tf_op jit(solution)/shard_map/all_gather | solution.py:168
  91.8 322.6 %all-gather.16.cloned.1.call-start = ((), (), s32[]{:S(2)}) async-start(), calls=%async_computation.14 | async-start | bytes 9437184 | tf_op jit(solution)/shard_map/all_gather | solution.py:170
  94.6 504.8 %all-reduce.12.cloned.1.call-start = ((), (), s32[]{:S(2)}) async-start(), calls=%async_computation.16 | async-start | bytes 8388608 | tf_op jit(solution)/shard_map/psum | solution.py:202
  246.0 2.0 copy-start.3
  248.4 50.7 %copy-start.19 = (bf16[512,2048]{1,0:T(8,128)(2,1)}, bf16[512,2048]{1,0:T(8,128)(2,1)S(1)}, u32[]{:S(2)}) copy-start(bf16[512,2048]{1,0:T(8,128)(2,1)S(1)} %multiply_convert_fusion.3) | copy-start | bytes 6291460
  308.7 105.8 %copy-start.17 = (bf16[512,2048]{1,0:T(8,128)(2,1)S(1)}, bf16[512,2048]{1,0:T(8,128)(2,1)}, u32[]{:S(2)}) copy-start(bf16[512,2048]{1,0:T(8,128)(2,1)} %param.13) | copy-start | bytes 6291460
  426.2 8.5 copy-start.33
  426.2 8.5 copy-start.34
  444.3 243.6 %all-reduce.10.cloned.1.call-start = ((), (), s32[]{:S(2)}) async-start(), calls=%async_computation.15 | async-start | bytes 4194304 | tf_op jit(solution)/shard_map/psum | solution.py:182
  454.4 293.3 %reduce-scatter.10.cloned.1.call-start = ((), (), s32[]{:S(2)}) async-start(), calls=%async_computation.17 | async-start | bytes 786432 | tf_op jit(solution)/shard_map/reduce_scatter | solution.py:251
  687.9 6.1 copy-start.22
  694.0 2.0 copy-start.6
  694.0 2.0 copy-start.24
  696.0 15.1 %copy-start.15 = (bf16[512,512]{0,1:T(8,128)(2,1)}, bf16[512,512]{0,1:T(8,128)(2,1)S(1)}, u32[]{:S(2)}) copy-start(bf16[512,512]{0,1:T(8,128)(2,1)S(1)} %convolution_convert_fusion.1) | copy-start | bytes 1572868
  696.0 15.1 %slice-start = ((s8[16777216]{0:T(1024)(128)(4,1)}), s8[4194304]{0:T(1024)(128)(4,1)S(1)}, s32[]{:S(2)}) async-start(s8[16777216]{0:T(1024)(128)(4,1)} %bitcast.130), calls=%async_computation.27 | async-start | bytes 8388608
  696.0 15.1 %slice-start.1 = ((s8[16777216]{0:T(1024)(128)(4,1)}), s8[4194304]{0:T(1024)(128)(4,1)S(1)}, s32[]{:S(2)}) async-start(s8[16777216]{0:T(1024)(128)(4,1)} %bitcast.130), calls=%async_computation.28 | async-start | bytes 8388608
  696.0 15.1 %slice-start.2 = ((s8[16777216]{0:T(1024)(128)(4,1)}), s8[4194304]{0:T(1024)(128)(4,1)S(1)}, s32[]{:S(2)}) async-start(s8[16777216]{0:T(1024)(128)(4,1)} %bitcast.130), calls=%async_computation.29 | async-start | bytes 8388608
  696.0 16.6 %slice-start.3 = ((s8[16777216]{0:T(1024)(128)(4,1)}), s8[4194304]{0:T(1024)(128)(4,1)S(1)}, s32[]{:S(2)}) async-start(s8[16777216]{0:T(1024)(128)(4,1)} %bitcast.130), calls=%async_computation.30 | async-start | bytes 8388608
  720.4 3.3 copy-start.2
  723.7 3.4 copy-start.14
  732.1 1.1 copy-start.16
  732.1 20.4 %reduce-scatter.12.cloned.1.call-start = ((), (), s32[]{:S(2)}) async-start(), calls=%async_computation.18 | async-start | bytes 786432 | tf_op jit(solution)/shard_map/reduce_scatter | solution.py:252
  742.7 7.1 copy-start.10
  742.8 171.7 %all-reduce.14.cloned.1.call-start = ((), (), s32[]{:S(2)}) async-start(), calls=%async_computation.19 | async-start | bytes 8388608 | tf_op jit(solution)/shard_map/psum | solution.py:277
  747.7 5.8 copy-start.8
  759.7 1.6 copy-start.1
  759.7 193.5 %reduce-scatter.18.cloned.1.call-start = ((), (), s32[]{:S(2)}) async-start(), calls=%async_computation.22 | async-start | bytes 1179648 | tf_op jit(solution)/shard_map/reduce_scatter | solution.py:286
  763.0 1.9 copy-start.12
  763.0 229.9 %reduce-scatter.16.cloned.1.call-start = ((), (), s32[]{:S(2)}) async-start(), calls=%async_computation.21 | async-start | bytes 1179648 | tf_op jit(solution)/shard_map/reduce_scatter | solution.py:285
  764.8 283.3 %reduce-scatter.20.cloned.1.call-start = ((), (), s32[]{:S(2)}) async-start(), calls=%async_computation.23 | async-start | bytes 4718592 | tf_op jit(solution)/shard_map/reduce_scatter | solution.py:287
  770.6 333.0 %reduce-scatter.14.cloned.1.call-start = ((), (), s32[]{:S(2)}) async-start(), calls=%async_computation.20 | async-start | bytes 4718592 | tf_op jit(solution)/shard_map/reduce_scatter | solution.py:284
  773.9 1.6 copy-start.18
  774.0 449.6 %reduce-scatter.26.cloned.1.call-start = ((), (), s32[]{:S(2)}) async-start(), calls=%async_computation.26 | async-start | bytes 18874368 | tf_op jit(solution)/shard_map/reduce_scatter | solution.py:209
  785.2 1.6 copy-start.20
  785.3 558.3 %reduce-scatter.24.cloned.1.call-start = ((), (), s32[]{:S(2)}) async-start(), calls=%async_computation.25 | async-start | bytes 18874368 | tf_op jit(solution)/shard_map/reduce_scatter | solution.py:208
  796.7 666.9 %reduce-scatter.22.cloned.1.call-start = ((), (), s32[]{:S(2)}) async-start(), calls=%async_computation.24 | async-start | bytes 18874368 | tf_op jit(solution)/shard_map/reduce_scatter | solution.py:207
  806.5 0.7 copy-start.32
  806.5 108.0 %copy-start.5 = (bf16[512,2048]{1,0:T(8,128)(2,1)S(1)}, bf16[512,2048]{1,0:T(8,128)(2,1)}, u32[]{:S(2)}) copy-start(bf16[512,2048]{1,0:T(8,128)(2,1)} %param.12) | copy-start | bytes 6291460
  806.5 108.0 %copy-start.26 = (f32[8,1,256]{2,1,0:T(1,128)S(1)}, f32[8,1,256]{2,1,0:T(1,128)}, u32[]{:S(2)}) copy-start(f32[8,1,256]{2,1,0:T(1,128)} %copy-done.25) | copy-start | bytes 24580
  806.5 108.0 %copy-start.30 = (f32[512]{0:T(512)S(1)}, f32[512]{0:T(512)}, u32[]{:S(2)}) copy-start(f32[512]{0:T(512)} %copy-done.29) | copy-start | bytes 6148
Sparse Core Ops, SparseCore 0:
  10.5 31.2 all-gather.7
  44.3 28.1 all-gather.9
  87.8 155.3 all-reduce.7
  245.7 53.3 all-gather.13
  301.6 54.3 all-gather.11
  358.5 55.9 all-gather.15
  444.4 154.9 all-reduce.11
  602.3 85.5 all-reduce.9
  732.3 6.8 reduce-scatter.9
  742.9 8.1 reduce-scatter.11
  759.8 154.6 all-reduce.13
  918.1 35.0 reduce-scatter.17
  956.9 35.9 reduce-scatter.15
  996.7 51.3 reduce-scatter.19
  1052.2 51.2 reduce-scatter.13
  1107.6 115.9 reduce-scatter.25
  1227.6 115.9 reduce-scatter.23
  1347.5 115.9 reduce-scatter.21
where the time goes:
time: 1480 us; the launch traced here: 1470 us
  waiting for transfers between devices  1130 us (76%)
  matrix products  174 us (12%)
  blocking collectives  68.2 us (5%)
  other arithmetic  61.7 us (4%)
  between operations  15.8 us (1%)
  local copies, waits for them, and re-layouts  15.1 us (1%)
    psum x1, waiting for transfers between devices, shards(): grad_normed_mlp = lax.psum(partial_two, 'tensor')  145 us
    psum x1, waiting for transfers between devices, shards(): branch = lax.psum(attention_terms, 'tensor')  139 us
    reduce_scatter x1, waiting for transfers between devices, shards(): lax.psum_scatter(grad_down, ('dp', 'context'), scatter_dimension=1, tiled...  120 us
    reduce_scatter x1, waiting for transfers between devices, shards(): lax.psum_scatter(grad_gate, ('dp', 'context'), scatter_dimension=0, tiled...  120 us
    reduce_scatter x1, waiting for transfers between devices, shards(): lax.psum_scatter(grad_up, ('dp', 'context'), scatter_dimension=0, tiled=T...  120 us
    psum x1, waiting for transfers between devices, shards(): grad_normed = lax.psum(partial_one, 'tensor')  106 us
    psum x1, waiting for transfers between devices, shards(): lax.psum(mlp_terms.astype(jnp.bfloat16), 'tensor').astype(jnp.float32)  84 us
    reduce_scatter x1, waiting for transfers between devices, shards(): lax.psum_scatter(grad_query, ('dp', 'context'), scatter_dimension=0, tile...  55.5 us
  transfers between devices with their start and end apart: 18, of which 14 were waited for; matrix products, arithmetic and copies ran while one was open for 11% of the time, Pallas kernels for 0%

commit v1 on v0

--- a/solution.py
+++ b/solution.py
@@ -170,7 +170,7 @@
         lax.all_gather(mlp_copy[3], ("dp", "context"), axis=1, tiled=True),
     )
     gain_two_f = gain_two.astype(jnp.float32)
-    branch = lax.psum(attention_terms, "tensor")
+    branch = lax.psum(attention_terms.astype(jnp.bfloat16), "tensor").astype(jnp.float32)
     hidden_state = source + branch
     normed_mlp, scaled_two, rscale_two = norm_forward(hidden_state, gain_two_f)
     gate_value = jnp.dot(normed_mlp, gate_full, preferred_element_type=jnp.float32)
@@ -199,14 +199,14 @@
     partial_two = partial_two + jnp.einsum(
         "tf,df->td", grad_upward, up_full, preferred_element_type=jnp.float32
     )
-    grad_normed_mlp = lax.psum(partial_two, "tensor")
+    grad_normed_mlp = lax.psum(partial_two.astype(jnp.bfloat16), "tensor").astype(jnp.float32)
     grad_hidden, gain_grad_two = norm_backward(grad_normed_mlp, scaled_two, rscale_two, gain_two_f)
     grad_hidden = grad_hidden + grad_output
     grad_branch = grad_hidden.astype(jnp.bfloat16)
     grad_gate_own, grad_up_own, grad_down_own = (
-        lax.psum_scatter(grad_gate, ("dp", "context"), scatter_dimension=0, tiled=True),
-        lax.psum_scatter(grad_up, ("dp", "context"), scatter_dimension=0, tiled=True),
-        lax.psum_scatter(grad_down, ("dp", "context"), scatter_dimension=1, tiled=True),
+        lax.psum_scatter(grad_gate.astype(jnp.bfloat16), ("dp", "context"), scatter_dimension=0, tiled=True).astype(jnp.float32),
+        lax.psum_scatter(grad_up.astype(jnp.bfloat16), ("dp", "context"), scatter_dimension=0, tiled=True).astype(jnp.float32),
+        lax.psum_scatter(grad_down.astype(jnp.bfloat16), ("dp", "context"), scatter_dimension=1, tiled=True).astype(jnp.float32),
     )
     grad_out = jnp.einsum("te,td->ed", mixed_heads, grad_branch, preferred_element_type=jnp.float32)
     grad_mixed = jnp.einsum(
@@ -274,17 +274,17 @@
     partial_one = partial_one + jnp.einsum(
         "te,de->td", grad_value_in, value_full, preferred_element_type=jnp.float32
     )
-    grad_normed = lax.psum(partial_one, "tensor")
+    grad_normed = lax.psum(partial_one.astype(jnp.bfloat16), "tensor").astype(jnp.float32)
     grad_source, gain_grad_one = norm_backward(grad_normed, scaled_one, rscale_one, gain_one_f)
     input_grad = grad_source + grad_hidden
     gain_total_one, gain_total_two = (gain_grad_one, gain_grad_two)
     grad_gain_attn, grad_gain_mlp, grad_query_own, grad_key_own, grad_value_own, grad_out_own = (
         lax.psum_scatter(gain_total_one, ("dp", "context"), scatter_dimension=0, tiled=True),
         lax.psum_scatter(gain_total_two, ("dp", "context"), scatter_dimension=0, tiled=True),
-        lax.psum_scatter(grad_query, ("dp", "context"), scatter_dimension=0, tiled=True),
-        lax.psum_scatter(grad_key, ("dp", "context"), scatter_dimension=0, tiled=True),
-        lax.psum_scatter(grad_value, ("dp", "context"), scatter_dimension=0, tiled=True),
-        lax.psum_scatter(grad_out, ("dp", "context"), scatter_dimension=1, tiled=True),
+        lax.psum_scatter(grad_query.astype(jnp.bfloat16), ("dp", "context"), scatter_dimension=0, tiled=True).astype(jnp.float32),
+        lax.psum_scatter(grad_key.astype(jnp.bfloat16), ("dp", "context"), scatter_dimension=0, tiled=True).astype(jnp.float32),
+        lax.psum_scatter(grad_value.astype(jnp.bfloat16), ("dp", "context"), scatter_dimension=0, tiled=True).astype(jnp.float32),
+        lax.psum_scatter(grad_out.astype(jnp.bfloat16), ("dp", "context"), scatter_dimension=1, tiled=True).astype(jnp.float32),
     )
     return (
         activations,

time: 1480 us -> 1080 us (0.73)
  waiting for transfers between devices: 1130 us -> 740 us
    reduce_scatter x7, waiting for transfers between devices: 514 us -> 277 us  [the longest x1 72.2 us: shards(): lax.psum_scatter(grad_gate.astype(jnp.bfloat16), ('dp', 'context'), scatt...]
    psum x3 -> x2, waiting for transfers between devices: 390 us -> 156 us  [the longest x1 86.6 us: shards(): lax.psum(partial_two.astype(jnp.bfloat16), 'tensor').astype(jnp.float32)]
    psum x1, waiting for transfers between devices: 84 us -> 157 us  [shards(): lax.psum(mlp_terms.astype(jnp.bfloat16), 'tensor').astype(jnp.float32)]
    convert_element_type x0 -> x7, other arithmetic: none -> 14.9 us  [the longest x1 2.79 us: shards(): lax.psum_scatter(grad_up.astype(jnp.bfloat16), ('dp', 'context'), scatter...]
  transfers between devices with their start and end apart: 18 -> 17, of which waited for: 14 -> 13; matrix products, arithmetic and copies ran while one was open for 11% -> 16% of each run, Pallas kernels for 0% -> 0%
where the time goes in v1:
time: 1080 us; the launch traced here: 1070 us
  waiting for transfers between devices  740 us (69%)
  matrix products  167 us (15%)
  other arithmetic  75.4 us (7%)
  blocking collectives  68 us (6%)
  between operations  15.3 us (1%)
    psum x1, waiting for transfers between devices, shards(): lax.psum(mlp_terms.astype(jnp.bfloat16), 'tensor').astype(jnp.float32)  157 us
    psum x1, waiting for transfers between devices, shards(): lax.psum(partial_two.astype(jnp.bfloat16), 'tensor').astype(jnp.float32)  86.6 us
    reduce_scatter x1, waiting for transfers between devices, shards(): lax.psum_scatter(grad_gate.astype(jnp.bfloat16), ('dp', 'context'), scatt...  72.2 us
    reduce_scatter x1, waiting for transfers between devices, shards(): lax.psum_scatter(grad_up.astype(jnp.bfloat16), ('dp', 'context'), scatter...  71.9 us
    psum x1, waiting for transfers between devices, shards(): lax.psum(attention_terms.astype(jnp.bfloat16), 'tensor').astype(jnp.float32)  69.1 us
    all_gather x1, waiting for transfers between devices, shards(): lax.all_gather(mlp_copy[2], ('dp', 'context'), axis=0, tiled=True)  51 us
    all_gather x1, waiting for transfers between devices, shards(): lax.all_gather(mlp_copy[3], ('dp', 'context'), axis=1, tiled=True)  47.9 us
    all_gather x1, waiting for transfers between devices, shards(): lax.all_gather(mlp_copy[1], ('dp', 'context'), axis=0, tiled=True)  46.4 us
  transfers between devices with their start and end apart: 17, of which 13 were waited for; matrix products, arithmetic and copies ran while one was open for 16% of the time, Pallas kernels for 0%

profile of v1, /device:TPU:0, one launch (start us, length us, event | category | flops | bytes accessed | tf_op | source)
XLA Modules:
  0.0 1073.5 jit_solution(3603809061519400514)
XLA Ops:
  7.3 1.9 convert_element_type.192
  9.3 1.8 convert_element_type.197
  13.3 2.1 fusion.25
  15.8 10.3 all-gather
  26.2 11.0 %all_gather.34 = bf16[2048,128]{1,0:T(8,128)(2,1)S(1)} all-gather(bf16[256,128]{1,0:T(8,128)(2,1)S(1)} %convert_element_type.185), channel_id=1, replica_groups=mesh['dp'=4,'context'=2,'tensor'=4] {'dp','context'}, dimensions={0}, use_global_device_ids=true | all-gather | bytes 589824 | tf_op jit(solution)/shard_map/all_gather | solution.py:124
  38.0 2.1 all_gather.35
  40.2 8.8 all_gather.36
  50.4 2.3 all_gather.37
  53.2 3.0 fusion.53
  57.1 7.5 fusion.62
  64.6 8.1 fusion.3
  72.7 8.2 fusion.29
  80.9 4.4 convolution_convert_fusion.6
  85.3 2.7 convert_element_type.204
  88.1 2.7 convert_element_type.203
  90.9 2.8 convert_element_type.206
  93.8 9.4 all-gather.1
  103.2 69.1 %all-reduce.8.cloned.1.call-done = bf16[512,2048]{1,0:T(8,128)(2,1)} async-done(((bf16[512,2048]{1,0:T(8,128)(2,1)}), bf16[512,2048]{1,0:T(8,128)(2,1)}) %all-reduce.8.cloned.1.call-update) | async-done | bytes 2097168 | tf_op jit(solution)/shard_map/psum | solution.py:173
  172.3 2.5 multiply_reduce_fusion
  174.8 2.4 multiply_convert_fusion.3
  177.2 51.0 %all-gather.14.cloned.1.call-done = bf16[2048,2048]{1,0:T(8,128)(2,1)} async-done(((bf16[256,2048]{1,0:T(8,128)(2,1)}), bf16[2048,2048]{1,0:T(8,128)(2,1)}) %all-gather.14.cloned.1.call-update) | async-done | bytes 8388624 | tf_op jit(solution)/shard_map/all_gather | solution.py:169
  228.1 10.5 fusion.64
  238.6 46.4 %all-gather.12.cloned.1.call-done = bf16[2048,2048]{1,0:T(8,128)(2,1)} async-done(((bf16[256,2048]{1,0:T(8,128)(2,1)}), bf16[2048,2048]{1,0:T(8,128)(2,1)}) %all-gather.12.cloned.1.call-update) | async-done | bytes 8388624 | tf_op jit(solution)/shard_map/all_gather | solution.py:168
  285.0 10.5 fusion.63
  295.6 47.9 %all-gather.16.cloned.1.call-done = bf16[2048,2048]{1,0:T(8,128)(2,1)} async-done(((bf16[2048,256]{1,0:T(8,128)(2,1)}), bf16[2048,2048]{1,0:T(8,128)(2,1)}) %all-gather.16.cloned.1.call-update) | async-done | bytes 8388624 | tf_op jit(solution)/shard_map/all_gather | solution.py:170
  343.5 13.8 %multiply_convert_fusion = (bf16[512,2048]{1,0:T(8,128)(2,1)S(1)}, bf16[512,2048]{1,0:T(8,128)(2,1)S(1)}, bf16[512,2048]{1,0:T(8,128)(2,1)}) fusion(f32[512,2048]{1,0:T(8,128)} %fusion.63, f32[512,2048]{1,0:T(8,128)} %fusion.64, bf16[512,2048]{1,0:T(8,128)(2,1)} %param.13, bf16[2048,2048]{1,0:T(8,128)(2,1)} %all-gather.16.cloned.1.call-done), kind=kOutput, calls=%fused_computation.42 | convolution fusion | flops 4310695936 | bytes 25165824 | tf_op jit(solution)/shard_map/td,fd->tf/dot_general | solution.py:185
  357.3 8.5 fusion.65
  365.8 9.2 add_convert_fusion.1
  375.0 86.6 %all-reduce.10.cloned.1.call-done = bf16[512,2048]{1,0:T(8,128)(2,1)} async-done(((bf16[512,2048]{1,0:T(8,128)(2,1)}), bf16[512,2048]{1,0:T(8,128)(2,1)}) %all-reduce.10.cloned.1.call-update) | async-done | bytes 2097168 | tf_op jit(solution)/shard_map/psum | solution.py:202
  461.6 3.9 fusion.21
  465.8 3.7 convolution_convert_fusion.9
  469.4 9.2 fusion.30
  478.7 10.8 %fusion = (f32[2,4,512]{2,1,0:T(4,128)S(1)}, f32[2,1024,512,4]{2,1,3,0:T(8,128)}) fusion(f32[2,4,512,1024]{2,3,1,0:T(8,128)} %get-tuple-element.92, f32[2,4,512]{2,1,0:T(4,128)S(1)} %bitcast.137, bf16[512,2,4,64]{0,3,2,1:T(8,128)(2,1)S(1)} %bitcast.127, bf16[1024,2,64]{0,2,1:T(8,128)(2,1)} %all_gather.35), kind=kOutput, calls=%fused_computation.2 | convolution fusion | flops 549449728 | bytes 34373632 | tf_op jit(solution)/shard_map/while/body/eval_jaxpr/bkgd,lkd->kgbl/dot_general | solution.py:222
  489.6 11.9 %fusion.2 = bf16[2,4,512,1024]{2,3,1,0:T(8,128)(2,1)S(1)} fusion(f32[2,1024,512,4]{2,1,3,0:T(8,128)} %get-tuple-element.94, f32[2,4,512,1024]{2,3,1,0:T(8,128)} %get-tuple-element.92, f32[2,4,512]{2,1,0:T(4,128)S(1)} %get-tuple-element.93, f32[2,4,512]{2,1,0:T(4,128)S(1)} %bitcast.138), kind=kLoop, calls=%fused_computation.4 | loop fusion | flops 16777216 | bytes 41975808 | tf_op jit(solution)/shard_map/while/body/eval_jaxpr/convert_element_type | solution.py:226
  501.5 3.2 copy-done.1
  504.7 3.4 fusion.34
  509.3 1.8 convolution_convert_fusion.7
  511.1 4.1 reduce-scatter.10.cloned.1.call-done
  517.2 1.8 convolution_convert_fusion.8
  519.6 6.5 convolution_convert_fusion.3
  526.2 5.1 convolution_multiply_fusion
  531.9 2.8 convolution_convert_fusion.4
  534.8 10.0 convolution_convert_fusion.5
  547.2 2.1 add_convert_fusion
  549.5 10.0 convolution_convert_fusion
  559.6 10.0 convolution_convert_fusion.1
  569.9 10.0 convolution_convert_fusion.2
  581.8 1.5 convert_element_type.229
  583.3 8.3 reduce-scatter.16.cloned.1.call-done
  591.6 1.5 convert_element_type.227
  593.1 42.9 %reduce-scatter.20.cloned.1.call-done = bf16[512,256]{1,0:T(8,128)(2,1)} async-done(((bf16[512,2048]{1,0:T(8,128)(2,1)}), bf16[512,256]{1,0:T(8,128)(2,1)}) %reduce-scatter.20.cloned.1.call-update) | async-done | bytes 262160 | tf_op jit(solution)/shard_map/reduce_scatter | solution.py:287
  636.0 1.8 convert_element_type.231
  637.8 43.7 %reduce-scatter.14.cloned.1.call-done = bf16[256,512]{1,0:T(8,128)(2,1)} async-done(((bf16[2048,512]{1,0:T(8,128)(2,1)}), bf16[256,512]{1,0:T(8,128)(2,1)}) %reduce-scatter.14.cloned.1.call-update) | async-done | bytes 262160 | tf_op jit(solution)/shard_map/reduce_scatter | solution.py:284
  681.5 1.8 convert_element_type.225
  683.3 157.0 %all-reduce.12.cloned.1.call-done = (bf16[512,2048]{1,0:T(8,128)(2,1)}, bf16[512,2048]{1,0:T(8,128)(2,1)}) async-done(((bf16[512,2048]{1,0:T(8,128)(2,1)}, bf16[512,2048]{1,0:T(8,128)(2,1)}), (bf16[512,2048]{1,0:T(8,128)(2,1)}, bf16[512,2048]{1,0:T(8,128)(2,1)})) %all-reduce.12.cloned.1.call-update) | async-done | bytes 4194320 | tf_op jit(solution)/shard_map/psum | solution.py:182
  840.2 2.9 fusion.24
  843.2 24.0 %all-reduce.2 = (f32[2048]{0:T(1024)S(1)}, f32[2048]{0:T(1024)S(1)}) all-reduce(f32[2048]{0:T(1024)S(1)} %get-tuple-element.59, f32[2048]{0:T(1024)S(1)} %get-tuple-element.57), channel_id=4, replica_groups=mesh['dp'=4,'context'=2,'tensor'=4] {'dp','context'}, use_global_device_ids=true, to_apply=%region_17.18.clone | all-reduce | flops 4096 | bytes 32768
  868.5 7.5 fusion.17
  876.0 38.3 %reduce-scatter.26.cloned.1.call-done = bf16[2048,256]{1,0:T(8,128)(2,1)} async-done(((bf16[2048,2048]{1,0:T(8,128)(2,1)}), bf16[2048,256]{1,0:T(8,128)(2,1)}) %reduce-scatter.26.cloned.1.call-update) | async-done | bytes 1048592 | tf_op jit(solution)/shard_map/reduce_scatter | solution.py:209
  914.3 2.7 convert_element_type.237
  917.0 71.9 %reduce-scatter.24.cloned.1.call-done = bf16[256,2048]{1,0:T(8,128)(2,1)} async-done(((bf16[2048,2048]{1,0:T(8,128)(2,1)}), bf16[256,2048]{1,0:T(8,128)(2,1)}) %reduce-scatter.24.cloned.1.call-update) | async-done | bytes 1048592 | tf_op jit(solution)/shard_map/reduce_scatter | solution.py:208
  988.9 2.8 convert_element_type.235
  991.7 72.2 %reduce-scatter.22.cloned.1.call-done = bf16[256,2048]{1,0:T(8,128)(2,1)} async-done(((bf16[2048,2048]{1,0:T(8,128)(2,1)}), bf16[256,2048]{1,0:T(8,128)(2,1)}) %reduce-scatter.22.cloned.1.call-update) | async-done | bytes 1048592 | tf_op jit(solution)/shard_map/reduce_scatter | solution.py:207
  1063.9 2.8 convert_element_type.233
  (121 shorter events, 16.7 us)
Async XLA Ops:
  7.2 29.9 %copy-start = (bf16[512,2048]{1,0:T(8,128)(2,1)S(1)}, bf16[512,2048]{1,0:T(8,128)(2,1)}, u32[]{:S(2)}) copy-start(bf16[512,2048]{1,0:T(8,128)(2,1)} %param.12) | copy-start | bytes 6291460
  7.2 18.9 %copy-start.14 = (f32[256,128]{1,0:T(8,128)S(1)}, f32[256,128]{1,0:T(8,128)}, u32[]{:S(2)}) copy-start(f32[256,128]{1,0:T(8,128)} %param.17) | copy-start | bytes 393220
  7.2 18.9 %copy-start.15 = (f32[256,128]{1,0:T(8,128)S(1)}, f32[256,128]{1,0:T(8,128)}, u32[]{:S(2)}) copy-start(f32[256,128]{1,0:T(8,128)} %param.18) | copy-start | bytes 393220
  7.2 46.0 %all-gather.8.cloned.1.call-start = ((), (), s32[]{:S(2)}) async-start(), calls=%async_computation.9 | async-start | bytes 2359296 | tf_op jit(solution)/shard_map/all_gather | solution.py:122
  9.2 71.7 %all-gather.10.cloned.1.call-start = ((), (), s32[]{:S(2)}) async-start(), calls=%async_computation.10 | async-start | bytes 2359296 | tf_op jit(solution)/shard_map/all_gather | solution.py:125
  11.1 161.2 %all-reduce.8.cloned.1.call-start = ((), (), s32[]{:S(2)}) async-start(), calls=%async_computation.11 | async-start | bytes 4194304 | tf_op jit(solution)/shard_map/psum | solution.py:173
  37.1 12.8 %copy-start.8 = (bf16[2048,128]{1,0:T(8,128)(2,1)}, bf16[2048,128]{1,0:T(8,128)(2,1)S(1)}, u32[]{:S(2)}) copy-start(bf16[2048,128]{1,0:T(8,128)(2,1)S(1)} %all_gather.34) | copy-start | bytes 1572868
  49.0 1.4 copy-start.10
  56.2 1.0 copy-start.5
  64.6 8.1 copy-start.13
  85.2 142.9 %all-gather.14.cloned.1.call-start = ((), (), s32[]{:S(2)}) async-start(), calls=%async_computation.13 | async-start | bytes 9437184 | tf_op jit(solution)/shard_map/all_gather | solution.py:169
  88.0 5.7 copy-start.16
  88.1 197.0 %all-gather.12.cloned.1.call-start = ((), (), s32[]{:S(2)}) async-start(), calls=%async_computation.12 | async-start | bytes 9437184 | tf_op jit(solution)/shard_map/all_gather | solution.py:168
  90.8 252.6 %all-gather.16.cloned.1.call-start = ((), (), s32[]{:S(2)}) async-start(), calls=%async_computation.14 | async-start | bytes 9437184 | tf_op jit(solution)/shard_map/all_gather | solution.py:170
  93.7 368.0 %all-reduce.10.cloned.1.call-start = ((), (), s32[]{:S(2)}) async-start(), calls=%async_computation.15 | async-start | bytes 4194304 | tf_op jit(solution)/shard_map/psum | solution.py:202
  172.3 2.5 copy-start.2
  357.3 8.5 copy-start.18
  357.3 8.5 copy-start.19
  375.0 133.3 %reduce-scatter.12.cloned.1.call-start = ((), (), s32[]{:S(2)}) async-start(), calls=%async_computation.17 | async-start | bytes 786432 | tf_op jit(solution)/shard_map/reduce_scatter | solution.py:252
  461.6 3.9 copy-start.3
  461.6 3.9 copy-start.4
  461.6 4.1 copy-start.7
  489.5 25.7 %reduce-scatter.10.cloned.1.call-start = ((), (), s32[]{:S(2)}) async-start(), calls=%async_computation.16 | async-start | bytes 786432 | tf_op jit(solution)/shard_map/reduce_scatter | solution.py:251
  501.5 3.2 copy-start.1
  508.2 73.6 %reduce-scatter.18.cloned.1.call-start = ((), (), s32[]{:S(2)}) async-start(), calls=%async_computation.20 | async-start | bytes 589824 | tf_op jit(solution)/shard_map/reduce_scatter | solution.py:286
  511.1 80.5 %reduce-scatter.16.cloned.1.call-start = ((), (), s32[]{:S(2)}) async-start(), calls=%async_computation.19 | async-start | bytes 589824 | tf_op jit(solution)/shard_map/reduce_scatter | solution.py:285
  519.1 7.1 copy-start.6
  519.1 116.9 %reduce-scatter.20.cloned.1.call-start = ((), (), s32[]{:S(2)}) async-start(), calls=%async_computation.21 | async-start | bytes 2359296 | tf_op jit(solution)/shard_map/reduce_scatter | solution.py:287
  526.1 155.3 %reduce-scatter.14.cloned.1.call-start = ((), (), s32[]{:S(2)}) async-start(), calls=%async_computation.18 | async-start | bytes 2359296 | tf_op jit(solution)/shard_map/reduce_scatter | solution.py:284
  534.8 305.5 %all-reduce.12.cloned.1.call-start = ((), (), s32[]{:S(2)}) async-start(), calls=%async_computation.25 | async-start | bytes 8388608 | tf_op jit(solution)/shard_map/psum | solution.py:182
  534.8 10.0 copy-start.12
  544.8 1.3 copy-start.11
  546.1 1.0 copy-start.9
  549.3 365.0 %reduce-scatter.26.cloned.1.call-start = ((), (), s32[]{:S(2)}) async-start(), calls=%async_computation.24 | async-start | bytes 9437184 | tf_op jit(solution)/shard_map/reduce_scatter | solution.py:209
  559.5 429.4 %reduce-scatter.24.cloned.1.call-start = ((), (), s32[]{:S(2)}) async-start(), calls=%async_computation.23 | async-start | bytes 9437184 | tf_op jit(solution)/shard_map/reduce_scatter | solution.py:208
  569.6 494.3 %reduce-scatter.22.cloned.1.call-start = ((), (), s32[]{:S(2)}) async-start(), calls=%async_computation.22 | async-start | bytes 9437184 | tf_op jit(solution)/shard_map/reduce_scatter | solution.py:207
  579.9 0.7 copy-start.17
Sparse Core Ops, SparseCore 0:
  10.5 31.2 all-gather.7
  44.3 28.1 all-gather.9
  85.4 86.8 all-reduce.7
  174.8 53.3 all-gather.13
  230.6 54.3 all-gather.11
  287.5 55.9 all-gather.15
  375.1 86.5 all-reduce.9
  489.7 6.9 reduce-scatter.11
  508.3 6.8 reduce-scatter.9
  518.2 35.2 reduce-scatter.17
  557.4 34.1 reduce-scatter.15
  594.8 41.2 reduce-scatter.19
  640.2 41.2 reduce-scatter.13
  684.9 155.3 all-reduce.11
  843.9 70.2 reduce-scatter.25
  917.6 71.2 reduce-scatter.23
  992.6 71.2 reduce-scatter.21

commit v2 on v1

v2 whole, which is shorter than its diff:
```python
import functools
import math

import jax
import jax.numpy as jnp
from jax import lax
from jax.experimental import pallas as pl
from jax.experimental.pallas import tpu as pltpu
from jax.sharding import PartitionSpec as P

HD = 64
WINDOW = 512
QROWS = 256
EPSILON = 1e-05
NEGATIVE = -1e30
MESH = pl.DeviceIdType.MESH
F32 = jnp.float32
BF16 = jnp.bfloat16
NN = (((1,), (0,)), ((), ()))
NT = (((1,), (1,)), ((), ()))
TN = (((0,), (0,)), ((), ()))
VMEM_LIMIT = 62 * 2**20


def dot(left, right, dims=NN):
    return lax.dot_general(left, right, dims, preferred_element_type=F32)


def frequencies():
    exponent = jnp.arange(0, HD, 2).astype(jnp.float32) / HD
    initial = 1.0 / 500000.0**exponent
    wavelength = 2.0 * math.pi / initial
    smoothing = (8192.0 / wavelength - 1.0) / 3.0
    blended = (1.0 - smoothing) * initial / 32.0 + smoothing * initial
    return jnp.where(
        wavelength < 2048.0, initial, jnp.where(wavelength > 8192.0, initial / 32.0, blended)
    )


def aligned(index, size):
    return pl.ds(pl.multiple_of(index * size, size), size)


class Place:
    def __init__(self, dp, tensor):
        self.dp, self.tensor = dp, tensor
        self.bits = dp.bit_length() - 1
        self.p = lax.axis_index("dp")
        self.c = lax.axis_index("context")
        self.t = lax.axis_index("tensor")
        self.core = (self.p, 1 - self.c, self.t)
        self.low = lax.rem(lax.div(self.t * 2, tensor), 2)
        self.early = 1 - self.low
        self.late = self.low
        step = 1 - 2 * self.low
        self.inward = (self.p, self.c, self.t + step)
        self.outward = (self.p, self.c, self.t - step)
        edge = self.low * (tensor - 1 - self.t) + (1 - self.low) * self.t
        self.depth = edge
        self.at_end = edge == 0

    def flipped(self, mask):
        position = self.p
        for b in range(self.bits):
            if mask >> b & 1:
                bit = lax.rem(lax.div(self.p, 2**b), 2)
                position = position + (1 - 2 * bit) * 2**b
        return position

    def across(self, b):
        return (self.flipped(1 << b), self.c, self.t)

    def greet(self):
        barrier = pltpu.get_barrier_semaphore()
        for device in [self.core] + [self.across(b) for b in range(self.bits)] + [self.inward]:
            pl.semaphore_signal(barrier, inc=1, device_id=device, device_id_type=MESH)

        @pl.when(jnp.logical_not(self.at_end))
        def _():
            pl.semaphore_signal(barrier, inc=1, device_id=self.outward, device_id_type=MESH)

    def meet(self):
        barrier = pltpu.get_barrier_semaphore()

        @pl.when(self.at_end)
        def _():
            pl.semaphore_wait(barrier, 2 + self.bits)

        @pl.when(jnp.logical_not(self.at_end))
        def _():
            pl.semaphore_wait(barrier, 3 + self.bits)


def remote(source, target, send, receive, device):
    return pltpu.make_async_remote_copy(
        src_ref=source,
        dst_ref=target,
        send_sem=send,
        recv_sem=receive,
        device_id=device,
        device_id_type=MESH,
    )


def orders_of(bits, halves):
    forward = tuple(range(bits))
    return (forward, forward[::-1]) if halves == 2 else (forward,)


def phase_masks(order, phase):
    masks = [0]
    for b in order[:phase]:
        masks = masks + [m | 1 << b for m in masks]
    return [m | 1 << order[phase] for m in masks]


class Gather:
    def __init__(self, place, shard, full, axis, sems, halves=2):
        self.place, self.shard, self.full, self.axis = place, shard, full, axis
        self.halves = halves
        self.send, self.receive, self.core_send, self.core_receive, self.local = sems
        self.orders = orders_of(place.bits, halves)
        self.rows = shard.shape[0] // halves
        self.sends = []

    @staticmethod
    def semaphores(dp, halves=2):
        bits = dp.bit_length() - 1
        return [
            pltpu.SemaphoreType.DMA((halves, dp, max(bits, 1))),
            pltpu.SemaphoreType.DMA((halves, dp)),
            pltpu.SemaphoreType.DMA((halves, dp)),
            pltpu.SemaphoreType.DMA((halves, dp)),
            pltpu.SemaphoreType.DMA((1,)),
        ]

    def part(self, half):
        return self.shard.at[pl.ds(half * self.rows, self.rows)]

    def slot(self, position, core, half):
        index = position * 2 + core
        if self.axis == 0:
            rows = self.shard.shape[0]
            first = pl.multiple_of(index * rows + half * self.rows, self.rows)
            return self.full.at[pl.ds(first, self.rows)]
        return self.full.at[
            pl.ds(half * self.rows, self.rows), aligned(index, self.shard.shape[1])
        ]

    def _forward(self, half, mask, source):
        place = self.place
        order = self.orders[half]
        last = max([order.index(b) for b in order if mask >> b & 1], default=-1)
        target = self.slot(place.flipped(mask), place.c, half)
        for j in range(last + 1, place.bits):
            copy = remote(
                source,
                target,
                self.send.at[half, mask, j],
                self.receive.at[half, mask | 1 << order[j]],
                place.across(order[j]),
            )
            copy.start()
            self.sends.append(copy)
        copy = remote(
            source,
            target,
            self.core_send.at[half, mask],
            self.core_receive.at[half, mask],
            place.core,
        )
        copy.start()
        self.sends.append(copy)

    def start(self):
        place = self.place
        for half in range(self.halves):
            self._forward(half, 0, self.part(half))
        index = place.p * 2 + place.c
        if self.axis == 0:
            own = self.full.at[aligned(index, self.shard.shape[0])]
        else:
            own = self.full.at[:, aligned(index, self.shard.shape[1])]
        self.own = pltpu.make_async_copy(self.shard, own, self.local.at[0])
        self.own.start()

    def pass_on(self, phase):
        place = self.place
        for half in range(self.halves):
            for mask in phase_masks(self.orders[half], phase):
                source = self.slot(place.flipped(mask), place.c, half)
                remote(
                    source,
                    source,
                    self.send.at[half, mask, 0],
                    self.receive.at[half, mask],
                    place.core,
                ).wait_recv()
                self._forward(half, mask, source)

    def finish(self):
        place = self.place
        self.own.wait()
        for half in range(self.halves):
            for mask in range(place.dp):
                target = self.slot(place.flipped(mask), 1 - place.c, half)
                remote(
                    target,
                    target,
                    self.core_send.at[half, mask],
                    self.core_receive.at[half, mask],
                    place.core,
                ).wait_recv()

    def drain(self):
        for copy in self.sends:
            copy.wait_send()
        self.sends = []


class LineSum:
    lags = (0, 3, 5, 7)

    def __init__(self, place, part, inbox, result, sems, pieces, root):
        self.place, self.part, self.inbox, self.result = place, part, inbox, result
        self.sum_send, self.sum_receive, self.back_send, self.back_receive = sems
        self.pieces = pieces
        self.rows = part.shape[1] // pieces
        self.rounds = pieces + self.lags[-1]
        self.root = root

    @staticmethod
    def semaphores(pieces):
        return [pltpu.SemaphoreType.DMA((2, pieces))] * 4

    def _copy(self, kind, flow, i, device):
        rows = aligned(i, self.rows)
        if kind == "sum":
            return remote(
                self.part.at[flow, rows],
                self.inbox.at[flow, rows],
                self.sum_send.at[flow, i],
                self.sum_receive.at[flow, i],
                device,
            )
        return remote(
            self.result.at[flow, rows],
            self.result.at[flow, rows],
            self.back_send.at[flow, i],
            self.back_receive.at[flow, i],
            device,
        )

    def _add(self, flow, i):
        rows = aligned(i, self.rows)
        total = self.part[flow, rows].astype(F32) + self.inbox[flow, rows].astype(F32)
        self.part[flow, rows] = total.astype(BF16)

    def early_start(self):
        @pl.when(self.place.at_end)
        def _():
            def one(i, carry):
                self._copy("sum", self.place.early, i, self.place.inward).start()
                return carry

            lax.fori_loop(0, self.pieces, one, 0)

    def early_sum(self, i):
        place = self.place

        @pl.when(jnp.logical_not(place.at_end))
        def _():
            copy = self._copy("sum", place.early, i, place.inward)
            copy.wait_recv()
            self._add(place.early, i)
            copy.start()

    def late_sum(self, i):
        place = self.place
        copy = self._copy("sum", place.late, i, place.outward)
        copy.wait_recv()

        @pl.when(jnp.logical_not(place.at_end))
        def _():
            self._add(place.late, i)
            copy.start()

        @pl.when(place.at_end)
        def _():
            rows = aligned(i, self.rows)
            total = self.part[place.late, rows].astype(F32)
            total = total + self.inbox[place.late, rows].astype(F32)
            self.root(i, rows, total)
            self._copy("back", place.late, i, place.inward).start()

    def late_back(self, i):
        place = self.place

        @pl.when(jnp.logical_not(place.at_end))
        def _():
            copy = self._copy("back", place.late, i, place.inward)
            copy.wait_recv()
            copy.start()

    def early_back(self, i):
        place = self.place
        copy = self._copy("back", place.early, i, place.outward)
        copy.wait_recv()

        @pl.when(jnp.logical_not(place.at_end))
        def _():
            copy.start()

    def round(self, n):
        for lag, kind in zip(self.lags, ("early_sum", "late_sum", "late_back", "early_back")):
            i = n - lag
            if isinstance(i, int):
                if 0 <= i < self.pieces:
                    getattr(self, kind)(i)
            else:

                @pl.when((i >= 0) & (i < self.pieces))
                def _(kind=kind, i=i):
                    getattr(self, kind)(i)

    def run(self, first, last):
        def one(n, carry):
            self.round(n)
            return carry

        lax.fori_loop(first, last, one, 0)

    def drain(self):
        place = self.place

        def one(i, carry):
            self._copy("sum", place.early, i, place.inward).wait_send()
            self._copy("back", place.late, i, place.inward).wait_send()

            @pl.when(jnp.logical_not(place.at_end))
            def _():
                self._copy("sum", place.late, i, place.outward).wait_send()
                self._copy("back", place.early, i, place.outward).wait_send()

            return carry

        lax.fori_loop(0, self.pieces, one, 0)


class Scatter:
    def __init__(self, place, part, inbox, out, axis, sems):
        self.place, self.part, self.inbox, self.out, self.axis = place, part, inbox, out, axis
        self.send, self.receive, self.local = sems
        self.orders = orders_of(place.bits, 2)
        self.rows = out.shape[1] // 2
        self.sends = []

    @staticmethod
    def semaphores(dp):
        return [
            pltpu.SemaphoreType.DMA((2, dp)),
            pltpu.SemaphoreType.DMA((2, dp)),
            pltpu.SemaphoreType.DMA((1,)),
        ]

    @staticmethod
    def inbox_shape(dp, rows, columns):
        slots = sum(2**phase - 1 for phase in range(1, dp.bit_length() - 1))
        return (2, max(slots, 1), rows // 2, columns)

    def slot(self, position, half):
        if self.axis == 0:
            rows = self.out.shape[1]
            first = pl.multiple_of(position * rows + half * self.rows, self.rows)
            return self.part.at[pl.ds(first, self.rows)]
        return self.part.at[
            pl.ds(half * self.rows, self.rows), aligned(position, self.out.shape[2])
        ]

    def landing(self, half, phase, mask):
        if mask == 0:
            return self.out.at[1 + phase, pl.ds(half * self.rows, self.rows)]
        return self.inbox.at[half, self.code(half, phase, mask)]

    def code(self, half, phase, mask):
        order = self.orders[half]
        number = 0
        for later in range(self.place.bits - 1, phase, -1):
            number += 2**later - 1
        inside = [m for m in range(1, self.place.dp) if all(b in order[:phase] for b in bits_of(m))]
        return number + inside.index(mask)

    def _copies(self, half, phase):
        order = self.orders[half]
        b = order[phase]
        for mask in phase_masks(order, phase):
            yield remote(
                self.slot(self.place.flipped(mask), half),
                self.landing(half, phase, mask & ~(1 << b)),
                self.send.at[half, mask],
                self.receive.at[half, mask],
                self.place.across(b),
            )

    def start(self):
        place = self.place
        index = place.p
        if self.axis == 0:
            own = self.part.at[aligned(index, self.out.shape[1])]
        else:
            own = self.part.at[:, aligned(index, self.out.shape[2])]
        self.own = pltpu.make_async_copy(own, self.out.at[0], self.local.at[0])
        self.own.start()
        if place.bits:
            self._send(place.bits - 1)

    def _send(self, phase):
        for half in range(2):
            for copy in self._copies(half, phase):
                copy.start()
                self.sends.append(copy)

    def pass_on(self, phase):
        for half in range(2):
            order = self.orders[half]
            for copy, mask in zip(self._copies(half, phase), phase_masks(order, phase)):
                rest = mask & ~(1 << order[phase])
                if rest:
                    copy.wait_recv()
                    target = self.slot(self.place.flipped(rest), half)
                    source = self.landing(half, phase, rest)
                    pieces = max(1, self.rows // 64)
                    size = self.rows // pieces

                    def add(i, carry, target=target, source=source, size=size):
                        rows = aligned(i, size)
                        total = target[rows].astype(F32) + source[rows].astype(F32)
                        target[rows] = total.astype(BF16)
                        return carry

                    lax.fori_loop(0, pieces, add, 0)
        self._send(phase - 1)

    def finish(self):
        self.own.wait()
        for phase in range(self.place.bits):
            for half in range(2):
                order = self.orders[half]
                for copy, mask in zip(self._copies(half, phase), phase_masks(order, phase)):
                    if not mask & ~(1 << order[phase]):
                        copy.wait_recv()
        for copy in self.sends:
            copy.wait_send()
        self.sends = []


def bits_of(mask):
    return [b for b in range(mask.bit_length()) if mask >> b & 1]


def turned(z):
    width = z.shape[-1]
    half = HD // 2
    if width == 2 * HD:
        lane = lax.broadcasted_iota(jnp.int32, z.shape, 1)
        return jnp.where(lax.rem(lane, HD) < half, pltpu.roll(z, width - half, 1), pltpu.roll(z, half, 1))
    pieces = []
    for h in range(width // HD):
        pieces += [z[:, h * HD + half : (h + 1) * HD], z[:, h * HD : h * HD + half]]
    return jnp.concatenate(pieces, -1)


def document_starts(lengths, rows):
    starts = jnp.zeros(rows.shape, jnp.int32)
    end = lengths[0, 0]
    for k in range(lengths.shape[1]):
        starts = jnp.where(rows >= end, end, starts)
        if k + 1 < lengths.shape[1]:
            end = end + lengths[0, k + 1]
    return starts


def tables(place, lengths, freq, cosine, sine, tokens):
    rows = lax.broadcasted_iota(jnp.int32, (tokens, 128), 0) + place.c * tokens
    angle = (rows - document_starts(lengths, rows)).astype(F32) * freq[0:1, :]
    lane = lax.broadcasted_iota(jnp.int32, (tokens, 128), 1)
    cosine[...] = jnp.cos(angle)
    turned_sine = jnp.sin(angle)
    sine[...] = jnp.where(lax.rem(lane, HD) < HD // 2, -turned_sine, turned_sine)


def fill_bias(place, lengths, bias, tokens):
    keys = bias.shape[1]
    for b in range(tokens // QROWS):
        shape = (keys, QROWS)
        query = lax.broadcasted_iota(jnp.int32, shape, 1) + (place.c * tokens + b * QROWS)
        key = lax.broadcasted_iota(jnp.int32, shape, 0) + place.c * b * QROWS
        row = lax.broadcasted_iota(jnp.int32, (8, QROWS), 1) + (place.c * tokens + b * QROWS)
        starts = document_starts(lengths, row)[0:1, :]
        bias[b] = jnp.where((key >= starts) & (key <= query), 0.0, NEGATIVE)


def softmax_of(key, query, bias):
    scores = dot(key, query, NT) + bias
    highest = jnp.max(scores, 0, keepdims=True)
    raw = jnp.exp(scores - highest)
    return raw * (1.0 / jnp.sum(raw, 0, keepdims=True))


def forward_kernel(cfg, *refs):
    (
        x_in, lengths, freq, gains_in, wq_in, wk_in, wv_in, wo_in, wg_in, wu_in, wd_in,
        qkv_out, wo_out, wg_full, wu_full, wd_full, gains_out,
        normed_out, q_out, k_out, v_out, mixed_out, hidden_out, normed_mlp_out,
        x, wq, wk, wv, wo, wg, wu, wd, gains32,
        sqkv, swo, swg, swu, swd, sgains,
        wqkv, wout, gains, normed, rscale, cosine, sine, bias,
        qh, kh, vh, kv, kv_in, mixed, part, inbox, result, hidden,
        load, store, kv_send, kv_receive, *sems,
    ) = refs
    place = Place(cfg.dp, cfg.tensor)
    tokens, width = x.shape
    heads, groups = cfg.heads, cfg.groups
    query_width, key_width = heads * HD, groups * HD
    loads = []
    for i, (source, target) in enumerate(
        [(gains_in, gains32), (wq_in, wq), (wk_in, wk), (wv_in, wv), (x_in, x), (wo_in, wo), (wg_in, wg), (wu_in, wu), (wd_in, wd)]
    ):
        copy = pltpu.make_async_copy(source, target, load.at[i])
        copy.start()
        loads.append(copy)
    place.greet()
    gathers = []
    for i, (shard, full, axis, halves) in enumerate(
        [
            (sgains, gains, 1, 1),
            (sqkv, wqkv, 0, 2),
            (swo, wout, 1, 2),
            (swg, wg_full, 0, 2),
            (swu, wu_full, 0, 2),
            (swd, wd_full, 1, 2),
        ]
    ):
        gathers.append(Gather(place, shard, full, axis, sems[5 * i : 5 * i + 5], halves))
    g_gains, g_qkv, g_wo, g_wg, g_wu, g_wd = gathers
    line_sems = sems[5 * len(gathers) :]
    for i in range(4):
        loads[i].wait()
    sgains[...] = gains32[...].astype(BF16)
    sqkv[:, :query_width] = wq[...].astype(BF16)
    sqkv[:, query_width : query_width + key_width] = wk[...].astype(BF16)
    sqkv[:, query_width + key_width :] = wv[...].astype(BF16)
    place.meet()
    g_gains.start()
    g_qkv.start()
    loads[5].wait()
    swo[...] = wo[...].astype(BF16)
    for i, (raw, staged) in enumerate([(wg, swg), (wu, swu), (wd, swd)]):
        loads[6 + i].wait()
        pieces = 8
        for n in range(pieces):
            rows = pl.ds(n * (raw.shape[0] // pieces), raw.shape[0] // pieces)
            staged[rows] = raw[rows].astype(BF16)
    for phase in range(place.bits):
        g_gains.pass_on(phase)
        g_qkv.pass_on(phase)
        if phase == 0:
            g_wo.start()
            g_wg.start()
            g_wu.start()
            g_wd.start()
            loads[4].wait()
            rows_at = 64

            def scale(i, carry):
                rows = aligned(i, rows_at)
                block = x[rows].astype(F32)
                mean = jnp.sum(block * block, -1, keepdims=True) * (1.0 / width)
                rscale[rows] = lax.rsqrt(mean + EPSILON)
                return carry

            lax.fori_loop(0, tokens // rows_at, scale, 0)
            tables(place, lengths, freq, cosine, sine, tokens)
            fill_bias(place, lengths, bias, tokens)
    g_gains.finish()

    def norm(i, carry):
        rows = aligned(i, 64)
        scaled = x[rows].astype(F32) * rscale[rows]
        normed[rows] = (scaled * gains[0:1, :].astype(F32)).astype(BF16)
        return carry

    lax.fori_loop(0, tokens // 64, norm, 0)
    stores = []

    def keep(source, target):
        copy = pltpu.make_async_copy(source, target, store.at[len(stores)])
        copy.start()
        stores.append(copy)

    keep(normed, normed_out)
    keep(gains, gains_out)
    g_qkv.finish()
    keep(wqkv, qkv_out)
    for b in range(tokens // QROWS):
        rows = pl.ds(b * QROWS, QROWS)
        product = dot(normed[rows], wqkv[...])
        table_c, table_s = cosine[rows], sine[rows]
        for block in range(query_width // 128):
            z = product[:, block * 128 : (block + 1) * 128]
            z = (z * table_c + turned(z) * table_s) * HD**-0.5
            for h in range(2):
                qh[2 * block + h, rows] = z[:, h * HD : (h + 1) * HD].astype(BF16)
        z = product[:, query_width : query_width + key_width]
        if key_width % 128 == 0:
            wide = key_width // 128
            table_c = jnp.concatenate([table_c] * wide, -1)
            table_s = jnp.concatenate([table_s] * wide, -1)
        else:
            table_c, table_s = table_c[:, :key_width], table_s[:, :key_width]
        z = z * table_c + turned(z) * table_s
        kv[rows, :key_width] = z.astype(BF16)
        kv[rows, key_width:] = product[:, query_width + key_width :].astype(BF16)
    pass_kv = remote(kv, kv_in, kv_send.at[0], kv_receive.at[0], place.core)

    @pl.when(place.c == 0)
    def _():
        pass_kv.start()
        for g in range(groups):
            kh[g, tokens:] = jnp.zeros((tokens, HD), BF16)
            vh[g, tokens:] = jnp.zeros((tokens, HD), BF16)

    own_rows = aligned(place.c, tokens)
    for g in range(groups):
        kh[g, own_rows] = kv[:, g * HD : (g + 1) * HD]
        vh[g, own_rows] = kv[:, key_width + g * HD : key_width + (g + 1) * HD]

    @pl.when(place.c == 1)
    def _():
        pass_kv.wait_recv()
        for g in range(groups):
            kh[g, :tokens] = kv_in[:, g * HD : (g + 1) * HD]
            vh[g, :tokens] = kv_in[:, key_width + g * HD : key_width + (g + 1) * HD]

    keep(qh, q_out)
    keep(kh, k_out)
    keep(vh, v_out)
    if place.bits:
        g_wo.pass_on(0)

    def attend(b):
        rows = aligned(b, QROWS)
        window = pl.ds(pl.multiple_of(place.c * b * QROWS, QROWS), bias.shape[1])

        def pair(j, carry):
            outs = []
            for h in range(2):
                head = 2 * j + h
                g = lax.div(head, heads // groups)
                weights = softmax_of(kh[g, window], qh[head, rows], bias[b]).astype(BF16)
                outs.append(dot(vh[g, window], weights, TN))
            mixed[rows, aligned(j, 128)] = jnp.concatenate(outs, 0).T.astype(BF16)
            return carry

        lax.fori_loop(0, heads // 2, pair, 0)

    def project(b):
        rows = aligned(b, QROWS)
        part[b] = dot(mixed[rows], wout[...]).astype(BF16)

    def root(i, rows, total):
        local = pl.ds(pl.multiple_of(place.late * QROWS + i * line.rows, line.rows), line.rows)
        total = total + x[local].astype(F32)
        hidden[rows] = total
        r = lax.rsqrt(jnp.sum(total * total, -1, keepdims=True) * (1.0 / width) + EPSILON)
        result[place.late, rows] = (total * r * gains[1:2, :].astype(F32)).astype(BF16)

    line = LineSum(place, part, inbox, result, line_sems, cfg.pieces, root)
    attend(place.early)
    for phase in range(1, place.bits):
        g_wo.pass_on(phase)
    g_wo.finish()
    keep(wout, wo_out)
    project(place.early)
    line.early_start()
    attend(place.late)
    project(place.late)
    keep(mixed, mixed_out)
    agenda = []
    for g in (g_wg, g_wu, g_wd):
        for phase in range(place.bits):
            agenda.append(functools.partial(g.pass_on, phase))
    marks = [line.rounds * (k + 1) // (len(agenda) + 1) for k in range(len(agenda))]
    at = 0
    for mark, item in zip(marks, agenda):
        line.run(at, mark)
        item()
        at = mark
    line.run(at, line.rounds)
    copy_back = pltpu.make_async_copy(result, normed_mlp_out, store.at[len(stores)])
    copy_back.start()
    stores.append(copy_back)
    keep(hidden, hidden_out)
    for g in (g_wg, g_wu, g_wd):
        g.finish()
    for g in gathers:
        g.drain()
    line.drain()

    @pl.when(place.c == 0)
    def _():
        pass_kv.wait_send()

    for copy in stores:
        copy.wait()


class Config:
    def __init__(self, dp, tensor, tokens, width, heads, groups, hidden_units):
        self.dp, self.tensor, self.tokens, self.width = dp, tensor, tokens, width
        self.heads, self.groups, self.hidden_units = heads, groups, hidden_units
        self.pieces = 8
        self.chunks = 4
        self.query_width, self.key_width = heads * HD, groups * HD
        self.qkv_width = self.query_width + 2 * self.key_width
        self.blocks = dp * 2
        self.block = width // self.blocks
        self.window = WINDOW + QROWS


def forward_call(cfg, x, lengths, freq, gains, wq, wk, wv, wo, wg, wu, wd):
    tokens, width, units = cfg.tokens, cfg.width, cfg.hidden_units
    any_spec = pl.BlockSpec(memory_space=pl.ANY)
    shape = jax.ShapeDtypeStruct
    outs = [
        shape((width, cfg.qkv_width), BF16),
        shape((cfg.query_width, width), BF16),
        shape((width, units), BF16),
        shape((width, units), BF16),
        shape((units, width), BF16),
        shape((16, width), BF16),
        shape((tokens, width), BF16),
        shape((cfg.heads, tokens, HD), BF16),
        shape((cfg.groups, 2 * tokens, HD), BF16),
        shape((cfg.groups, 2 * tokens, HD), BF16),
        shape((tokens, cfg.query_width), BF16),
        shape((QROWS, width), F32),
        shape((2, QROWS, width), BF16),
    ]
    shards = [wq, wk, wv, wo, wg, wu, wd]
    scratch = [pltpu.VMEM(x.shape, BF16)]
    scratch += [pltpu.VMEM(w.shape, F32) for w in shards]
    scratch += [pltpu.VMEM(gains.shape, F32)]
    scratch += [pltpu.VMEM((wq.shape[0], cfg.qkv_width), BF16)]
    scratch += [pltpu.VMEM(w.shape, BF16) for w in (wo, wg, wu, wd, gains)]
    scratch += [
        pltpu.VMEM((width, cfg.qkv_width), BF16),
        pltpu.VMEM((cfg.query_width, width), BF16),
        pltpu.VMEM((16, width), BF16),
        pltpu.VMEM((tokens, width), BF16),
        pltpu.VMEM((tokens, 1), F32),
        pltpu.VMEM((tokens, 128), F32),
        pltpu.VMEM((tokens, 128), F32),
        pltpu.VMEM((2, cfg.window, QROWS), F32),
        pltpu.VMEM((cfg.heads, tokens, HD), BF16),
        pltpu.VMEM((cfg.groups, 2 * tokens, HD), BF16),
        pltpu.VMEM((cfg.groups, 2 * tokens, HD), BF16),
        pltpu.VMEM((tokens, 2 * cfg.key_width), BF16),
        pltpu.VMEM((tokens, 2 * cfg.key_width), BF16),
        pltpu.VMEM((tokens, cfg.query_width), BF16),
        pltpu.VMEM((2, QROWS, width), BF16),
        pltpu.VMEM((2, QROWS, width), BF16),
        pltpu.VMEM((2, QROWS, width), BF16),
        pltpu.VMEM((QROWS, width), F32),
        pltpu.SemaphoreType.DMA((9,)),
        pltpu.SemaphoreType.DMA((12,)),
        pltpu.SemaphoreType.DMA((1,)),
        pltpu.SemaphoreType.DMA((1,)),
    ]
    for halves in (1, 2, 2, 2, 2, 2):
        scratch += Gather.semaphores(cfg.dp, halves)
    scratch += LineSum.semaphores(cfg.pieces)
    return pl.pallas_call(
        functools.partial(forward_kernel, cfg),
        out_shape=outs,
        in_specs=[
            any_spec,
            pl.BlockSpec(memory_space=pltpu.SMEM),
            pl.BlockSpec(memory_space=pltpu.VMEM),
        ]
        + [any_spec] * 8,
        out_specs=[any_spec] * len(outs),
        scratch_shapes=scratch,
        compiler_params=pltpu.CompilerParams(
            collective_id=1, has_side_effects=True, vmem_limit_bytes=VMEM_LIMIT
        ),
        name="attention_forward",
    )(x, lengths, freq, gains, wq, wk, wv, wo, wg, wu, wd)


def mlp_kernel(cfg, *refs):
    (
        n2_in, wg_in, wu_in, wd_in, dy_in, hidden_in, gains_in,
        terms_out, gate_out, up_out, down_out, db_out, dh_out, gain_out,
        n2, wg, wu, wd, dy, hidden, gains, n2_all, dy_all, act, dgate, dup,
        part, inbox, result, relay, gain_sum,
        load, store, own_sem, swap_send, swap_receive, chunk_send, chunk_receive, *sems,
    ) = refs
    place = Place(cfg.dp, cfg.tensor)
    tokens, width = n2.shape
    units = wg.shape[1]
    block, owners = cfg.block, cfg.dp
    chunk = units // cfg.chunks
    loads = []

    def fetch(source, target):
        copy = pltpu.make_async_copy(source, target, load.at[len(loads)])
        copy.start()
        loads.append(copy)
        return copy

    def weights(i):
        columns = aligned(i, chunk)
        return [
            pltpu.make_async_copy(wg_in.at[:, columns], wg.at[:, columns], load.at[5 + 3 * i]),
            pltpu.make_async_copy(wu_in.at[:, columns], wu.at[:, columns], load.at[6 + 3 * i]),
            pltpu.make_async_copy(wd_in.at[columns], wd.at[columns], load.at[7 + 3 * i]),
        ]

    fetch(n2_in.at[0], n2.at[pl.ds(0, QROWS)])
    fetch(n2_in.at[1], n2.at[pl.ds(QROWS, QROWS)])
    fetch(dy_in, dy)
    for i in range(cfg.chunks):
        for copy in weights(i):
            copy.start()
    fetch(gains_in, gains)
    fetch(hidden_in, hidden)
    place.greet()
    place.meet()
    swaps, owns = [], []
    for k, (source, target) in enumerate([(n2, n2_all), (dy, dy_all)]):
        loads[0 if k == 0 else 2].wait()
        if k == 0:
            loads[1].wait()
        for q in range(owners):
            columns = pl.ds(q * block, block)
            copy = remote(
                source.at[:, aligned(2 * q + 1 - place.c, block)],
                target.at[pl.ds(tokens, tokens), columns],
                swap_send.at[k, q],
                swap_receive.at[k, q],
                place.core,
            )
            copy.start()
            swaps.append(copy)
            copy = pltpu.make_async_copy(
                source.at[:, aligned(2 * q + place.c, block)],
                target.at[pl.ds(0, tokens), columns],
                own_sem.at[k, q],
            )
            copy.start()
            owns.append(copy)

    def exchange(i):
        columns = aligned(i, chunk)
        return [
            remote(
                array.at[pl.ds(0, tokens), columns],
                array.at[pl.ds(tokens, tokens), columns],
                chunk_send.at[k, i],
                chunk_receive.at[k, i],
                place.core,
            )
            for k, array in enumerate((act, dgate, dup))
        ]

    def hidden_units(i, carry):
        columns = aligned(i, chunk)
        for copy in weights(i):
            copy.wait()
        gate = dot(n2[...], wg[:, columns])
        upward = dot(n2[...], wu[:, columns])
        back = dot(dy[...], wd[columns], NT)
        sigmoid = 1.0 / (1.0 + jnp.exp(-gate))
        swish = gate * sigmoid
        act[:tokens, columns] = (swish * upward).astype(BF16)
        dgate[:tokens, columns] = (
            back * upward * sigmoid * (1.0 + gate * (1.0 - sigmoid))
        ).astype(BF16)
        dup[:tokens, columns] = (back * swish).astype(BF16)
        for copy in exchange(i):
            copy.start()
        return carry

    lax.fori_loop(0, cfg.chunks, hidden_units, 0)
    columns_at = width // 4

    def back_through(b):
        def one(i, carry):
            rows, columns = aligned(b, QROWS), aligned(i, columns_at)
            total = dot(dgate[rows], wg[columns], NT) + dot(dup[rows], wu[columns], NT)
            part[b, :, columns] = total.astype(BF16)
            return carry

        lax.fori_loop(0, 4, one, 0)

    def root(i, rows, total):
        local = pl.ds(pl.multiple_of(place.late * QROWS + i * line.rows, line.rows), line.rows)
        source = hidden[rows]
        r = lax.rsqrt(jnp.sum(source * source, -1, keepdims=True) * (1.0 / width) + EPSILON)
        scaled = source * r
        gain_sum[...] += jnp.sum((total * scaled).reshape(line.rows // 8, 8, width), 0)
        e = total * gains[1:2, :].astype(F32)
        mean = jnp.sum(e * scaled, -1, keepdims=True) * (1.0 / width)
        dh = dy[local].astype(F32) + r * (e - scaled * mean)
        hidden[rows] = dh
        result[place.late, rows] = dh.astype(BF16)

    line_count = 4
    line = LineSum(place, part, inbox, result, sems[:line_count], cfg.pieces, root)
    back_through(place.early)
    line.early_start()
    back_through(place.late)
    gain_sum[...] = jnp.zeros_like(gain_sum)
    for copy in loads[3:]:
        copy.wait()
    for copy in owns:
        copy.wait()
    for copy in swaps:
        copy.wait_recv()

    def arrived(i, carry):
        for copy in exchange(i):
            copy.wait_recv()
        return carry

    lax.fori_loop(0, cfg.chunks, arrived, 0)
    down = wd.at[:, pl.ds(0, owners * block)]
    gate_rows = wg.at[pl.ds(0, owners * block)]
    up_rows = wu.at[pl.ds(0, owners * block)]
    scatter = Scatter(place, down, relay, down_out, 1, sems[line_count:])
    stores = []

    def keep(source, target):
        copy = pltpu.make_async_copy(source, target, store.at[len(stores)])
        copy.start()
        stores.append(copy)

    def forward_terms(i):
        columns = aligned(i, columns_at)
        n2[:, columns] = dot(act[:tokens], wd[:, columns]).astype(BF16)

    def grad_down(i):
        rows = aligned(i, units // 4)
        down[rows] = dot(act[:, rows], dy_all[...], TN).astype(BF16)

    def grad_gate(i):
        columns = aligned(i, units // 4)
        gate_rows[:, columns] = dot(n2_all[...], dgate[:, columns], TN).astype(BF16)

    def grad_up(i):
        columns = aligned(i, units // 4)
        up_rows[:, columns] = dot(n2_all[...], dup[:, columns], TN).astype(BF16)

    for copy in swaps:
        copy.wait_send()

    def between(fill, first):
        def one(i, carry):
            line.round(first + i)
            fill(i)
            return carry

        lax.fori_loop(0, 4, one, 0)

    between(forward_terms, 0)
    keep(n2, terms_out)
    between(grad_down, 4)
    scatter.start()
    between(grad_gate, 8)
    keep(gate_rows, gate_out)
    between(grad_up, 12)
    keep(up_rows, up_out)
    line.run(16, line.rounds)
    keep(hidden, dh_out)
    keep(result, db_out)
    keep(gain_sum, gain_out)
    for phase in range(place.bits - 1, 0, -1):
        scatter.pass_on(phase)
    scatter.finish()
    line.drain()

    def gone(i, carry):
        for copy in exchange(i):
            copy.wait_send()
        return carry

    lax.fori_loop(0, cfg.chunks, gone, 0)
    for copy in stores:
        copy.wait()


def mlp_call(cfg, n2, wg, wu, wd, dy, hidden, gains):
    tokens, width, units = cfg.tokens, cfg.width, cfg.hidden_units
    any_spec = pl.BlockSpec(memory_space=pl.ANY)
    shape = jax.ShapeDtypeStruct
    bits = cfg.dp.bit_length() - 1
    mine = cfg.dp * cfg.block
    outs = [
        shape((tokens, width), BF16),
        shape((mine, units), BF16),
        shape((mine, units), BF16),
        shape((1 + bits, units, cfg.block), BF16),
        shape((2, QROWS, width), BF16),
        shape((QROWS, width), F32),
        shape((8, width), F32),
    ]
    scratch = [
        pltpu.VMEM((tokens, width), BF16),
        pltpu.VMEM((width, units), BF16),
        pltpu.VMEM((width, units), BF16),
        pltpu.VMEM((units, width), BF16),
        pltpu.VMEM((tokens, width), BF16),
        pltpu.VMEM((QROWS, width), F32),
        pltpu.VMEM((16, width), BF16),
        pltpu.VMEM((2 * tokens, mine), BF16),
        pltpu.VMEM((2 * tokens, mine), BF16),
        pltpu.VMEM((2 * tokens, units), BF16),
        pltpu.VMEM((2 * tokens, units), BF16),
        pltpu.VMEM((2 * tokens, units), BF16),
        pltpu.VMEM((2, QROWS, width), BF16),
        pltpu.VMEM((2, QROWS, width), BF16),
        pltpu.VMEM((2, QROWS, width), BF16),
        pltpu.VMEM(Scatter.inbox_shape(cfg.dp, units, cfg.block), BF16),
        pltpu.VMEM((8, width), F32),
        pltpu.SemaphoreType.DMA((5 + 3 * cfg.chunks,)),
        pltpu.SemaphoreType.DMA((6,)),
        pltpu.SemaphoreType.DMA((2, cfg.dp)),
        pltpu.SemaphoreType.DMA((2, cfg.dp)),
        pltpu.SemaphoreType.DMA((2, cfg.dp)),
        pltpu.SemaphoreType.DMA((3, cfg.chunks)),
        pltpu.SemaphoreType.DMA((3, cfg.chunks)),
    ]
    scratch += LineSum.semaphores(cfg.pieces)
    scratch += Scatter.semaphores(cfg.dp)
    return pl.pallas_call(
        functools.partial(mlp_kernel, cfg),
        out_shape=outs,
        in_specs=[any_spec] * 7,
        out_specs=[any_spec] * len(outs),
        scratch_shapes=scratch,
        compiler_params=pltpu.CompilerParams(
            collective_id=2, has_side_effects=True, vmem_limit_bytes=VMEM_LIMIT
        ),
        name="feed_forward",
    )(n2, wg, wu, wd, dy, hidden, gains)


def backward_kernel(cfg, *refs):
    (
        db_in, mixed_in, wo_in, qkv_in, q_in, k_in, v_in, normed_in, x_in, dh_in,
        terms_in, hidden_in, gate_in, up_in, gain_in, gains_in, lengths, freq,
        activations_out, grad_out, gate_out, up_out, qkv_out, out_out, gain_out,
        db, wo, wqkv, qh, kh, vh, normed_all, mixed_all, db_all, dqkv, x, dh,
        terms, inbox_two, final, hidden, part, inbox_one, result,
        gate_rows, up_rows, relay_gate, relay_up, relay_qkv, relay_out,
        qkv_rows, out_columns, dmixed, dk, dv, dkv, dkv_in, cosine, sine, bias,
        gains, gain_two, gain_one, gain_rows, gain_box, gain_line,
        load, store, own_sem, swap_send, swap_receive, dkv_send, dkv_receive,
        gain_send, gain_receive, last_send, last_receive, *sems,
    ) = refs
    place = Place(cfg.dp, cfg.tensor)
    tokens, width = x.shape
    heads, groups = cfg.heads, cfg.groups
    query_width, key_width = cfg.query_width, cfg.key_width
    block, owners = cfg.block, cfg.dp
    loads = []

    def fetch(source, target):
        copy = pltpu.make_async_copy(source, target, load.at[len(loads)])
        copy.start()
        loads.append(copy)
        return copy

    first = [
        fetch(db_in, db),
        fetch(wo_in, wo),
        fetch(q_in, qh),
        fetch(k_in, kh),
        fetch(v_in, vh),
        fetch(terms_in.at[pl.ds(0, QROWS)], terms.at[0]),
        fetch(terms_in.at[pl.ds(QROWS, QROWS)], terms.at[1]),
    ]
    wide = [fetch(gate_in, gate_rows), fetch(up_in, up_rows)]
    rest = [
        fetch(hidden_in, hidden),
        fetch(qkv_in, wqkv),
        fetch(mixed_in, mixed_all.at[pl.ds(0, tokens)]),
        fetch(x_in, x),
        fetch(dh_in, dh),
        fetch(gains_in, gains),
        fetch(gain_in, gain_two),
    ]
    barrier = pltpu.get_barrier_semaphore()
    greeted = [place.core]
    for mask in range(1, cfg.dp):
        greeted += [(place.flipped(mask), place.c, place.t), (place.flipped(mask), 1 - place.c, place.t)]
    for step in range(1, cfg.tensor):
        greeted.append((place.p, place.c, lax.rem(place.t + step, cfg.tensor)))
    for device in greeted:
        pl.semaphore_signal(barrier, inc=1, device_id=device, device_id_type=MESH)
    tables(place, lengths, freq, cosine, sine, tokens)
    fill_bias(place, lengths, bias, tokens)
    pl.semaphore_wait(barrier, len(greeted))

    for copy in first[:2]:
        copy.wait()
    swaps, owns = [], []

    def swap(source, target, k, q):
        copy = remote(source, target, swap_send.at[k, q], swap_receive.at[k, q], place.core)
        copy.start()
        swaps.append(copy)

    for q in range(owners):
        columns = pl.ds(q * block, block)
        other, own = aligned(2 * q + 1 - place.c, block), aligned(2 * q + place.c, block)
        swap(normed_in.at[:, other], normed_all.at[pl.ds(tokens, tokens), columns], 0, q)
        copy = pltpu.make_async_copy(
            normed_in.at[:, own], normed_all.at[pl.ds(0, tokens), columns], own_sem.at[0, q]
        )
        copy.start()
        owns.append(copy)
        for b in range(2):
            target = pl.ds(tokens + b * QROWS, QROWS)
            swap(db.at[b, :, other], db_all.at[target, columns], 1 + b, q)
            copy = pltpu.make_async_copy(
                db.at[b, :, own], db_all.at[pl.ds(b * QROWS, QROWS), columns], own_sem.at[1 + b, q]
            )
            copy.start()
            owns.append(copy)
    swap(mixed_in, mixed_all.at[pl.ds(tokens, tokens)], 3, 0)

    n_line, n_scatter = 4, 3
    scatters = []
    for i, (rows, relay, out, axis) in enumerate(
        [
            (out_columns, relay_out, out_out, 1),
            (gate_rows, relay_gate, gate_out, 0),
            (up_rows, relay_up, up_out, 0),
            (qkv_rows, relay_qkv, qkv_out, 0),
        ]
    ):
        at = 2 * n_line + n_scatter * i
        scatters.append(Scatter(place, rows, relay, out, axis, sems[at : at + n_scatter]))
    s_out, s_gate, s_up, s_qkv = scatters

    def local_rows(line, i):
        return pl.ds(pl.multiple_of(place.late * QROWS + i * line.rows, line.rows), line.rows)

    def root_two(i, rows, total):
        final[place.late, rows] = (hidden[rows] + total).astype(BF16)

    def root_one(i, rows, total):
        source = x[local_rows(line_one, i)].astype(F32)
        r = lax.rsqrt(jnp.sum(source * source, -1, keepdims=True) * (1.0 / width) + EPSILON)
        scaled = source * r
        gain_one[...] += jnp.sum((total * scaled).reshape(line_one.rows // 8, 8, width), 0)
        e = total * gains[0:1, :].astype(F32)
        mean = jnp.sum(e * scaled, -1, keepdims=True) * (1.0 / width)
        result[place.late, rows] = (dh[rows] + r * (e - scaled * mean)).astype(BF16)

    line_two = LineSum(place, terms, inbox_two, final, sems[:n_line], cfg.pieces, root_two)
    line_one = LineSum(
        place, part, inbox_one, result, sems[n_line : 2 * n_line], cfg.pieces, root_one
    )
    for copy in first[2:]:
        copy.wait()
    line_two.early_start()
    for copy in wide:
        copy.wait()
    s_gate.start()
    s_up.start()

    def back_out(b, carry):
        product = dot(db[b], wo[...], NT)
        rows = aligned(b, QROWS)
        for h in range(heads):
            dmixed[h, rows] = product[:, h * HD : (h + 1) * HD].astype(BF16)
        return carry

    lax.fori_loop(0, 2, back_out, 0)
    for copy in rest:
        copy.wait()
    dk[...] = jnp.zeros_like(dk)
    dv[...] = jnp.zeros_like(dv)

    def attend_back(b, rounds):
        rows = aligned(b, QROWS)
        window = pl.ds(pl.multiple_of(place.c * b * QROWS, QROWS), bias.shape[1])

        def pair(j, carry):
            outs = []
            for h in range(2):
                head = 2 * j + h
                g = lax.div(head, heads // groups)
                key, value = kh[g, window], vh[g, window]
                query, grad = qh[head, rows], dmixed[head, rows]
                weights = softmax_of(key, query, bias[b])
                dprobs = dot(value, grad, NT)
                delta = jnp.sum(weights * dprobs, 0, keepdims=True)
                dscores = (weights * (dprobs - delta)).astype(BF16)
                dv[g, window] += dot(weights.astype(BF16), grad)
                dk[g, window] += dot(dscores, query)
                outs.append(dot(key, dscores, TN))
            z = jnp.concatenate(outs, 0).T * HD**-0.5
            z = z * cosine[rows] - turned(z) * sine[rows]
            dqkv[rows, aligned(j, 128)] = z.astype(BF16)
            for k in range(2):
                line_two.round(rounds + 2 * j + k)
            return carry

        lax.fori_loop(0, heads // 2, pair, 0)

    attend_back(place.early, 0)
    attend_back(place.late, heads)
    line_two.run(min(2 * heads, line_two.rounds), line_two.rounds)
    stores = []

    def keep(source, target):
        copy = pltpu.make_async_copy(source, target, store.at[len(stores)])
        copy.start()
        stores.append(copy)

    keep(final, activations_out)
    pass_back = remote(dkv, dkv_in, dkv_send.at[0], dkv_receive.at[0], place.core)

    def packed(rows):
        return jnp.concatenate(
            [dk[g, rows] for g in range(groups)] + [dv[g, rows] for g in range(groups)], -1
        )

    @pl.when(place.c == 1)
    def _():
        dkv[...] = packed(pl.ds(0, tokens))
        pass_back.start()

    own_rows = aligned(place.c, tokens)
    z = packed(own_rows)

    @pl.when(place.c == 0)
    def _():
        pass_back.wait_recv()
        dkv[...] = z + dkv_in[...]

    @pl.when(place.c == 1)
    def _():
        pass_back.wait_send()
        dkv[...] = z

    dkeys = dkv[:, :key_width]
    if key_width % 128 == 0:
        wide_by = key_width // 128
        table_c = jnp.concatenate([cosine[...]] * wide_by, -1)
        table_s = jnp.concatenate([sine[...]] * wide_by, -1)
    else:
        table_c, table_s = cosine[:, :key_width], sine[:, :key_width]
    dkeys = dkeys * table_c - turned(dkeys) * table_s
    dqkv[:tokens, query_width : query_width + key_width] = dkeys.astype(BF16)
    dqkv[:tokens, query_width + key_width :] = dkv[:, key_width:].astype(BF16)
    swap(dqkv.at[pl.ds(0, tokens)], dqkv.at[pl.ds(tokens, tokens)], 3, 1)
    columns_at = width // 4

    def back_through(b):
        def one(i, carry):
            rows, columns = aligned(b, QROWS), aligned(i, columns_at)
            part[b, :, columns] = dot(dqkv[rows], wqkv[columns], NT).astype(BF16)
            return carry

        lax.fori_loop(0, 4, one, 0)

    gain_one[...] = jnp.zeros_like(gain_one)
    back_through(place.early)
    line_one.early_start()
    back_through(place.late)
    line_one.run(0, 1)
    for copy in owns:
        copy.wait()
    for copy in swaps:
        copy.wait_recv()
    qkv_rows[...] = dot(normed_all[...], dqkv[...], TN).astype(BF16)
    s_qkv.start()
    line_one.run(1, 3)
    out_columns[...] = dot(mixed_all[...], db_all[...], TN).astype(BF16)
    s_out.start()
    line_one.run(3, 4)
    agenda = []
    for phase in range(place.bits - 1, 0, -1):
        for s in (s_gate, s_up, s_qkv, s_out):
            agenda.append(functools.partial(s.pass_on, phase))
    last_sum = cfg.pieces + line_one.lags[1]
    marks = [4 + (last_sum - 4) * (k + 1) // (len(agenda) + 1) for k in range(len(agenda))]
    at = 4
    for mark, item in zip(marks, agenda):
        line_one.run(at, mark)
        item()
        at = mark
    line_one.run(at, last_sum)

    ends = (0, cfg.tensor - 1)
    mine = place.p * 2 + place.c

    def gain_copy(mask, core):
        index = place.flipped(mask) * 2 + core
        return remote(
            gain_rows.at[:, aligned(index, block)],
            gain_box.at[mine],
            gain_send.at[mask, lax.rem(core + place.c, 2)],
            gain_receive.at[mask, lax.rem(core + place.c, 2)],
            (place.flipped(mask), core, place.t),
        )

    others = [(mask, core) for mask in range(cfg.dp) for core in range(2)]

    @pl.when(place.at_end)
    def _():
        gain_rows[0:1, :] = jnp.sum(gain_one[...], 0, keepdims=True)
        gain_rows[1:2, :] = jnp.sum(gain_two[...], 0, keepdims=True)
        gain_rows[2:, :] = jnp.zeros((6, width), F32)
        for mask in range(cfg.dp):
            for apart in range(2):
                if mask or apart:
                    core = place.c if apart == 0 else 1 - place.c
                    gain_copy(mask, core).start()
        gain_box[mine] = gain_rows[:, aligned(mine, block)]

    line_one.run(last_sum, line_one.rounds - 2)

    def line_copy(step, end):
        return remote(
            gain_line.at[end],
            gain_line.at[end],
            last_send.at[step],
            last_receive.at[end],
            (place.p, place.c, lax.rem(place.t + step, cfg.tensor)),
        )

    for end, at_t in enumerate(ends):

        @pl.when(place.t == at_t)
        def _(end=end):
            for mask in range(cfg.dp):
                for apart in range(2):
                    if mask or apart:
                        core = place.c if apart == 0 else 1 - place.c
                        gain_copy(mask, core).wait_recv()
            gain_line[end] = jnp.sum(gain_box[...], 0)
            for step in range(1, cfg.tensor):
                line_copy(step, end).start()

    line_one.run(line_one.rounds - 2, line_one.rounds)
    keep(result, grad_out)
    for end, at_t in enumerate(ends):

        @pl.when(place.t != at_t)
        def _(end=end):
            line_copy(1, end).wait_recv()

    gain_one[:, :block] = gain_line[0] + gain_line[1]
    keep(gain_one.at[:, pl.ds(0, block)], gain_out)
    for s in scatters:
        s.finish()

    @pl.when(place.at_end)
    def _():
        for mask in range(cfg.dp):
            for apart in range(2):
                if mask or apart:
                    core = place.c if apart == 0 else 1 - place.c
                    gain_copy(mask, core).wait_send()
        for step in range(1, cfg.tensor):
            line_copy(step, 0).wait_send()

    for copy in swaps:
        copy.wait_send()
    line_two.drain()
    line_one.drain()
    for copy in stores:
        copy.wait()


def backward_call(cfg, *operands):
    tokens, width, units = cfg.tokens, cfg.width, cfg.hidden_units
    any_spec = pl.BlockSpec(memory_space=pl.ANY)
    shape = jax.ShapeDtypeStruct
    bits = cfg.dp.bit_length() - 1
    mine = cfg.dp * cfg.block
    heads, groups, qkv_width = cfg.heads, cfg.groups, cfg.qkv_width
    outs = [
        shape((2, QROWS, width), BF16),
        shape((2, QROWS, width), BF16),
        shape((1 + bits, cfg.block, units), BF16),
        shape((1 + bits, cfg.block, units), BF16),
        shape((1 + bits, cfg.block, qkv_width), BF16),
        shape((1 + bits, cfg.query_width, cfg.block), BF16),
        shape((8, cfg.block), F32),
    ]
    halves = (2, QROWS, width)
    scratch = [
        pltpu.VMEM(halves, BF16),
        pltpu.VMEM((cfg.query_width, width), BF16),
        pltpu.VMEM((width, qkv_width), BF16),
        pltpu.VMEM((heads, tokens, HD), BF16),
        pltpu.VMEM((groups, 2 * tokens, HD), BF16),
        pltpu.VMEM((groups, 2 * tokens, HD), BF16),
        pltpu.VMEM((2 * tokens, mine), BF16),
        pltpu.VMEM((2 * tokens, cfg.query_width), BF16),
        pltpu.VMEM((2 * tokens, mine), BF16),
        pltpu.VMEM((2 * tokens, qkv_width), BF16),
        pltpu.VMEM((tokens, width), BF16),
        pltpu.VMEM((QROWS, width), F32),
        pltpu.VMEM(halves, BF16),
        pltpu.VMEM(halves, BF16),
        pltpu.VMEM(halves, BF16),
        pltpu.VMEM((QROWS, width), F32),
        pltpu.VMEM(halves, BF16),
        pltpu.VMEM(halves, BF16),
        pltpu.VMEM(halves, BF16),
        pltpu.VMEM((mine, units), BF16),
        pltpu.VMEM((mine, units), BF16),
        pltpu.VMEM(Scatter.inbox_shape(cfg.dp, cfg.block, units), BF16),
        pltpu.VMEM(Scatter.inbox_shape(cfg.dp, cfg.block, units), BF16),
        pltpu.VMEM(Scatter.inbox_shape(cfg.dp, cfg.block, qkv_width), BF16),
        pltpu.VMEM(Scatter.inbox_shape(cfg.dp, cfg.query_width, cfg.block), BF16),
        pltpu.VMEM((mine, qkv_width), BF16),
        pltpu.VMEM((cfg.query_width, mine), BF16),
        pltpu.VMEM((heads, tokens, HD), BF16),
        pltpu.VMEM((groups, 2 * tokens, HD), F32),
        pltpu.VMEM((groups, 2 * tokens, HD), F32),
        pltpu.VMEM((tokens, 2 * cfg.key_width), F32),
        pltpu.VMEM((tokens, 2 * cfg.key_width), F32),
        pltpu.VMEM((tokens, 128), F32),
        pltpu.VMEM((tokens, 128), F32),
        pltpu.VMEM((2, cfg.window, QROWS), F32),
        pltpu.VMEM((16, width), BF16),
        pltpu.VMEM((8, width), F32),
        pltpu.VMEM((8, width), F32),
        pltpu.VMEM((8, width), F32),
        pltpu.VMEM((2 * cfg.dp, 8, cfg.block), F32),
        pltpu.VMEM((2, 8, cfg.block), F32),
        pltpu.SemaphoreType.DMA((16,)),
        pltpu.SemaphoreType.DMA((3,)),
        pltpu.SemaphoreType.DMA((3, cfg.dp)),
        pltpu.SemaphoreType.DMA((4, max(cfg.dp, 2))),
        pltpu.SemaphoreType.DMA((4, max(cfg.dp, 2))),
        pltpu.SemaphoreType.DMA((1,)),
        pltpu.SemaphoreType.DMA((1,)),
        pltpu.SemaphoreType.DMA((cfg.dp, 2)),
        pltpu.SemaphoreType.DMA((cfg.dp, 2)),
        pltpu.SemaphoreType.DMA((cfg.tensor,)),
        pltpu.SemaphoreType.DMA((2,)),
    ]
    scratch += LineSum.semaphores(cfg.pieces) * 2
    scratch += Scatter.semaphores(cfg.dp) * 4
    in_specs = [any_spec] * 16 + [
        pl.BlockSpec(memory_space=pltpu.SMEM),
        pl.BlockSpec(memory_space=pltpu.VMEM),
    ]
    return pl.pallas_call(
        functools.partial(backward_kernel, cfg),
        out_shape=outs,
        in_specs=in_specs,
        out_specs=[any_spec] * len(outs),
        scratch_shapes=scratch,
        compiler_params=pltpu.CompilerParams(
            collective_id=3, has_side_effects=True, vmem_limit_bytes=VMEM_LIMIT
        ),
        name="attention_backward",
    )(*operands)


def solution(mesh):
    dp, tensor = mesh.shape["dp"], mesh.shape["tensor"]

    def shards(
        inputs, cotangent, doc_lengths, gain_attn, w_query, w_key, w_value, w_out, gain_mlp,
        w_gate, w_up, w_down,
    ):
        tokens, width = inputs.shape
        cfg = Config(
            dp,
            tensor,
            tokens,
            width,
            w_query.shape[1] // HD,
            w_key.shape[1] // HD,
            w_gate.shape[1],
        )
        freq = jnp.tile(frequencies(), (8, 4))
        gains = jnp.zeros((16, gain_attn.shape[0]), F32).at[0].set(gain_attn).at[1].set(gain_mlp)
        (
            wqkv, wo, wg, wu, wd, gains_full, normed, q, k, v, mixed, hidden, normed_mlp,
        ) = forward_call(
            cfg, inputs, doc_lengths, freq, gains, w_query, w_key, w_value, w_out, w_gate, w_up, w_down
        )
        terms, gate_rows, up_rows, down_terms, db, dh, gain_two = mlp_call(
            cfg, normed_mlp, wg, wu, wd, cotangent, hidden, gains_full
        )
        activations, input_grad, gate_terms, up_terms, qkv_terms, out_terms, gain_sums = (
            backward_call(
                cfg, db, mixed, wo, wqkv, q, k, v, normed, inputs, dh, terms, hidden,
                gate_rows, up_rows, gain_two, gains_full, doc_lengths, freq,
            )
        )

        def total(pieces):
            return jnp.sum(pieces.astype(F32), 0)

        qkv_grad = total(qkv_terms)
        query_width, key_width = cfg.query_width, cfg.key_width
        return (
            activations.reshape(tokens, width),
            input_grad.reshape(tokens, width).astype(F32),
            gain_sums[0],
            qkv_grad[:, :query_width],
            qkv_grad[:, query_width : query_width + key_width],
            qkv_grad[:, query_width + key_width :],
            total(out_terms),
            gain_sums[1],
            total(gate_terms),
            total(up_terms),
            total(down_terms),
        )

    rows, columns, gain = P(("dp", "context"), "tensor"), P("tensor", ("dp", "context")), P(("dp", "context"))
    tokens = P(("dp", "context"), None)
    return jax.shard_map(
        shards,
        mesh=mesh,
        in_specs=(tokens, tokens, P("dp", None), gain, rows, rows, rows, columns, gain, rows, rows, columns),
        out_specs=(tokens, tokens, gain, rows, rows, rows, columns, gain, rows, rows, columns),
        check_vma=False,
    )
```

time: 1080 us -> 445 us (0.41)
  waiting for transfers between devices: 740 us -> 0 us
  Pallas kernels: 0 us -> 417 us
  matrix products: 167 us -> 0 us
  blocking collectives: 68 us -> 0 us
  other arithmetic: 75.4 us -> 10 us
  between operations: 15.3 us -> 1.14 us
    pallas_call x0 -> x3, Pallas kernels: none -> 417 us  [the longest x1 172 us: forward_call(): pl.pallas_call(functools.partial(forward_kernel, cfg), out_shape=outs, in...]
    psum x3 -> x0, waiting for transfers between devices: 313 us -> none  [the longest x1 157 us: shards(): lax.psum(mlp_terms.astype(jnp.bfloat16), 'tensor').astype(jnp.float32)]
    reduce_scatter x9 -> x0, waiting for transfers between devices: 281 us -> none  [the longest x1 72.2 us: shards(): lax.psum_scatter(grad_gate.astype(jnp.bfloat16), ('dp', 'context'), scatt...]
    dot_general x27 -> x0, matrix products: 167 us -> none  [the longest x1 13.8 us: shards(): jnp.einsum('td,fd->tf', cotangent, down_full, preferred_element_type=jnp....]
    all_gather x5 -> x0, waiting for transfers between devices: 145 us -> none  [the longest x1 51 us: shards(): lax.all_gather(mlp_copy[2], ('dp', 'context'), axis=0, tiled=True)]
    all_gather x6 -> x0, blocking collectives: 44 us -> none  [the longest x1 11 us: shards(): lax.all_gather(attention_copy[3], ('dp', 'context'), axis=0, tiled=True)]
    convert_element_type x26 -> x1, other arithmetic: 44.5 us -> 2.8 us  [shards(): input_grad.reshape(tokens, width).astype(F32)]
    unnamed x1 -> x0, blocking collectives: 24 us -> none
  transfers between devices with their start and end apart: 17 -> 0, of which waited for: 13 -> 0; matrix products, arithmetic and copies ran while one was open for 16% -> 0% of each run, Pallas kernels for 0% -> 0%
where the time goes in v2:
time: 445 us; the launch traced here: 437 us
  Pallas kernels  417 us (94%)
  other arithmetic  10 us (2%)
  local copies, waits for them, and re-layouts  9.28 us (2%)
    pallas_call x1, Pallas kernels, forward_call(): pl.pallas_call(functools.partial(forward_kernel, cfg), out_shape=outs, in...  172 us
    pallas_call x1, Pallas kernels, backward_call(): pl.pallas_call(functools.partial(backward_kernel, cfg), out_shape=outs, i...  140 us
    pallas_call x1, Pallas kernels, mlp_call(): pl.pallas_call(functools.partial(mlp_kernel, cfg), out_shape=outs, in_spe...  104 us

profile of v2, /device:TPU:0, one launch (start us, length us, event | category | flops | bytes accessed | tf_op | source)
XLA Modules:
  0.0 437.0 jit_solution(16203249480528128076)
XLA Ops:
  0.7 0.1 tile.17
  0.8 0.6 tile.18.refs_2_.refs_17_
  1.4 0.7 scatter.6
  2.0 0.7 scatter.9.refs_3_
  2.7 0.0 copy-start.6
  2.7 0.6 copy-done.6
  3.3 172.5 %attention_forward.1 = (bf16[2048,768]{1,0:T(8,128)(2,1)}, bf16[512,2048]{1,0:T(8,128)(2,1)}, bf16[2048,2048]{1,0:T(8,128)(2,1)}, bf16[2048,2048]{1,0:T(8,128)(2...) custom-call(bf16[512,2048]{1,0:T(8,128)(2,1)} %refs_8_.3, ...), custom_call_target="tpu_custom_call" | custom-call | tf_op jit(solution)/shard_map/attention_forward/pallas_call | solution.py:783
  175.8 104.2 %feed_forward.1 = (bf16[512,2048]{1,0:T(8,128)(2,1)}, bf16[1024,2048]{1,0:T(8,128)(2,1)}, bf16[1024,2048]{1,0:T(8,128)(2,1)}, bf16[3,2048,256]{2,1,0:T(8,128)(2,...) custom-call(bf16[2,256,2048]{2,1,0:T(8,128)(2,1)} %get-tuple-element.62.refs_0_, ...), custom_call_target="tpu_custom_call" | custom-call | tf_op jit(solution)/shard_map/feed_forward/pallas_call | solution.py:1046
  280.1 139.9 %attention_backward.1 = (bf16[2,256,2048]{2,1,0:T(8,128)(2,1)}, bf16[2,256,2048]{2,1,0:T(8,128)(2,1)}, bf16[3,256,2048]{2,1,0:T(8,128)(2,1)}, bf16[3,256,2048]{2...) custom-call(bf16[2,256,2048]{2,1,0:T(8,128)(2,1)} %get-tuple-element.68.refs_0_, ...), custom_call_target="tpu_custom_call" | custom-call | tf_op jit(solution)/shard_map/attention_backward/pallas_call | solution.py:1469
  420.0 0.0 copy-start.5
  420.0 1.4 fusion.1
  421.3 2.1 convert_reduce_fusion.4
  423.4 0.0 copy-done.5
  423.4 0.0 copy-start
  423.4 0.2 convert_reduce_fusion.3
  423.6 0.7 fusion
  424.3 0.9 slice.49
  425.2 0.4 copy-done
  425.6 0.0 copy-start.3
  425.6 1.7 convert_reduce_fusion
  427.3 0.4 copy-done.3
  427.7 0.0 copy-start.1
  427.7 0.0 copy-start.2
  427.7 2.8 bitcast_convert_fusion
  430.5 0.0 copy-done.1
  430.5 1.6 copy-done.2
  432.0 0.0 copy-start.4
  432.0 3.2 convert_reduce_fusion.1
  435.3 0.0 copy-done.4
  435.3 1.3 copy.25
  (2 shorter events, 0.0 us)
Async XLA Ops:
  2.7 0.6 copy-start.6
  420.0 3.5 copy-start.5
  423.4 2.1 copy-start
  425.6 2.1 copy-start.3
  427.7 2.8 copy-start.1
  427.7 4.4 copy-start.2
  432.0 3.2 copy-start.4

commit v3 on v2

--- a/solution.py
+++ b/solution.py
@@ -509,43 +509,60 @@
 
 def forward_kernel(cfg, *refs):
     (
-        x_in, lengths, freq, gains_in, wq_in, wk_in, wv_in, wo_in, wg_in, wu_in, wd_in,
-        qkv_out, wo_out, wg_full, wu_full, wd_full, gains_out,
-        normed_out, q_out, k_out, v_out, mixed_out, hidden_out, normed_mlp_out,
-        x, wq, wk, wv, wo, wg, wu, wd, gains32,
-        sqkv, swo, swg, swu, swd, sgains,
+        x_in, dy_in, lengths, freq, gains_in, wq_in, wk_in, wv_in, wo_in, wg_in, wu_in, wd_in,
+        gu_full, wd_full,
+        qkv_out, wo_out, gains_out, normed_out, q_out, k_out, v_out, mixed_out, hidden_out,
+        n2_all, dy_all, act_all, dgu_all, dn2_out, terms_out,
+        x, wq, wk, wv, wo, wraw, wd, gains32,
+        sqkv, swo, sgu, swd, sgains,
         wqkv, wout, gains, normed, rscale, cosine, sine, bias,
         qh, kh, vh, kv, kv_in, mixed, part, inbox, result, hidden,
-        load, store, kv_send, kv_receive, *sems,
+        gu_buffer, wd_buffer, act, dgu, dn2_sum, terms_sum,
+        load, store, kv_send, kv_receive, fill, spill, swap_send, swap_receive,
+        chunk_send, chunk_receive, *sems,
     ) = refs
     place = Place(cfg.dp, cfg.tensor)
     tokens, width = x.shape
     heads, groups = cfg.heads, cfg.groups
-    query_width, key_width = heads * HD, groups * HD
+    query_width, key_width = cfg.query_width, cfg.key_width
+    units, chunks = cfg.hidden_units, cfg.chunks
+    chunk = units // chunks
+    block, owners = cfg.block, cfg.dp
     loads = []
-    for i, (source, target) in enumerate(
-        [(gains_in, gains32), (wq_in, wq), (wk_in, wk), (wv_in, wv), (x_in, x), (wo_in, wo), (wg_in, wg), (wu_in, wu), (wd_in, wd)]
-    ):
-        copy = pltpu.make_async_copy(source, target, load.at[i])
+
+    def fetch(source, target):
+        copy = pltpu.make_async_copy(source, target, load.at[len(loads)])
         copy.start()
         loads.append(copy)
+        return copy
+
+    small = [
+        fetch(source, target)
+        for source, target in ((gains_in, gains32), (wq_in, wq), (wk_in, wk), (wv_in, wv))
+    ]
+    load_x, load_wo = fetch(x_in, x), fetch(wo_in, wo)
+    load_wg, load_wd = fetch(wg_in, wraw), fetch(wd_in, wd)
     place.greet()
+    n_sems = 5
     gathers = []
-    for i, (shard, full, axis, halves) in enumerate(
-        [
-            (sgains, gains, 1, 1),
-            (sqkv, wqkv, 0, 2),
-            (swo, wout, 1, 2),
-            (swg, wg_full, 0, 2),
-            (swu, wu_full, 0, 2),
-            (swd, wd_full, 1, 2),
-        ]
-    ):
-        gathers.append(Gather(place, shard, full, axis, sems[5 * i : 5 * i + 5], halves))
-    g_gains, g_qkv, g_wo, g_wg, g_wu, g_wd = gathers
-    line_sems = sems[5 * len(gathers) :]
-    for i in range(4):
-        loads[i].wait()
+
+    def gather(shard, full, axis, halves=2):
+        at = n_sems * len(gathers)
+        gathers.append(Gather(place, shard, full, axis, sems[at : at + n_sems], halves))
+        return gathers[-1]
+
+    g_gains = gather(sgains, gains, 1, 1)
+    g_qkv = gather(sqkv, wqkv, 0)
+    g_wo = gather(swo, wout, 1)
+    g_gu, g_wd = [], []
+    for i in range(chunks):
+        columns = pl.ds(i * 2 * chunk, 2 * chunk)
+        g_gu.append(gather(sgu.at[:, columns], gu_full.at[:, columns], 0))
+        rows = pl.ds(i * chunk, chunk)
+        g_wd.append(gather(swd.at[rows], wd_full.at[rows], 1))
+    line_sems = sems[n_sems * len(gathers) :]
+    for copy in small:
+        copy.wait()
     sgains[...] = gains32[...].astype(BF16)
     sqkv[:, :query_width] = wq[...].astype(BF16)
     sqkv[:, query_width : query_width + key_width] = wk[...].astype(BF16)
@@ -553,35 +570,41 @@
     place.meet()
     g_gains.start()
     g_qkv.start()
-    loads[5].wait()
+    load_wo.wait()
     swo[...] = wo[...].astype(BF16)
-    for i, (raw, staged) in enumerate([(wg, swg), (wu, swu), (wd, swd)]):
-        loads[6 + i].wait()
-        pieces = 8
-        for n in range(pieces):
-            rows = pl.ds(n * (raw.shape[0] // pieces), raw.shape[0] // pieces)
-            staged[rows] = raw[rows].astype(BF16)
+
+    def stage(second):
+        for i in range(chunks):
+            first = (2 * i + second) * chunk
+            sgu[:, first : first + chunk] = wraw[:, i * chunk : (i + 1) * chunk].astype(BF16)
+
+    load_wg.wait()
+    stage(0)
+    load_wu = fetch(wu_in, wraw)
     for phase in range(place.bits):
         g_gains.pass_on(phase)
         g_qkv.pass_on(phase)
         if phase == 0:
             g_wo.start()
-            g_wg.start()
-            g_wu.start()
-            g_wd.start()
-            loads[4].wait()
+            load_x.wait()
             rows_at = 64
 
             def scale(i, carry):
                 rows = aligned(i, rows_at)
-                block = x[rows].astype(F32)
-                mean = jnp.sum(block * block, -1, keepdims=True) * (1.0 / width)
+                wide = x[rows].astype(F32)
+                mean = jnp.sum(wide * wide, -1, keepdims=True) * (1.0 / width)
                 rscale[rows] = lax.rsqrt(mean + EPSILON)
                 return carry
 
             lax.fori_loop(0, tokens // rows_at, scale, 0)
             tables(place, lengths, freq, cosine, sine, tokens)
             fill_bias(place, lengths, bias, tokens)
+            load_wu.wait()
+            stage(1)
+            load_wd.wait()
+            for i in range(chunks):
+                rows = pl.ds(i * chunk, chunk)
+                swd[rows] = wd[rows].astype(BF16)
     g_gains.finish()
 
     def norm(i, carry):
@@ -597,20 +620,35 @@
         copy = pltpu.make_async_copy(source, target, store.at[len(stores)])
         copy.start()
         stores.append(copy)
-
-    keep(normed, normed_out)
+        return copy
+
+    normed_kept = keep(normed, normed_out)
     keep(gains, gains_out)
     g_qkv.finish()
     keep(wqkv, qkv_out)
+
+    def begin(i):
+        g_gu[i].start()
+        g_wd[i].start()
+
+    def advance(i, phase):
+        g_gu[i].pass_on(phase)
+        g_wd[i].pass_on(phase)
+
     for b in range(tokens // QROWS):
         rows = pl.ds(b * QROWS, QROWS)
         product = dot(normed[rows], wqkv[...])
+        if b == 0:
+            if place.bits:
+                g_wo.pass_on(0)
+            begin(0)
+            begin(1)
         table_c, table_s = cosine[rows], sine[rows]
-        for block in range(query_width // 128):
-            z = product[:, block * 128 : (block + 1) * 128]
+        for column in range(query_width // 128):
+            z = product[:, column * 128 : (column + 1) * 128]
             z = (z * table_c + turned(z) * table_s) * HD**-0.5
             for h in range(2):
-                qh[2 * block + h, rows] = z[:, h * HD : (h + 1) * HD].astype(BF16)
+                qh[2 * column + h, rows] = z[:, h * HD : (h + 1) * HD].astype(BF16)
         z = product[:, query_width : query_width + key_width]
         if key_width % 128 == 0:
             wide = key_width // 128
@@ -645,8 +683,9 @@
     keep(qh, q_out)
     keep(kh, k_out)
     keep(vh, v_out)
-    if place.bits:
-        g_wo.pass_on(0)
+    normed_kept.wait()
+    dy = normed
+    load_dy = fetch(dy_in, dy)
 
     def attend(b):
         rows = aligned(b, QROWS)
@@ -686,32 +725,171 @@
     attend(place.late)
     project(place.late)
     keep(mixed, mixed_out)
-    agenda = []
-    for g in (g_wg, g_wu, g_wd):
-        for phase in range(place.bits):
-            agenda.append(functools.partial(g.pass_on, phase))
-    marks = [line.rounds * (k + 1) // (len(agenda) + 1) for k in range(len(agenda))]
+
+    swaps, owns = [], []
+
+    def swap(source, target, k, q, target_rows, sub):
+        columns = pl.ds(q * block, block)
+        copy = remote(
+            source.at[:, aligned(2 * q + 1 - place.c, block)],
+            target.at[pl.ds(tokens + sub, target_rows), columns],
+            swap_send.at[k, q],
+            swap_receive.at[k, q],
+            place.core,
+        )
+        copy.start()
+        swaps.append(copy)
+        copy = pltpu.make_async_copy(
+            source.at[:, aligned(2 * q + place.c, block)],
+            target.at[pl.ds(sub, target_rows), columns],
+            fill.at[k, q],
+        )
+        copy.start()
+        owns.append(copy)
+
+    load_dy.wait()
+    for q in range(owners):
+        swap(dy, dy_all, 0, q, tokens, 0)
+
+    agenda = [(2, advance, 0, 0), (2, begin, 2), (9, advance, 1, 0), (9, begin, 3)]
+    if not place.bits:
+        agenda = [item for item in agenda if item[1] is begin]
     at = 0
-    for mark, item in zip(marks, agenda):
+    for mark, action, *rest in agenda:
         line.run(at, mark)
-        item()
+        action(*rest)
         at = mark
     line.run(at, line.rounds)
-    copy_back = pltpu.make_async_copy(result, normed_mlp_out, store.at[len(stores)])
-    copy_back.start()
-    stores.append(copy_back)
+    for i in range(2):
+        for phase in range(1, place.bits):
+            advance(i, phase)
+    if place.bits:
+        advance(2, 0)
+    for b in range(2):
+        for q in range(owners):
+            swap(result.at[b], n2_all, 1 + b, q, QROWS, b * QROWS)
     keep(hidden, hidden_out)
-    for g in (g_wg, g_wu, g_wd):
-        g.finish()
+
+    def chunk_load(i):
+        slot = i % 2
+        return [
+            pltpu.make_async_copy(
+                gu_full.at[:, pl.ds(i * 2 * chunk, 2 * chunk)], gu_buffer.at[slot], spill.at[slot, 0]
+            ),
+            pltpu.make_async_copy(
+                wd_full.at[pl.ds(i * chunk, chunk)], wd_buffer.at[slot], spill.at[slot, 1]
+            ),
+        ]
+
+    def take(i):
+        g_gu[i].finish()
+        g_wd[i].finish()
+        for copy in chunk_load(i):
+            copy.start()
+
+    def give(i):
+        slot = i % 2
+        act_columns, dgu_columns = pl.ds(i * chunk, chunk), pl.ds(i * 2 * chunk, 2 * chunk)
+        copies = []
+        for k, (source, target, columns) in enumerate(
+            ((act, act_all, act_columns), (dgu, dgu_all, dgu_columns))
+        ):
+            copies.append(
+                pltpu.make_async_copy(
+                    source.at[slot], target.at[pl.ds(0, tokens), columns], spill.at[slot, 2 + k]
+                )
+            )
+            copies.append(
+                remote(
+                    source.at[slot],
+                    target.at[pl.ds(tokens, tokens), columns],
+                    chunk_send.at[i, k],
+                    chunk_receive.at[i, k],
+                    place.core,
+                )
+            )
+        return copies
+
+    tile = width // 4
+    n2 = result[...].reshape(tokens, width)
+    take(0)
+    for i in range(chunks):
+        slot = i % 2
+        for copy in chunk_load(i):
+            copy.wait()
+        if i + 1 < chunks:
+            if i == 0:
+                take(1)
+        if i >= 2:
+            own_act, sent_act, own_dgu, sent_dgu = give(i - 2)
+            own_act.wait()
+            own_dgu.wait()
+            sent_act.wait_send()
+            sent_dgu.wait_send()
+        n2 = result[...].reshape(tokens, width)
+        both = dot(n2, gu_buffer[slot])
+        back = dot(dy[...], wd_buffer[slot], NT)
+        gate, upward = both[:, :chunk], both[:, chunk:]
+        sigmoid = 1.0 / (1.0 + jnp.exp(-gate))
+        swish = gate * sigmoid
+        act[slot] = (swish * upward).astype(BF16)
+        dgu[slot, :, :chunk] = (
+            back * upward * sigmoid * (1.0 + gate * (1.0 - sigmoid))
+        ).astype(BF16)
+        dgu[slot, :, chunk:] = (back * swish).astype(BF16)
+        for copy in give(i):
+            copy.start()
+
+        def add(n, carry, i=i, slot=slot):
+            columns = aligned(n, tile)
+            more = dot(dgu[slot], gu_buffer[slot, columns], NT)
+            terms = dot(act[slot], wd_buffer[slot, :, columns])
+            if i:
+                more = more + dn2_sum[:, columns]
+                terms = terms + terms_sum[:, columns]
+            if i + 1 < chunks:
+                dn2_sum[:, columns] = more
+                terms_sum[:, columns] = terms
+            else:
+                for b in range(2):
+                    part[b, :, columns] = more[b * QROWS : (b + 1) * QROWS].astype(BF16)
+                    inbox[b, :, columns] = terms[b * QROWS : (b + 1) * QROWS].astype(BF16)
+            return carry
+
+        if i + 1 == chunks:
+            line.drain()
+        lax.fori_loop(0, 4, add, 0)
+        if 2 <= i + 1 < chunks:
+            if i + 2 < chunks and place.bits:
+                advance(i + 2, 0)
+            for phase in range(1, place.bits):
+                advance(i + 1, phase)
+            take(i + 1)
+    keep(part, dn2_out)
+    keep(inbox, terms_out)
+    for i in range(max(chunks - 2, 0), chunks):
+        own_act, sent_act, own_dgu, sent_dgu = give(i)
+        own_act.wait()
+        own_dgu.wait()
+        sent_act.wait_send()
+        sent_dgu.wait_send()
+    for i in range(chunks):
+        own_act, sent_act, own_dgu, sent_dgu = give(i)
+        sent_act.wait_recv()
+        sent_dgu.wait_recv()
     for g in gathers:
         g.drain()
-    line.drain()
+    for copy in owns:
+        copy.wait()
+    for copy in swaps:
+        copy.wait_recv()
+        copy.wait_send()
 
     @pl.when(place.c == 0)
     def _():
         pass_kv.wait_send()
 
-    for copy in stores:
+    for copy in stores[1:]:
         copy.wait()
 
 
@@ -721,6 +899,7 @@
         self.heads, self.groups, self.hidden_units = heads, groups, hidden_units
         self.pieces = 8
         self.chunks = 4
+        self.marks = (4, 4, 11)
         self.query_width, self.key_width = heads * HD, groups * HD
         self.qkv_width = self.query_width + 2 * self.key_width
         self.blocks = dp * 2
@@ -728,16 +907,17 @@
         self.window = WINDOW + QROWS
 
 
-def forward_call(cfg, x, lengths, freq, gains, wq, wk, wv, wo, wg, wu, wd):
+def forward_call(cfg, x, dy, lengths, freq, gains, wq, wk, wv, wo, wg, wu, wd):
     tokens, width, units = cfg.tokens, cfg.width, cfg.hidden_units
     any_spec = pl.BlockSpec(memory_space=pl.ANY)
     shape = jax.ShapeDtypeStruct
+    mine = cfg.dp * cfg.block
+    chunk = units // cfg.chunks
     outs = [
+        shape((width, 2 * units), BF16),
+        shape((units, width), BF16),
         shape((width, cfg.qkv_width), BF16),
         shape((cfg.query_width, width), BF16),
-        shape((width, units), BF16),
-        shape((width, units), BF16),
-        shape((units, width), BF16),
         shape((16, width), BF16),
         shape((tokens, width), BF16),
         shape((cfg.heads, tokens, HD), BF16),
@@ -745,14 +925,20 @@
         shape((cfg.groups, 2 * tokens, HD), BF16),
         shape((tokens, cfg.query_width), BF16),
         shape((QROWS, width), F32),
+        shape((2 * tokens, mine), BF16),
+        shape((2 * tokens, mine), BF16),
+        shape((2 * tokens, units), BF16),
+        shape((2 * tokens, 2 * units), BF16),
+        shape((2, QROWS, width), BF16),
         shape((2, QROWS, width), BF16),
     ]
-    shards = [wq, wk, wv, wo, wg, wu, wd]
     scratch = [pltpu.VMEM(x.shape, BF16)]
-    scratch += [pltpu.VMEM(w.shape, F32) for w in shards]
-    scratch += [pltpu.VMEM(gains.shape, F32)]
+    scratch += [pltpu.VMEM(w.shape, F32) for w in (wq, wk, wv, wo, wg, wd, gains)]
     scratch += [pltpu.VMEM((wq.shape[0], cfg.qkv_width), BF16)]
-    scratch += [pltpu.VMEM(w.shape, BF16) for w in (wo, wg, wu, wd, gains)]
+    scratch += [pltpu.VMEM(wo.shape, BF16)]
+    scratch += [pltpu.VMEM((wg.shape[0], 2 * units), BF16)]
+    scratch += [pltpu.VMEM(wd.shape, BF16)]
+    scratch += [pltpu.VMEM(gains.shape, BF16)]
     scratch += [
         pltpu.VMEM((width, cfg.qkv_width), BF16),
         pltpu.VMEM((cfg.query_width, width), BF16),
@@ -772,18 +958,31 @@
         pltpu.VMEM((2, QROWS, width), BF16),
         pltpu.VMEM((2, QROWS, width), BF16),
         pltpu.VMEM((QROWS, width), F32),
-        pltpu.SemaphoreType.DMA((9,)),
-        pltpu.SemaphoreType.DMA((12,)),
+        pltpu.VMEM((2, width, 2 * chunk), BF16),
+        pltpu.VMEM((2, chunk, width), BF16),
+        pltpu.VMEM((2, tokens, chunk), BF16),
+        pltpu.VMEM((2, tokens, 2 * chunk), BF16),
+        pltpu.VMEM((tokens, width), F32),
+        pltpu.VMEM((tokens, width), F32),
+        pltpu.SemaphoreType.DMA((10,)),
+        pltpu.SemaphoreType.DMA((14,)),
         pltpu.SemaphoreType.DMA((1,)),
         pltpu.SemaphoreType.DMA((1,)),
+        pltpu.SemaphoreType.DMA((3, cfg.dp)),
+        pltpu.SemaphoreType.DMA((2, 4)),
+        pltpu.SemaphoreType.DMA((3, cfg.dp)),
+        pltpu.SemaphoreType.DMA((3, cfg.dp)),
+        pltpu.SemaphoreType.DMA((cfg.chunks, 2)),
+        pltpu.SemaphoreType.DMA((cfg.chunks, 2)),
     ]
-    for halves in (1, 2, 2, 2, 2, 2):
+    for halves in [1] + [2] * (2 + 2 * cfg.chunks):
         scratch += Gather.semaphores(cfg.dp, halves)
     scratch += LineSum.semaphores(cfg.pieces)
     return pl.pallas_call(
         functools.partial(forward_kernel, cfg),
         out_shape=outs,
         in_specs=[
+            any_spec,
             any_spec,
             pl.BlockSpec(memory_space=pltpu.SMEM),
             pl.BlockSpec(memory_space=pltpu.VMEM),
@@ -795,21 +994,20 @@
             collective_id=1, has_side_effects=True, vmem_limit_bytes=VMEM_LIMIT
         ),
         name="attention_forward",
-    )(x, lengths, freq, gains, wq, wk, wv, wo, wg, wu, wd)
+    )(x, dy, lengths, freq, gains, wq, wk, wv, wo, wg, wu, wd)
 
 
 def mlp_kernel(cfg, *refs):
     (
-        n2_in, wg_in, wu_in, wd_in, dy_in, hidden_in, gains_in,
-        terms_out, gate_out, up_out, down_out, db_out, dh_out, gain_out,
-        n2, wg, wu, wd, dy, hidden, gains, n2_all, dy_all, act, dgate, dup,
+        dn2_in, n2_in, dy_all_in, act_in, dgu_in, dy_in, hidden_in, gains_in,
+        gu_out, down_out, db_out, dh_out, gain_out,
+        dy, hidden, gains, n2_all, dy_all, act, dgu, gu_rows, down,
         part, inbox, result, relay, gain_sum,
-        load, store, own_sem, swap_send, swap_receive, chunk_send, chunk_receive, *sems,
+        load, store, *sems,
     ) = refs
     place = Place(cfg.dp, cfg.tensor)
-    tokens, width = n2.shape
-    units = wg.shape[1]
-    block, owners = cfg.block, cfg.dp
+    tokens, width = dy.shape
+    units = act.shape[1]
     chunk = units // cfg.chunks
     loads = []
 
@@ -819,90 +1017,13 @@
         loads.append(copy)
         return copy
 
-    def weights(i):
-        columns = aligned(i, chunk)
-        return [
-            pltpu.make_async_copy(wg_in.at[:, columns], wg.at[:, columns], load.at[5 + 3 * i]),
-            pltpu.make_async_copy(wu_in.at[:, columns], wu.at[:, columns], load.at[6 + 3 * i]),
-            pltpu.make_async_copy(wd_in.at[columns], wd.at[columns], load.at[7 + 3 * i]),
-        ]
-
-    fetch(n2_in.at[0], n2.at[pl.ds(0, QROWS)])
-    fetch(n2_in.at[1], n2.at[pl.ds(QROWS, QROWS)])
-    fetch(dy_in, dy)
-    for i in range(cfg.chunks):
-        for copy in weights(i):
-            copy.start()
-    fetch(gains_in, gains)
-    fetch(hidden_in, hidden)
+    load_part = fetch(dn2_in, part)
+    first = [fetch(dy_in, dy), fetch(hidden_in, hidden), fetch(gains_in, gains)]
+    second = [fetch(act_in, act), fetch(dy_all_in, dy_all)]
+    third = [fetch(n2_in, n2_all), fetch(dgu_in, dgu)]
     place.greet()
+    gain_sum[...] = jnp.zeros_like(gain_sum)
     place.meet()
-    swaps, owns = [], []
-    for k, (source, target) in enumerate([(n2, n2_all), (dy, dy_all)]):
-        loads[0 if k == 0 else 2].wait()
-        if k == 0:
-            loads[1].wait()
-        for q in range(owners):
-            columns = pl.ds(q * block, block)
-            copy = remote(
-                source.at[:, aligned(2 * q + 1 - place.c, block)],
-                target.at[pl.ds(tokens, tokens), columns],
-                swap_send.at[k, q],
-                swap_receive.at[k, q],
-                place.core,
-            )
-            copy.start()
-            swaps.append(copy)
-            copy = pltpu.make_async_copy(
-                source.at[:, aligned(2 * q + place.c, block)],
-                target.at[pl.ds(0, tokens), columns],
-                own_sem.at[k, q],
-            )
-            copy.start()
-            owns.append(copy)
-
-    def exchange(i):
-        columns = aligned(i, chunk)
-        return [
-            remote(
-                array.at[pl.ds(0, tokens), columns],
-                array.at[pl.ds(tokens, tokens), columns],
-                chunk_send.at[k, i],
-                chunk_receive.at[k, i],
-                place.core,
-            )
-            for k, array in enumerate((act, dgate, dup))
-        ]
-
-    def hidden_units(i, carry):
-        columns = aligned(i, chunk)
-        for copy in weights(i):
-            copy.wait()
-        gate = dot(n2[...], wg[:, columns])
-        upward = dot(n2[...], wu[:, columns])
-        back = dot(dy[...], wd[columns], NT)
-        sigmoid = 1.0 / (1.0 + jnp.exp(-gate))
-        swish = gate * sigmoid
-        act[:tokens, columns] = (swish * upward).astype(BF16)
-        dgate[:tokens, columns] = (
-            back * upward * sigmoid * (1.0 + gate * (1.0 - sigmoid))
-        ).astype(BF16)
-        dup[:tokens, columns] = (back * swish).astype(BF16)
-        for copy in exchange(i):
-            copy.start()
-        return carry
-
-    lax.fori_loop(0, cfg.chunks, hidden_units, 0)
-    columns_at = width // 4
-
-    def back_through(b):
-        def one(i, carry):
-            rows, columns = aligned(b, QROWS), aligned(i, columns_at)
-            total = dot(dgate[rows], wg[columns], NT) + dot(dup[rows], wu[columns], NT)
-            part[b, :, columns] = total.astype(BF16)
-            return carry
-
-        lax.fori_loop(0, 4, one, 0)
 
     def root(i, rows, total):
         local = pl.ds(pl.multiple_of(place.late * QROWS + i * line.rows, line.rows), line.rows)
@@ -918,26 +1039,6 @@
 
     line_count = 4
     line = LineSum(place, part, inbox, result, sems[:line_count], cfg.pieces, root)
-    back_through(place.early)
-    line.early_start()
-    back_through(place.late)
-    gain_sum[...] = jnp.zeros_like(gain_sum)
-    for copy in loads[3:]:
-        copy.wait()
-    for copy in owns:
-        copy.wait()
-    for copy in swaps:
-        copy.wait_recv()
-
-    def arrived(i, carry):
-        for copy in exchange(i):
-            copy.wait_recv()
-        return carry
-
-    lax.fori_loop(0, cfg.chunks, arrived, 0)
-    down = wd.at[:, pl.ds(0, owners * block)]
-    gate_rows = wg.at[pl.ds(0, owners * block)]
-    up_rows = wu.at[pl.ds(0, owners * block)]
     scatter = Scatter(place, down, relay, down_out, 1, sems[line_count:])
     stores = []
 
@@ -946,70 +1047,54 @@
         copy.start()
         stores.append(copy)
 
-    def forward_terms(i):
-        columns = aligned(i, columns_at)
-        n2[:, columns] = dot(act[:tokens], wd[:, columns]).astype(BF16)
+    load_part.wait()
+    line.early_start()
 
     def grad_down(i):
         rows = aligned(i, units // 4)
         down[rows] = dot(act[:, rows], dy_all[...], TN).astype(BF16)
 
-    def grad_gate(i):
-        columns = aligned(i, units // 4)
-        gate_rows[:, columns] = dot(n2_all[...], dgate[:, columns], TN).astype(BF16)
-
-    def grad_up(i):
-        columns = aligned(i, units // 4)
-        up_rows[:, columns] = dot(n2_all[...], dup[:, columns], TN).astype(BF16)
-
-    for copy in swaps:
-        copy.wait_send()
-
-    def between(fill, first):
+    def grad_gate_up(i):
+        target = aligned(lax.rem(i, 2) * cfg.chunks + lax.div(i, 2), chunk)
+        gu_rows[:, target] = dot(n2_all[...], dgu[:, aligned(i, chunk)], TN).astype(BF16)
+
+    def between(fill, rounds, fills):
         def one(i, carry):
-            line.round(first + i)
-            fill(i)
+            line.round(rounds + i)
+            fill(fills + i)
             return carry
 
         lax.fori_loop(0, 4, one, 0)
 
-    between(forward_terms, 0)
-    keep(n2, terms_out)
-    between(grad_down, 4)
+    for copy in first + second:
+        copy.wait()
+    between(grad_down, 0, 0)
     scatter.start()
-    between(grad_gate, 8)
-    keep(gate_rows, gate_out)
-    between(grad_up, 12)
-    keep(up_rows, up_out)
-    line.run(16, line.rounds)
+    for copy in third:
+        copy.wait()
+    between(grad_gate_up, 4, 0)
+    between(grad_gate_up, 8, 4)
+    keep(gu_rows, gu_out)
+    for phase in range(place.bits - 1, 0, -1):
+        scatter.pass_on(phase)
+    line.run(12, line.rounds)
     keep(hidden, dh_out)
     keep(result, db_out)
     keep(gain_sum, gain_out)
-    for phase in range(place.bits - 1, 0, -1):
-        scatter.pass_on(phase)
     scatter.finish()
     line.drain()
-
-    def gone(i, carry):
-        for copy in exchange(i):
-            copy.wait_send()
-        return carry
-
-    lax.fori_loop(0, cfg.chunks, gone, 0)
     for copy in stores:
         copy.wait()
 
 
-def mlp_call(cfg, n2, wg, wu, wd, dy, hidden, gains):
+def mlp_call(cfg, *operands):
     tokens, width, units = cfg.tokens, cfg.width, cfg.hidden_units
     any_spec = pl.BlockSpec(memory_space=pl.ANY)
     shape = jax.ShapeDtypeStruct
     bits = cfg.dp.bit_length() - 1
     mine = cfg.dp * cfg.block
     outs = [
-        shape((tokens, width), BF16),
-        shape((mine, units), BF16),
-        shape((mine, units), BF16),
+        shape((mine, 2 * units), BF16),
         shape((1 + bits, units, cfg.block), BF16),
         shape((2, QROWS, width), BF16),
         shape((QROWS, width), F32),
@@ -1017,53 +1102,45 @@
     ]
     scratch = [
         pltpu.VMEM((tokens, width), BF16),
-        pltpu.VMEM((width, units), BF16),
-        pltpu.VMEM((width, units), BF16),
-        pltpu.VMEM((units, width), BF16),
-        pltpu.VMEM((tokens, width), BF16),
         pltpu.VMEM((QROWS, width), F32),
         pltpu.VMEM((16, width), BF16),
         pltpu.VMEM((2 * tokens, mine), BF16),
         pltpu.VMEM((2 * tokens, mine), BF16),
         pltpu.VMEM((2 * tokens, units), BF16),
-        pltpu.VMEM((2 * tokens, units), BF16),
-        pltpu.VMEM((2 * tokens, units), BF16),
+        pltpu.VMEM((2 * tokens, 2 * units), BF16),
+        pltpu.VMEM((mine, 2 * units), BF16),
+        pltpu.VMEM((units, mine), BF16),
         pltpu.VMEM((2, QROWS, width), BF16),
         pltpu.VMEM((2, QROWS, width), BF16),
         pltpu.VMEM((2, QROWS, width), BF16),
         pltpu.VMEM(Scatter.inbox_shape(cfg.dp, units, cfg.block), BF16),
         pltpu.VMEM((8, width), F32),
-        pltpu.SemaphoreType.DMA((5 + 3 * cfg.chunks,)),
-        pltpu.SemaphoreType.DMA((6,)),
-        pltpu.SemaphoreType.DMA((2, cfg.dp)),
-        pltpu.SemaphoreType.DMA((2, cfg.dp)),
-        pltpu.SemaphoreType.DMA((2, cfg.dp)),
-        pltpu.SemaphoreType.DMA((3, cfg.chunks)),
-        pltpu.SemaphoreType.DMA((3, cfg.chunks)),
+        pltpu.SemaphoreType.DMA((8,)),
+        pltpu.SemaphoreType.DMA((4,)),
     ]
     scratch += LineSum.semaphores(cfg.pieces)
     scratch += Scatter.semaphores(cfg.dp)
     return pl.pallas_call(
         functools.partial(mlp_kernel, cfg),
         out_shape=outs,
-        in_specs=[any_spec] * 7,
+        in_specs=[any_spec] * 8,
         out_specs=[any_spec] * len(outs),
         scratch_shapes=scratch,
         compiler_params=pltpu.CompilerParams(
             collective_id=2, has_side_effects=True, vmem_limit_bytes=VMEM_LIMIT
         ),
         name="feed_forward",
-    )(n2, wg, wu, wd, dy, hidden, gains)
+    )(*operands)
 
 
 def backward_kernel(cfg, *refs):
     (
         db_in, mixed_in, wo_in, qkv_in, q_in, k_in, v_in, normed_in, x_in, dh_in,
-        terms_in, hidden_in, gate_in, up_in, gain_in, gains_in, lengths, freq,
-        activations_out, grad_out, gate_out, up_out, qkv_out, out_out, gain_out,
+        terms_in, hidden_in, gu_in, gain_in, gains_in, lengths, freq,
+        activations_out, grad_out, gu_out, qkv_out, out_out, gain_out,
         db, wo, wqkv, qh, kh, vh, normed_all, mixed_all, db_all, dqkv, x, dh,
         terms, inbox_two, final, hidden, part, inbox_one, result,
-        gate_rows, up_rows, relay_gate, relay_up, relay_qkv, relay_out,
+        gu_rows, relay_gu, relay_qkv, relay_out,
         qkv_rows, out_columns, dmixed, dk, dv, dkv, dkv_in, cosine, sine, bias,
         gains, gain_two, gain_one, gain_rows, gain_box, gain_line,
         load, store, own_sem, swap_send, swap_receive, dkv_send, dkv_receive,
@@ -1088,10 +1165,9 @@
         fetch(q_in, qh),
         fetch(k_in, kh),
         fetch(v_in, vh),
-        fetch(terms_in.at[pl.ds(0, QROWS)], terms.at[0]),
-        fetch(terms_in.at[pl.ds(QROWS, QROWS)], terms.at[1]),
+        fetch(terms_in, terms),
     ]
-    wide = [fetch(gate_in, gate_rows), fetch(up_in, up_rows)]
+    wide = [fetch(gu_in, gu_rows)]
     rest = [
         fetch(hidden_in, hidden),
         fetch(qkv_in, wqkv),
@@ -1146,14 +1222,13 @@
     for i, (rows, relay, out, axis) in enumerate(
         [
             (out_columns, relay_out, out_out, 1),
-            (gate_rows, relay_gate, gate_out, 0),
-            (up_rows, relay_up, up_out, 0),
+            (gu_rows, relay_gu, gu_out, 0),
             (qkv_rows, relay_qkv, qkv_out, 0),
         ]
     ):
         at = 2 * n_line + n_scatter * i
         scatters.append(Scatter(place, rows, relay, out, axis, sems[at : at + n_scatter]))
-    s_out, s_gate, s_up, s_qkv = scatters
+    s_out, s_gu, s_qkv = scatters
 
     def local_rows(line, i):
         return pl.ds(pl.multiple_of(place.late * QROWS + i * line.rows, line.rows), line.rows)
@@ -1179,8 +1254,7 @@
     line_two.early_start()
     for copy in wide:
         copy.wait()
-    s_gate.start()
-    s_up.start()
+    s_gu.start()
 
     def back_out(b, carry):
         product = dot(db[b], wo[...], NT)
@@ -1216,15 +1290,13 @@
             z = jnp.concatenate(outs, 0).T * HD**-0.5
             z = z * cosine[rows] - turned(z) * sine[rows]
             dqkv[rows, aligned(j, 128)] = z.astype(BF16)
-            for k in range(2):
-                line_two.round(rounds + 2 * j + k)
+            line_two.round(rounds + j)
             return carry
 
         lax.fori_loop(0, heads // 2, pair, 0)
 
     attend_back(place.early, 0)
-    attend_back(place.late, heads)
-    line_two.run(min(2 * heads, line_two.rounds), line_two.rounds)
+    attend_back(place.late, heads // 2)
     stores = []
 
     def keep(source, target):
@@ -1232,7 +1304,6 @@
         copy.start()
         stores.append(copy)
 
-    keep(final, activations_out)
     pass_back = remote(dkv, dkv_in, dkv_send.at[0], dkv_receive.at[0], place.core)
 
     def packed(rows):
@@ -1279,33 +1350,41 @@
 
         lax.fori_loop(0, 4, one, 0)
 
+    def run_lines(start, stop):
+        def one(n, carry):
+            line_two.round(heads + n)
+            line_one.round(n)
+            return carry
+
+        lax.fori_loop(start, stop, one, 0)
+
     gain_one[...] = jnp.zeros_like(gain_one)
     back_through(place.early)
     line_one.early_start()
     back_through(place.late)
-    line_one.run(0, 1)
+    run_lines(0, 1)
     for copy in owns:
         copy.wait()
     for copy in swaps:
         copy.wait_recv()
     qkv_rows[...] = dot(normed_all[...], dqkv[...], TN).astype(BF16)
     s_qkv.start()
-    line_one.run(1, 3)
+    run_lines(1, 3)
     out_columns[...] = dot(mixed_all[...], db_all[...], TN).astype(BF16)
     s_out.start()
-    line_one.run(3, 4)
+    run_lines(3, 4)
     agenda = []
     for phase in range(place.bits - 1, 0, -1):
-        for s in (s_gate, s_up, s_qkv, s_out):
+        for s in (s_gu, s_qkv, s_out):
             agenda.append(functools.partial(s.pass_on, phase))
     last_sum = cfg.pieces + line_one.lags[1]
     marks = [4 + (last_sum - 4) * (k + 1) // (len(agenda) + 1) for k in range(len(agenda))]
     at = 4
     for mark, item in zip(marks, agenda):
-        line_one.run(at, mark)
+        run_lines(at, mark)
         item()
         at = mark
-    line_one.run(at, last_sum)
+    run_lines(at, last_sum)
 
     ends = (0, cfg.tensor - 1)
     mine = place.p * 2 + place.c
@@ -1334,7 +1413,7 @@
                     gain_copy(mask, core).start()
         gain_box[mine] = gain_rows[:, aligned(mine, block)]
 
-    line_one.run(last_sum, line_one.rounds - 2)
+    run_lines(last_sum, line_one.rounds - 2)
 
     def line_copy(step, end):
         return remote(
@@ -1358,8 +1437,10 @@
             for step in range(1, cfg.tensor):
                 line_copy(step, end).start()
 
-    line_one.run(line_one.rounds - 2, line_one.rounds)
+    run_lines(line_one.rounds - 2, line_one.rounds)
     keep(result, grad_out)
+    line_two.run(heads + line_one.rounds, line_two.rounds)
+    keep(final, activations_out)
     for end, at_t in enumerate(ends):
 
         @pl.when(place.t != at_t)
@@ -1399,8 +1480,7 @@
     outs = [
         shape((2, QROWS, width), BF16),
         shape((2, QROWS, width), BF16),
-        shape((1 + bits, cfg.block, units), BF16),
-        shape((1 + bits, cfg.block, units), BF16),
+        shape((1 + bits, cfg.block, 2 * units), BF16),
         shape((1 + bits, cfg.block, qkv_width), BF16),
         shape((1 + bits, cfg.query_width, cfg.block), BF16),
         shape((8, cfg.block), F32),
@@ -1426,10 +1506,8 @@
         pltpu.VMEM(halves, BF16),
         pltpu.VMEM(halves, BF16),
         pltpu.VMEM(halves, BF16),
-        pltpu.VMEM((mine, units), BF16),
-        pltpu.VMEM((mine, units), BF16),
-        pltpu.VMEM(Scatter.inbox_shape(cfg.dp, cfg.block, units), BF16),
-        pltpu.VMEM(Scatter.inbox_shape(cfg.dp, cfg.block, units), BF16),
+        pltpu.VMEM((mine, 2 * units), BF16),
+        pltpu.VMEM(Scatter.inbox_shape(cfg.dp, cfg.block, 2 * units), BF16),
         pltpu.VMEM(Scatter.inbox_shape(cfg.dp, cfg.block, qkv_width), BF16),
         pltpu.VMEM(Scatter.inbox_shape(cfg.dp, cfg.query_width, cfg.block), BF16),
         pltpu.VMEM((mine, qkv_width), BF16),
@@ -1461,8 +1539,8 @@
         pltpu.SemaphoreType.DMA((2,)),
     ]
     scratch += LineSum.semaphores(cfg.pieces) * 2
-    scratch += Scatter.semaphores(cfg.dp) * 4
-    in_specs = [any_spec] * 16 + [
+    scratch += Scatter.semaphores(cfg.dp) * 3
+    in_specs = [any_spec] * 15 + [
         pl.BlockSpec(memory_space=pltpu.SMEM),
         pl.BlockSpec(memory_space=pltpu.VMEM),
     ]
@@ -1499,24 +1577,25 @@
         freq = jnp.tile(frequencies(), (8, 4))
         gains = jnp.zeros((16, gain_attn.shape[0]), F32).at[0].set(gain_attn).at[1].set(gain_mlp)
         (
-            wqkv, wo, wg, wu, wd, gains_full, normed, q, k, v, mixed, hidden, normed_mlp,
+            _, _, wqkv, wo, gains_full, normed, q, k, v, mixed, hidden,
+            n2_all, dy_all, act_all, dgu_all, dn2, terms,
         ) = forward_call(
-            cfg, inputs, doc_lengths, freq, gains, w_query, w_key, w_value, w_out, w_gate, w_up, w_down
+            cfg, inputs, cotangent, doc_lengths, freq, gains,
+            w_query, w_key, w_value, w_out, w_gate, w_up, w_down,
         )
-        terms, gate_rows, up_rows, down_terms, db, dh, gain_two = mlp_call(
-            cfg, normed_mlp, wg, wu, wd, cotangent, hidden, gains_full
+        gu_rows, down_terms, db, dh, gain_two = mlp_call(
+            cfg, dn2, n2_all, dy_all, act_all, dgu_all, cotangent, hidden, gains_full
         )
-        activations, input_grad, gate_terms, up_terms, qkv_terms, out_terms, gain_sums = (
-            backward_call(
-                cfg, db, mixed, wo, wqkv, q, k, v, normed, inputs, dh, terms, hidden,
-                gate_rows, up_rows, gain_two, gains_full, doc_lengths, freq,
-            )
+        activations, input_grad, gu_terms, qkv_terms, out_terms, gain_sums = backward_call(
+            cfg, db, mixed, wo, wqkv, q, k, v, normed, inputs, dh, terms, hidden,
+            gu_rows, gain_two, gains_full, doc_lengths, freq,
         )
 
         def total(pieces):
             return jnp.sum(pieces.astype(F32), 0)
 
         qkv_grad = total(qkv_terms)
+        units = cfg.hidden_units
         query_width, key_width = cfg.query_width, cfg.key_width
         return (
             activations.reshape(tokens, width),
@@ -1527,8 +1606,8 @@
             qkv_grad[:, query_width + key_width :],
             total(out_terms),
             gain_sums[1],
-            total(gate_terms),
-            total(up_terms),
+            total(gu_terms[:, :, :units]),
+            total(gu_terms[:, :, units:]),
             total(down_terms),
         )
 

time: 445 us -> 399 us (0.90)
  Pallas kernels: 417 us -> 376 us
    pallas_call x1, Pallas kernels: 104 us -> 76.8 us  [mlp_call(): pl.pallas_call(functools.partial(mlp_kernel, cfg), out_shape=outs, in_spe...]
    pallas_call x1, Pallas kernels: 172 us -> 161 us  [forward_call(): pl.pallas_call(functools.partial(forward_kernel, cfg), out_shape=outs, in...]
where the time goes in v3:
time: 399 us; the launch traced here: 394 us
  Pallas kernels  376 us (94%)
  other arithmetic  9.92 us (2%)
  local copies, waits for them, and re-layouts  7.31 us (2%)
    pallas_call x1, Pallas kernels, forward_call(): pl.pallas_call(functools.partial(forward_kernel, cfg), out_shape=outs, in...  161 us
    pallas_call x1, Pallas kernels, backward_call(): pl.pallas_call(functools.partial(backward_kernel, cfg), out_shape=outs, i...  138 us
    pallas_call x1, Pallas kernels, mlp_call(): pl.pallas_call(functools.partial(mlp_kernel, cfg), out_shape=outs, in_spe...  76.8 us

profile of v3, /device:TPU:0, one launch (start us, length us, event | category | flops | bytes accessed | tf_op | source)
XLA Modules:
  0.0 394.1 jit_solution(2135298512959488520)
XLA Ops:
  0.7 0.1 tile.17
  0.8 0.6 tile.18.refs_3_.refs_16_
  1.4 0.7 scatter.6
  2.0 0.7 scatter.9.refs_4_
  2.7 0.0 copy-start.4
  2.7 0.6 copy-done.4
  3.3 161.0 %attention_forward.1 = (bf16[2048,4096]{1,0:T(8,128)(2,1)}, bf16[2048,2048]{1,0:T(8,128)(2,1)}, bf16[2048,768]{1,0:T(8,128)(2,1)}, bf16[512,2048]{1,0:T(8,128)(2...) custom-call(bf16[512,2048]{1,0:T(8,128)(2,1)} %refs_8_.3, ...), custom_call_target="tpu_custom_call" | custom-call | tf_op jit(solution)/shard_map/attention_forward/pallas_call | solution.py:981
  164.4 76.8 %feed_forward.1 = (bf16[1024,4096]{1,0:T(8,128)(2,1)}, bf16[3,2048,256]{2,1,0:T(8,128)(2,1)}, bf16[2,256,2048]{2,1,0:T(8,128)(2,1)}, f32[256,2048]{1,0:T(8,128)}, f32[8,2048]{1,0:T(8,128)}) custom-call(bf16[2,256,2048]{2,1,0:T(8,128)(2,1)} %get-tuple-element.61.refs_0_, bf16[1024,1024]{1,0:T(8,128)(2,1)} %get-tuple-element.62.refs_1_, ...), custom_call_target="tpu_custom_call" | custom-call | tf_op jit(solution)/shard_map/feed_forward/pallas_call | solution.py:1123
  241.2 138.1 %attention_backward.1 = (bf16[2,256,2048]{2,1,0:T(8,128)(2,1)}, bf16[2,256,2048]{2,1,0:T(8,128)(2,1)}, bf16[3,256,4096]{2,1,0:T(8,128)(2,1)}, bf16[3,256,768]{2,...) custom-call(bf16[2,256,2048]{2,1,0:T(8,128)(2,1)} %get-tuple-element.68.refs_0_, ...), custom_call_target="tpu_custom_call" | custom-call | tf_op jit(solution)/shard_map/attention_backward/pallas_call | solution.py:1547
  379.3 0.0 copy-start.3
  379.3 1.4 fusion.1
  380.7 2.1 convert_reduce_fusion.4
  382.8 0.0 copy-done.3
  382.8 0.0 copy-start
  382.8 0.2 convert_reduce_fusion.3
  383.0 0.0 copy-start.1
  383.0 0.7 fusion
  383.7 0.0 slice-start
  383.7 0.9 slice.57
  384.5 0.3 copy-done
  384.9 0.0 slice-start.1
  384.9 1.7 convert_reduce_fusion
  386.6 0.0 copy-done.1
  386.6 2.7 bitcast_convert_fusion
  389.3 0.0 slice-done
  389.3 0.0 slice-done.1
  389.3 0.0 copy-start.2
  389.3 3.2 convert_reduce_fusion.1
  392.5 0.0 copy-done.2
  392.5 1.3 copy.25
  (3 shorter events, 0.0 us)
Async XLA Ops:
  2.7 0.6 copy-start.4
  379.3 3.5 copy-start.3
  382.8 2.1 copy-start
  383.0 3.7 copy-start.1
  383.7 5.6 %slice-start = ((s8[6291456]{0:T(1024)(128)(4,1)}), s8[4194304]{0:T(1024)(128)(4,1)S(1)}, s32[]{:S(2)}) async-start(s8[6291456]{0:T(1024)(128)(4,1)} %bitcast.8), calls=%async_computation | async-start | bytes 8388608
  384.9 4.4 %slice-start.1 = ((s8[6291456]{0:T(1024)(128)(4,1)}), s8[2097152]{0:T(1024)(128)(4,1)S(1)}, s32[]{:S(2)}) async-start(s8[6291456]{0:T(1024)(128)(4,1)} %bitcast.8), calls=%async_computation.1 | async-start | bytes 4194304
  389.3 3.2 copy-start.2

commit v4 on v3

--- a/solution.py
+++ b/solution.py
@@ -19,7 +19,7 @@
 NN = (((1,), (0,)), ((), ()))
 NT = (((1,), (1,)), ((), ()))
 TN = (((0,), (0,)), ((), ()))
-VMEM_LIMIT = 62 * 2**20
+VMEM_LIMIT = 127 * 2**19
 
 
 def dot(left, right, dims=NN):
@@ -899,6 +899,7 @@
         self.heads, self.groups, self.hidden_units = heads, groups, hidden_units
         self.pieces = 8
         self.chunks = 4
+        self.behind = 12
         self.marks = (4, 4, 11)
         self.query_width, self.key_width = heads * HD, groups * HD
         self.qkv_width = self.query_width + 2 * self.key_width
@@ -997,18 +998,44 @@
     )(x, dy, lengths, freq, gains, wq, wk, wv, wo, wg, wu, wd)
 
 
-def mlp_kernel(cfg, *refs):
+def backward_kernel(cfg, *refs):
     (
-        dn2_in, n2_in, dy_all_in, act_in, dgu_in, dy_in, hidden_in, gains_in,
-        gu_out, down_out, db_out, dh_out, gain_out,
-        dy, hidden, gains, n2_all, dy_all, act, dgu, gu_rows, down,
-        part, inbox, result, relay, gain_sum,
-        load, store, *sems,
+        dn2_in, n2_in, dy_all_in, act_in, dgu_in, dy_in, hidden_in, terms_in,
+        mixed_in, wo_in, qkv_in, q_in, k_in, v_in, normed_in, x_in, gains_in, lengths, freq,
+        activations_out, grad_out, down_out, gu_out, qkv_out, out_out, gain_out,
+        dy, hidden, dh, gains, n2_all, dy_all, act, dgu, gu_rows, down,
+        part, inbox, result, terms, inbox_two, final,
+        relay_down, relay_gu, relay_qkv, relay_out, qh, kh, vh,
+        dmixed, dk, dv, dkv, dkv_in, cosine, sine, bias,
+        gain_two, gain_one, gain_rows, gain_box, gain_line,
+        load, store, own_sem, swap_send, swap_receive, dkv_send, dkv_receive,
+        gain_send, gain_receive, last_send, last_receive, ready, *sems,
     ) = refs
     place = Place(cfg.dp, cfg.tensor)
     tokens, width = dy.shape
+    heads, groups = cfg.heads, cfg.groups
+    query_width, key_width, qkv_width = cfg.query_width, cfg.key_width, cfg.qkv_width
     units = act.shape[1]
     chunk = units // cfg.chunks
+    block, owners = cfg.block, cfg.dp
+    mine = owners * block
+    spare = list(sems[3 * 4 + 4 * 3 :])
+    at = 0
+
+    def carve(array, rows, columns, first_row=0, first_column=0):
+        if array.shape[0] >= first_row + rows and array.shape[1] >= first_column + columns:
+            return array.at[pl.ds(first_row, rows), pl.ds(first_column, columns)]
+        return spare.pop(0)
+
+    views = []
+    for columns in (mine, mine, qkv_width, qkv_width, query_width):
+        views.append(carve(dgu, 2 * tokens, columns, 0, at))
+        at += columns
+    normed_all, db_all, dqkv, qkv_rows, mixed_all = views
+    x = carve(act, tokens, width)
+    wo = carve(act, query_width, width, tokens)
+    wqkv = carve(down, width, qkv_width)
+    out_columns = carve(n2_all, query_width, mine)
     loads = []
 
     def fetch(source, target):
@@ -1018,165 +1045,15 @@
         return copy
 
     load_part = fetch(dn2_in, part)
-    first = [fetch(dy_in, dy), fetch(hidden_in, hidden), fetch(gains_in, gains)]
-    second = [fetch(act_in, act), fetch(dy_all_in, dy_all)]
-    third = [fetch(n2_in, n2_all), fetch(dgu_in, dgu)]
-    place.greet()
-    gain_sum[...] = jnp.zeros_like(gain_sum)
-    place.meet()
-
-    def root(i, rows, total):
-        local = pl.ds(pl.multiple_of(place.late * QROWS + i * line.rows, line.rows), line.rows)
-        source = hidden[rows]
-        r = lax.rsqrt(jnp.sum(source * source, -1, keepdims=True) * (1.0 / width) + EPSILON)
-        scaled = source * r
-        gain_sum[...] += jnp.sum((total * scaled).reshape(line.rows // 8, 8, width), 0)
-        e = total * gains[1:2, :].astype(F32)
-        mean = jnp.sum(e * scaled, -1, keepdims=True) * (1.0 / width)
-        dh = dy[local].astype(F32) + r * (e - scaled * mean)
-        hidden[rows] = dh
-        result[place.late, rows] = dh.astype(BF16)
-
-    line_count = 4
-    line = LineSum(place, part, inbox, result, sems[:line_count], cfg.pieces, root)
-    scatter = Scatter(place, down, relay, down_out, 1, sems[line_count:])
-    stores = []
-
-    def keep(source, target):
-        copy = pltpu.make_async_copy(source, target, store.at[len(stores)])
-        copy.start()
-        stores.append(copy)
-
-    load_part.wait()
-    line.early_start()
-
-    def grad_down(i):
-        rows = aligned(i, units // 4)
-        down[rows] = dot(act[:, rows], dy_all[...], TN).astype(BF16)
-
-    def grad_gate_up(i):
-        target = aligned(lax.rem(i, 2) * cfg.chunks + lax.div(i, 2), chunk)
-        gu_rows[:, target] = dot(n2_all[...], dgu[:, aligned(i, chunk)], TN).astype(BF16)
-
-    def between(fill, rounds, fills):
-        def one(i, carry):
-            line.round(rounds + i)
-            fill(fills + i)
-            return carry
-
-        lax.fori_loop(0, 4, one, 0)
-
-    for copy in first + second:
-        copy.wait()
-    between(grad_down, 0, 0)
-    scatter.start()
-    for copy in third:
-        copy.wait()
-    between(grad_gate_up, 4, 0)
-    between(grad_gate_up, 8, 4)
-    keep(gu_rows, gu_out)
-    for phase in range(place.bits - 1, 0, -1):
-        scatter.pass_on(phase)
-    line.run(12, line.rounds)
-    keep(hidden, dh_out)
-    keep(result, db_out)
-    keep(gain_sum, gain_out)
-    scatter.finish()
-    line.drain()
-    for copy in stores:
-        copy.wait()
-
-
-def mlp_call(cfg, *operands):
-    tokens, width, units = cfg.tokens, cfg.width, cfg.hidden_units
-    any_spec = pl.BlockSpec(memory_space=pl.ANY)
-    shape = jax.ShapeDtypeStruct
-    bits = cfg.dp.bit_length() - 1
-    mine = cfg.dp * cfg.block
-    outs = [
-        shape((mine, 2 * units), BF16),
-        shape((1 + bits, units, cfg.block), BF16),
-        shape((2, QROWS, width), BF16),
-        shape((QROWS, width), F32),
-        shape((8, width), F32),
+    first = [
+        fetch(dy_in, dy),
+        fetch(hidden_in, hidden),
+        fetch(gains_in, gains),
+        fetch(act_in, act),
+        fetch(dy_all_in, dy_all),
     ]
-    scratch = [
-        pltpu.VMEM((tokens, width), BF16),
-        pltpu.VMEM((QROWS, width), F32),
-        pltpu.VMEM((16, width), BF16),
-        pltpu.VMEM((2 * tokens, mine), BF16),
-        pltpu.VMEM((2 * tokens, mine), BF16),
-        pltpu.VMEM((2 * tokens, units), BF16),
-        pltpu.VMEM((2 * tokens, 2 * units), BF16),
-        pltpu.VMEM((mine, 2 * units), BF16),
-        pltpu.VMEM((units, mine), BF16),
-        pltpu.VMEM((2, QROWS, width), BF16),
-        pltpu.VMEM((2, QROWS, width), BF16),
-        pltpu.VMEM((2, QROWS, width), BF16),
-        pltpu.VMEM(Scatter.inbox_shape(cfg.dp, units, cfg.block), BF16),
-        pltpu.VMEM((8, width), F32),
-        pltpu.SemaphoreType.DMA((8,)),
-        pltpu.SemaphoreType.DMA((4,)),
-    ]
-    scratch += LineSum.semaphores(cfg.pieces)
-    scratch += Scatter.semaphores(cfg.dp)
-    return pl.pallas_call(
-        functools.partial(mlp_kernel, cfg),
-        out_shape=outs,
-        in_specs=[any_spec] * 8,
-        out_specs=[any_spec] * len(outs),
-        scratch_shapes=scratch,
-        compiler_params=pltpu.CompilerParams(
-            collective_id=2, has_side_effects=True, vmem_limit_bytes=VMEM_LIMIT
-        ),
-        name="feed_forward",
-    )(*operands)
-
-
-def backward_kernel(cfg, *refs):
-    (
-        db_in, mixed_in, wo_in, qkv_in, q_in, k_in, v_in, normed_in, x_in, dh_in,
-        terms_in, hidden_in, gu_in, gain_in, gains_in, lengths, freq,
-        activations_out, grad_out, gu_out, qkv_out, out_out, gain_out,
-        db, wo, wqkv, qh, kh, vh, normed_all, mixed_all, db_all, dqkv, x, dh,
-        terms, inbox_two, final, hidden, part, inbox_one, result,
-        gu_rows, relay_gu, relay_qkv, relay_out,
-        qkv_rows, out_columns, dmixed, dk, dv, dkv, dkv_in, cosine, sine, bias,
-        gains, gain_two, gain_one, gain_rows, gain_box, gain_line,
-        load, store, own_sem, swap_send, swap_receive, dkv_send, dkv_receive,
-        gain_send, gain_receive, last_send, last_receive, *sems,
-    ) = refs
-    place = Place(cfg.dp, cfg.tensor)
-    tokens, width = x.shape
-    heads, groups = cfg.heads, cfg.groups
-    query_width, key_width = cfg.query_width, cfg.key_width
-    block, owners = cfg.block, cfg.dp
-    loads = []
-
-    def fetch(source, target):
-        copy = pltpu.make_async_copy(source, target, load.at[len(loads)])
-        copy.start()
-        loads.append(copy)
-        return copy
-
-    first = [
-        fetch(db_in, db),
-        fetch(wo_in, wo),
-        fetch(q_in, qh),
-        fetch(k_in, kh),
-        fetch(v_in, vh),
-        fetch(terms_in, terms),
-    ]
-    wide = [fetch(gu_in, gu_rows)]
-    rest = [
-        fetch(hidden_in, hidden),
-        fetch(qkv_in, wqkv),
-        fetch(mixed_in, mixed_all.at[pl.ds(0, tokens)]),
-        fetch(x_in, x),
-        fetch(dh_in, dh),
-        fetch(gains_in, gains),
-        fetch(gain_in, gain_two),
-    ]
+    second = [fetch(n2_in, n2_all), fetch(dgu_in, dgu)]
+    third = [fetch(terms_in, terms), fetch(q_in, qh), fetch(k_in, kh), fetch(v_in, vh)]
     barrier = pltpu.get_barrier_semaphore()
     greeted = [place.core]
     for mask in range(1, cfg.dp):
@@ -1185,76 +1062,133 @@
         greeted.append((place.p, place.c, lax.rem(place.t + step, cfg.tensor)))
     for device in greeted:
         pl.semaphore_signal(barrier, inc=1, device_id=device, device_id_type=MESH)
-    tables(place, lengths, freq, cosine, sine, tokens)
-    fill_bias(place, lengths, bias, tokens)
+    gain_two[...] = jnp.zeros_like(gain_two)
+    gain_one[...] = jnp.zeros_like(gain_one)
     pl.semaphore_wait(barrier, len(greeted))
-
-    for copy in first[:2]:
-        copy.wait()
-    swaps, owns = [], []
-
-    def swap(source, target, k, q):
-        copy = remote(source, target, swap_send.at[k, q], swap_receive.at[k, q], place.core)
-        copy.start()
-        swaps.append(copy)
-
-    for q in range(owners):
-        columns = pl.ds(q * block, block)
-        other, own = aligned(2 * q + 1 - place.c, block), aligned(2 * q + place.c, block)
-        swap(normed_in.at[:, other], normed_all.at[pl.ds(tokens, tokens), columns], 0, q)
-        copy = pltpu.make_async_copy(
-            normed_in.at[:, own], normed_all.at[pl.ds(0, tokens), columns], own_sem.at[0, q]
-        )
-        copy.start()
-        owns.append(copy)
-        for b in range(2):
-            target = pl.ds(tokens + b * QROWS, QROWS)
-            swap(db.at[b, :, other], db_all.at[target, columns], 1 + b, q)
-            copy = pltpu.make_async_copy(
-                db.at[b, :, own], db_all.at[pl.ds(b * QROWS, QROWS), columns], own_sem.at[1 + b, q]
-            )
-            copy.start()
-            owns.append(copy)
-    swap(mixed_in, mixed_all.at[pl.ds(tokens, tokens)], 3, 0)
-
     n_line, n_scatter = 4, 3
     scatters = []
     for i, (rows, relay, out, axis) in enumerate(
         [
+            (down, relay_down, down_out, 1),
+            (gu_rows, relay_gu, gu_out, 0),
             (out_columns, relay_out, out_out, 1),
-            (gu_rows, relay_gu, gu_out, 0),
             (qkv_rows, relay_qkv, qkv_out, 0),
         ]
     ):
-        at = 2 * n_line + n_scatter * i
+        at = 3 * n_line + n_scatter * i
         scatters.append(Scatter(place, rows, relay, out, axis, sems[at : at + n_scatter]))
-    s_out, s_gu, s_qkv = scatters
-
-    def local_rows(line, i):
-        return pl.ds(pl.multiple_of(place.late * QROWS + i * line.rows, line.rows), line.rows)
+    s_down, s_gu, s_out, s_qkv = scatters
+
+    def local_rows(i):
+        rows = QROWS // cfg.pieces
+        return pl.ds(pl.multiple_of(place.late * QROWS + i * rows, rows), rows)
+
+    def norm_back(source, total, gain, gain_sum):
+        r = lax.rsqrt(jnp.sum(source * source, -1, keepdims=True) * (1.0 / width) + EPSILON)
+        scaled = source * r
+        gain_sum[...] += jnp.sum((total * scaled).reshape(-1, 8, width), 0)
+        e = total * gain
+        mean = jnp.sum(e * scaled, -1, keepdims=True) * (1.0 / width)
+        return r * (e - scaled * mean)
+
+    def root_three(i, rows, total):
+        back = norm_back(hidden[rows], total, gains[1:2, :].astype(F32), gain_two)
+        grad = dy[local_rows(i)].astype(F32) + back
+        dh[rows] = grad
+        result[place.late, rows] = grad.astype(BF16)
 
     def root_two(i, rows, total):
         final[place.late, rows] = (hidden[rows] + total).astype(BF16)
 
     def root_one(i, rows, total):
-        source = x[local_rows(line_one, i)].astype(F32)
-        r = lax.rsqrt(jnp.sum(source * source, -1, keepdims=True) * (1.0 / width) + EPSILON)
-        scaled = source * r
-        gain_one[...] += jnp.sum((total * scaled).reshape(line_one.rows // 8, 8, width), 0)
-        e = total * gains[0:1, :].astype(F32)
-        mean = jnp.sum(e * scaled, -1, keepdims=True) * (1.0 / width)
-        result[place.late, rows] = (dh[rows] + r * (e - scaled * mean)).astype(BF16)
-
-    line_two = LineSum(place, terms, inbox_two, final, sems[:n_line], cfg.pieces, root_two)
+        source = x[local_rows(i)].astype(F32)
+        back = norm_back(source, total, gains[0:1, :].astype(F32), gain_one)
+        result[place.late, rows] = (dh[rows] + back).astype(BF16)
+
+    line_three = LineSum(place, part, inbox, result, sems[:n_line], cfg.pieces, root_three)
+    line_two = LineSum(
+        place, terms, inbox_two, final, sems[n_line : 2 * n_line], cfg.pieces, root_two
+    )
     line_one = LineSum(
-        place, part, inbox_one, result, sems[n_line : 2 * n_line], cfg.pieces, root_one
+        place, part, inbox, result, sems[2 * n_line : 3 * n_line], cfg.pieces, root_one
     )
-    for copy in first[2:]:
+    load_part.wait()
+    line_three.early_start()
+
+    def grad_down(i):
+        rows = aligned(i, units // 4)
+        down[rows] = dot(act[:, rows], dy_all[...], TN).astype(BF16)
+
+    def grad_gate_up(i):
+        target = aligned(lax.rem(i, 2) * cfg.chunks + lax.div(i, 2), chunk)
+        gu_rows[:, target] = dot(n2_all[...], dgu[:, aligned(i, chunk)], TN).astype(BF16)
+
+    def lines(n):
+        line_three.round(n)
+        line_two.round(n - cfg.behind)
+
+    def between(fill, rounds, fills):
+        def one(i, carry):
+            lines(rounds + i)
+            fill(fills + i)
+            return carry
+
+        lax.fori_loop(0, 4, one, 0)
+
+    for copy in first:
         copy.wait()
+    between(grad_down, 0, 0)
+    s_down.start()
+    tables(place, lengths, freq, cosine, sine, tokens)
+    fill_bias(place, lengths, bias, tokens)
+    for copy in second + third:
+        copy.wait()
+    between(grad_gate_up, 4, 0)
+    between(grad_gate_up, 8, 4)
     line_two.early_start()
-    for copy in wide:
+    pl.semaphore_signal(ready, inc=1, device_id=place.core, device_id_type=MESH)
+    rest = [
+        fetch(wo_in, wo),
+        fetch(x_in, x),
+        fetch(mixed_in, mixed_all.at[pl.ds(0, tokens)]),
+    ]
+    for phase in range(place.bits - 1, 0, -1):
+        s_down.pass_on(phase)
+    s_gu.start()
+    lines(12)
+    pl.semaphore_wait(ready, 1)
+    swaps, owns, db_swaps, db_owns = [], [], [], []
+
+    def swap(source, target, k, q, kept):
+        copy = remote(source, target, swap_send.at[k, q], swap_receive.at[k, q], place.core)
+        copy.start()
+        kept.append(copy)
+
+    def own(source, target, k, q, kept):
+        copy = pltpu.make_async_copy(source, target, own_sem.at[k, q])
+        copy.start()
+        kept.append(copy)
+
+    def shares(q):
+        return pl.ds(q * block, block), aligned(2 * q + 1 - place.c, block), aligned(2 * q + place.c, block)
+
+    for q in range(owners):
+        columns, theirs, ours = shares(q)
+        swap(normed_in.at[:, theirs], normed_all.at[pl.ds(tokens, tokens), columns], 0, q, swaps)
+        own(normed_in.at[:, ours], normed_all.at[pl.ds(0, tokens), columns], 0, q, owns)
+    swap(mixed_in, mixed_all.at[pl.ds(tokens, tokens)], 3, 0, swaps)
+    lines(13)
+    lines(14)
+    db = result
+    for b in range(2):
+        for q in range(owners):
+            columns, theirs, ours = shares(q)
+            target = pl.ds(tokens + b * QROWS, QROWS)
+            swap(db.at[b, :, theirs], db_all.at[target, columns], 1 + b, q, db_swaps)
+            target = pl.ds(b * QROWS, QROWS)
+            own(db.at[b, :, ours], db_all.at[target, columns], 1 + b, q, db_owns)
+    for copy in rest:
         copy.wait()
-    s_gu.start()
 
     def back_out(b, carry):
         product = dot(db[b], wo[...], NT)
@@ -1264,8 +1198,6 @@
         return carry
 
     lax.fori_loop(0, 2, back_out, 0)
-    for copy in rest:
-        copy.wait()
     dk[...] = jnp.zeros_like(dk)
     dv[...] = jnp.zeros_like(dv)
 
@@ -1295,8 +1227,19 @@
 
         lax.fori_loop(0, heads // 2, pair, 0)
 
-    attend_back(place.early, 0)
-    attend_back(place.late, heads // 2)
+    done = line_three.rounds - cfg.behind
+    attend_back(place.early, done)
+    for copy in db_owns + owns:
+        copy.wait()
+    for copy in db_swaps + swaps:
+        copy.wait_recv()
+        copy.wait_send()
+    s_down.finish()
+    load_qkv = fetch(qkv_in, wqkv)
+    out_columns[...] = dot(mixed_all[...], db_all[...], TN).astype(BF16)
+    s_out.start()
+    attend_back(place.late, done + heads // 2)
+    done = done + heads
     stores = []
 
     def keep(source, target):
@@ -1339,7 +1282,9 @@
     dkeys = dkeys * table_c - turned(dkeys) * table_s
     dqkv[:tokens, query_width : query_width + key_width] = dkeys.astype(BF16)
     dqkv[:tokens, query_width + key_width :] = dkv[:, key_width:].astype(BF16)
-    swap(dqkv.at[pl.ds(0, tokens)], dqkv.at[pl.ds(tokens, tokens)], 3, 1)
+    late_swaps = []
+    swap(dqkv.at[pl.ds(0, tokens)], dqkv.at[pl.ds(tokens, tokens)], 3, 1, late_swaps)
+    load_qkv.wait()
     columns_at = width // 4
 
     def back_through(b):
@@ -1352,30 +1297,25 @@
 
     def run_lines(start, stop):
         def one(n, carry):
-            line_two.round(heads + n)
             line_one.round(n)
+            line_two.round(done + n)
             return carry
 
         lax.fori_loop(start, stop, one, 0)
 
-    gain_one[...] = jnp.zeros_like(gain_one)
+    line_three.drain()
     back_through(place.early)
     line_one.early_start()
     back_through(place.late)
     run_lines(0, 1)
-    for copy in owns:
-        copy.wait()
-    for copy in swaps:
+    for copy in late_swaps:
         copy.wait_recv()
     qkv_rows[...] = dot(normed_all[...], dqkv[...], TN).astype(BF16)
     s_qkv.start()
-    run_lines(1, 3)
-    out_columns[...] = dot(mixed_all[...], db_all[...], TN).astype(BF16)
-    s_out.start()
-    run_lines(3, 4)
+    run_lines(1, 4)
     agenda = []
     for phase in range(place.bits - 1, 0, -1):
-        for s in (s_gu, s_qkv, s_out):
+        for s in (s_gu, s_out, s_qkv):
             agenda.append(functools.partial(s.pass_on, phase))
     last_sum = cfg.pieces + line_one.lags[1]
     marks = [4 + (last_sum - 4) * (k + 1) // (len(agenda) + 1) for k in range(len(agenda))]
@@ -1439,7 +1379,7 @@
 
     run_lines(line_one.rounds - 2, line_one.rounds)
     keep(result, grad_out)
-    line_two.run(heads + line_one.rounds, line_two.rounds)
+    line_two.run(done + line_one.rounds, line_two.rounds)
     keep(final, activations_out)
     for end, at_t in enumerate(ends):
 
@@ -1449,7 +1389,7 @@
 
     gain_one[:, :block] = gain_line[0] + gain_line[1]
     keep(gain_one.at[:, pl.ds(0, block)], gain_out)
-    for s in scatters:
+    for s in scatters[1:]:
         s.finish()
 
     @pl.when(place.at_end)
@@ -1462,7 +1402,7 @@
         for step in range(1, cfg.tensor):
             line_copy(step, 0).wait_send()
 
-    for copy in swaps:
+    for copy in late_swaps:
         copy.wait_send()
     line_two.drain()
     line_one.drain()
@@ -1480,6 +1420,7 @@
     outs = [
         shape((2, QROWS, width), BF16),
         shape((2, QROWS, width), BF16),
+        shape((1 + bits, units, cfg.block), BF16),
         shape((1 + bits, cfg.block, 2 * units), BF16),
         shape((1 + bits, cfg.block, qkv_width), BF16),
         shape((1 + bits, cfg.query_width, cfg.block), BF16),
@@ -1487,31 +1428,26 @@
     ]
     halves = (2, QROWS, width)
     scratch = [
-        pltpu.VMEM(halves, BF16),
-        pltpu.VMEM((cfg.query_width, width), BF16),
-        pltpu.VMEM((width, qkv_width), BF16),
+        pltpu.VMEM((tokens, width), BF16),
+        pltpu.VMEM((QROWS, width), F32),
+        pltpu.VMEM((QROWS, width), F32),
+        pltpu.VMEM((16, width), BF16),
+        pltpu.VMEM((2 * tokens, mine), BF16),
+        pltpu.VMEM((2 * tokens, mine), BF16),
+        pltpu.VMEM((2 * tokens, units), BF16),
+        pltpu.VMEM((2 * tokens, 2 * units), BF16),
+        pltpu.VMEM((mine, 2 * units), BF16),
+        pltpu.VMEM((units, mine), BF16),
+    ]
+    scratch += [pltpu.VMEM(halves, BF16)] * 6
+    scratch += [
+        pltpu.VMEM(Scatter.inbox_shape(cfg.dp, units, cfg.block), BF16),
+        pltpu.VMEM(Scatter.inbox_shape(cfg.dp, cfg.block, 2 * units), BF16),
+        pltpu.VMEM(Scatter.inbox_shape(cfg.dp, cfg.block, qkv_width), BF16),
+        pltpu.VMEM(Scatter.inbox_shape(cfg.dp, cfg.query_width, cfg.block), BF16),
         pltpu.VMEM((heads, tokens, HD), BF16),
         pltpu.VMEM((groups, 2 * tokens, HD), BF16),
         pltpu.VMEM((groups, 2 * tokens, HD), BF16),
-        pltpu.VMEM((2 * tokens, mine), BF16),
-        pltpu.VMEM((2 * tokens, cfg.query_width), BF16),
-        pltpu.VMEM((2 * tokens, mine), BF16),
-        pltpu.VMEM((2 * tokens, qkv_width), BF16),
-        pltpu.VMEM((tokens, width), BF16),
-        pltpu.VMEM((QROWS, width), F32),
-        pltpu.VMEM(halves, BF16),
-        pltpu.VMEM(halves, BF16),
-        pltpu.VMEM(halves, BF16),
-        pltpu.VMEM((QROWS, width), F32),
-        pltpu.VMEM(halves, BF16),
-        pltpu.VMEM(halves, BF16),
-        pltpu.VMEM(halves, BF16),
-        pltpu.VMEM((mine, 2 * units), BF16),
-        pltpu.VMEM(Scatter.inbox_shape(cfg.dp, cfg.block, 2 * units), BF16),
-        pltpu.VMEM(Scatter.inbox_shape(cfg.dp, cfg.block, qkv_width), BF16),
-        pltpu.VMEM(Scatter.inbox_shape(cfg.dp, cfg.query_width, cfg.block), BF16),
-        pltpu.VMEM((mine, qkv_width), BF16),
-        pltpu.VMEM((cfg.query_width, mine), BF16),
         pltpu.VMEM((heads, tokens, HD), BF16),
         pltpu.VMEM((groups, 2 * tokens, HD), F32),
         pltpu.VMEM((groups, 2 * tokens, HD), F32),
@@ -1520,7 +1456,6 @@
         pltpu.VMEM((tokens, 128), F32),
         pltpu.VMEM((tokens, 128), F32),
         pltpu.VMEM((2, cfg.window, QROWS), F32),
-        pltpu.VMEM((16, width), BF16),
         pltpu.VMEM((8, width), F32),
         pltpu.VMEM((8, width), F32),
         pltpu.VMEM((8, width), F32),
@@ -1537,10 +1472,24 @@
         pltpu.SemaphoreType.DMA((cfg.dp, 2)),
         pltpu.SemaphoreType.DMA((cfg.tensor,)),
         pltpu.SemaphoreType.DMA((2,)),
+        pltpu.SemaphoreType.REGULAR,
     ]
-    scratch += LineSum.semaphores(cfg.pieces) * 2
-    scratch += Scatter.semaphores(cfg.dp) * 3
-    in_specs = [any_spec] * 15 + [
+    scratch += LineSum.semaphores(cfg.pieces) * 3
+    scratch += Scatter.semaphores(cfg.dp) * 4
+    at = 0
+    for columns in (mine, mine, qkv_width, qkv_width, cfg.query_width):
+        if 2 * units < at + columns:
+            scratch.append(pltpu.VMEM((2 * tokens, columns), BF16))
+        at += columns
+    if units < width:
+        scratch.append(pltpu.VMEM((tokens, width), BF16))
+    if units < width or 2 * tokens < tokens + cfg.query_width:
+        scratch.append(pltpu.VMEM((cfg.query_width, width), BF16))
+    if units < width or mine < qkv_width:
+        scratch.append(pltpu.VMEM((width, qkv_width), BF16))
+    if 2 * tokens < cfg.query_width:
+        scratch.append(pltpu.VMEM((cfg.query_width, mine), BF16))
+    in_specs = [any_spec] * 17 + [
         pl.BlockSpec(memory_space=pltpu.SMEM),
         pl.BlockSpec(memory_space=pltpu.VMEM),
     ]
@@ -1553,7 +1502,7 @@
         compiler_params=pltpu.CompilerParams(
             collective_id=3, has_side_effects=True, vmem_limit_bytes=VMEM_LIMIT
         ),
-        name="attention_backward",
+        name="backward",
     )(*operands)
 
 
@@ -1583,12 +1532,11 @@
             cfg, inputs, cotangent, doc_lengths, freq, gains,
             w_query, w_key, w_value, w_out, w_gate, w_up, w_down,
         )
-        gu_rows, down_terms, db, dh, gain_two = mlp_call(
-            cfg, dn2, n2_all, dy_all, act_all, dgu_all, cotangent, hidden, gains_full
-        )
-        activations, input_grad, gu_terms, qkv_terms, out_terms, gain_sums = backward_call(
-            cfg, db, mixed, wo, wqkv, q, k, v, normed, inputs, dh, terms, hidden,
-            gu_rows, gain_two, gains_full, doc_lengths, freq,
+        (
+            activations, input_grad, down_terms, gu_terms, qkv_terms, out_terms, gain_sums,
+        ) = backward_call(
+            cfg, dn2, n2_all, dy_all, act_all, dgu_all, cotangent, hidden, terms,
+            mixed, wo, wqkv, q, k, v, normed, inputs, gains_full, doc_lengths, freq,
         )
 
         def total(pieces):

time: 399 us -> 380 us (0.952)
  Pallas kernels: 376 us -> 356 us
    pallas_call x1 -> x0, Pallas kernels: 76.8 us -> none  [mlp_call(): pl.pallas_call(functools.partial(mlp_kernel, cfg), out_shape=outs, in_spe...]
    pallas_call x1, Pallas kernels: 138 us -> 195 us  [backward_call(): pl.pallas_call(functools.partial(backward_kernel, cfg), out_shape=outs, i...]
where the time goes in v4:
time: 380 us; the launch traced here: 375 us
  Pallas kernels  356 us (94%)
  other arithmetic  9.92 us (3%)
  local copies, waits for them, and re-layouts  7.31 us (2%)
    pallas_call x1, Pallas kernels, backward_call(): pl.pallas_call(functools.partial(backward_kernel, cfg), out_shape=outs, i...  195 us
    pallas_call x1, Pallas kernels, forward_call(): pl.pallas_call(functools.partial(forward_kernel, cfg), out_shape=outs, in...  161 us

profile of v4, /device:TPU:0, one launch (start us, length us, event | category | flops | bytes accessed | tf_op | source)
XLA Modules:
  0.0 374.5 jit_solution(5175940625570583417)
XLA Ops:
  0.7 0.1 tile.17
  0.8 0.6 tile.18.refs_3_.refs_18_
  1.4 0.7 scatter.6
  2.0 0.7 scatter.9.refs_4_
  2.7 0.0 copy-start.4
  2.7 0.6 copy-done.4
  3.3 161.0 %attention_forward.1 = (bf16[2048,4096]{1,0:T(8,128)(2,1)}, bf16[2048,2048]{1,0:T(8,128)(2,1)}, bf16[2048,768]{1,0:T(8,128)(2,1)}, bf16[512,2048]{1,0:T(8,128)(2...) custom-call(bf16[512,2048]{1,0:T(8,128)(2,1)} %refs_15_.1, ...), custom_call_target="tpu_custom_call" | custom-call | tf_op jit(solution)/shard_map/attention_forward/pallas_call | solution.py:982
  164.4 195.4 %backward.1 = (bf16[2,256,2048]{2,1,0:T(8,128)(2,1)}, bf16[2,256,2048]{2,1,0:T(8,128)(2,1)}, bf16[3,2048,256]{2,1,0:T(8,128)(2,1)}, bf16[3,256,4096]{2,1,0:T(8,1...) custom-call(bf16[2,256,2048]{2,1,0:T(8,128)(2,1)} %get-tuple-element.57.refs_0_, ...), custom_call_target="tpu_custom_call" | custom-call | tf_op jit(solution)/shard_map/backward/pallas_call | solution.py:1496
  359.8 0.0 copy-start.3
  359.8 1.4 fusion.1
  361.1 2.1 convert_reduce_fusion.4
  363.2 0.0 copy-done.3
  363.2 0.0 copy-start
  363.2 0.2 convert_reduce_fusion.3
  363.4 0.0 copy-start.1
  363.4 0.7 fusion
  364.1 0.0 slice-start
  364.1 0.9 slice.57
  365.0 0.3 copy-done
  365.3 0.0 slice-start.1
  365.3 1.7 convert_reduce_fusion
  367.1 0.0 copy-done.1
  367.1 2.7 bitcast_convert_fusion
  369.7 0.0 slice-done
  369.7 0.0 slice-done.1
  369.8 0.0 copy-start.2
  369.8 3.2 convert_reduce_fusion.1
  373.0 0.0 copy-done.2
  373.0 1.3 copy.25
  (3 shorter events, 0.0 us)
Async XLA Ops:
  2.7 0.6 copy-start.4
  359.8 3.5 copy-start.3
  363.2 2.1 copy-start
  363.4 3.7 copy-start.1
  364.1 5.6 %slice-start = ((s8[6291456]{0:T(1024)(128)(4,1)}), s8[4194304]{0:T(1024)(128)(4,1)S(1)}, s32[]{:S(2)}) async-start(s8[6291456]{0:T(1024)(128)(4,1)} %bitcast.8), calls=%async_computation | async-start | bytes 8388608
  365.3 4.4 %slice-start.1 = ((s8[6291456]{0:T(1024)(128)(4,1)}), s8[2097152]{0:T(1024)(128)(4,1)S(1)}, s32[]{:S(2)}) async-start(s8[6291456]{0:T(1024)(128)(4,1)} %bitcast.8), calls=%async_computation.1 | async-start | bytes 4194304
  369.8 3.2 copy-start.2

commit v5 on v4

--- a/solution.py
+++ b/solution.py
@@ -3,6 +3,7 @@
 
 import jax
 import jax.numpy as jnp
+import numpy as np
 from jax import lax
 from jax.experimental import pallas as pl
 from jax.experimental.pallas import tpu as pltpu
@@ -27,14 +28,13 @@
 
 
 def frequencies():
-    exponent = jnp.arange(0, HD, 2).astype(jnp.float32) / HD
-    initial = 1.0 / 500000.0**exponent
-    wavelength = 2.0 * math.pi / initial
-    smoothing = (8192.0 / wavelength - 1.0) / 3.0
-    blended = (1.0 - smoothing) * initial / 32.0 + smoothing * initial
-    return jnp.where(
-        wavelength < 2048.0, initial, jnp.where(wavelength > 8192.0, initial / 32.0, blended)
-    )
+    exponent = np.arange(0, HD, 2).astype(np.float32) / np.float32(HD)
+    initial = np.float32(1.0) / np.float32(500000.0) ** exponent
+    wavelength = np.float32(2.0 * math.pi) / initial
+    smoothing = (np.float32(8192.0) / wavelength - np.float32(1.0)) / np.float32(3.0)
+    low = initial / np.float32(32.0)
+    blended = (np.float32(1.0) - smoothing) * low + smoothing * initial
+    return np.where(wavelength < 2048.0, initial, np.where(wavelength > 8192.0, low, blended))
 
 
 def aligned(index, size):
@@ -509,15 +509,15 @@
 
 def forward_kernel(cfg, *refs):
     (
-        x_in, dy_in, lengths, freq, gains_in, wq_in, wk_in, wv_in, wo_in, wg_in, wu_in, wd_in,
+        x_in, dy_in, lengths, freq, gain_a_in, gain_m_in, wq_in, wk_in, wv_in, wo_in, wg_in, wu_in, wd_in,
         gu_full, wd_full,
         qkv_out, wo_out, gains_out, normed_out, q_out, k_out, v_out, mixed_out, hidden_out,
         n2_all, dy_all, act_all, dgu_all, dn2_out, terms_out,
-        x, wq, wk, wv, wo, wraw, wd, gains32,
+        x, wq, wk, wv, wo, wraw, wd, gain_a, gain_m,
         sqkv, swo, sgu, swd, sgains,
         wqkv, wout, gains, normed, rscale, cosine, sine, bias,
         qh, kh, vh, kv, kv_in, mixed, part, inbox, result, hidden,
-        gu_buffer, wd_buffer, act, dgu, dn2_sum, terms_sum,
+        gu_buffer, wd_buffer, act, dgu, dn2_sum, terms_sum, backs,
         load, store, kv_send, kv_receive, fill, spill, swap_send, swap_receive,
         chunk_send, chunk_receive, *sems,
     ) = refs
@@ -525,8 +525,7 @@
     tokens, width = x.shape
     heads, groups = cfg.heads, cfg.groups
     query_width, key_width = cfg.query_width, cfg.key_width
-    units, chunks = cfg.hidden_units, cfg.chunks
-    chunk = units // chunks
+    units, chunks = cfg.hidden_units, len(cfg.chunks)
     block, owners = cfg.block, cfg.dp
     loads = []
 
@@ -538,7 +537,9 @@
 
     small = [
         fetch(source, target)
-        for source, target in ((gains_in, gains32), (wq_in, wq), (wk_in, wk), (wv_in, wv))
+        for source, target in (
+            (gain_a_in, gain_a), (gain_m_in, gain_m), (wq_in, wq), (wk_in, wk), (wv_in, wv)
+        )
     ]
     load_x, load_wo = fetch(x_in, x), fetch(wo_in, wo)
     load_wg, load_wd = fetch(wg_in, wraw), fetch(wd_in, wd)
@@ -555,15 +556,17 @@
     g_qkv = gather(sqkv, wqkv, 0)
     g_wo = gather(swo, wout, 1)
     g_gu, g_wd = [], []
-    for i in range(chunks):
-        columns = pl.ds(i * 2 * chunk, 2 * chunk)
+    for start, count in cfg.chunks:
+        columns = pl.ds(2 * start, 2 * count)
         g_gu.append(gather(sgu.at[:, columns], gu_full.at[:, columns], 0))
-        rows = pl.ds(i * chunk, chunk)
+        rows = pl.ds(start, count)
         g_wd.append(gather(swd.at[rows], wd_full.at[rows], 1))
     line_sems = sems[n_sems * len(gathers) :]
     for copy in small:
         copy.wait()
-    sgains[...] = gains32[...].astype(BF16)
+    sgains[...] = jnp.zeros_like(sgains)
+    sgains[0:1] = gain_a[...].astype(BF16)
+    sgains[1:2] = gain_m[...].astype(BF16)
     sqkv[:, :query_width] = wq[...].astype(BF16)
     sqkv[:, query_width : query_width + key_width] = wk[...].astype(BF16)
     sqkv[:, query_width + key_width :] = wv[...].astype(BF16)
@@ -574,9 +577,9 @@
     swo[...] = wo[...].astype(BF16)
 
     def stage(second):
-        for i in range(chunks):
-            first = (2 * i + second) * chunk
-            sgu[:, first : first + chunk] = wraw[:, i * chunk : (i + 1) * chunk].astype(BF16)
+        for start, count in cfg.chunks:
+            first = 2 * start + second * count
+            sgu[:, first : first + count] = wraw[:, start : start + count].astype(BF16)
 
     load_wg.wait()
     stage(0)
@@ -602,8 +605,8 @@
             load_wu.wait()
             stage(1)
             load_wd.wait()
-            for i in range(chunks):
-                rows = pl.ds(i * chunk, chunk)
+            for start, count in cfg.chunks:
+                rows = pl.ds(start, count)
                 swd[rows] = wd[rows].astype(BF16)
     g_gains.finish()
 
@@ -751,18 +754,54 @@
     for q in range(owners):
         swap(dy, dy_all, 0, q, tokens, 0)
 
-    agenda = [(2, advance, 0, 0), (2, begin, 2), (9, advance, 1, 0), (9, begin, 3)]
-    if not place.bits:
-        agenda = [item for item in agenda if item[1] is begin]
+    def chunk_load(i):
+        slot = i % 2
+        start, count = cfg.chunks[i]
+        return [
+            pltpu.make_async_copy(
+                gu_full.at[:, pl.ds(2 * start, 2 * count)],
+                gu_buffer.at[slot, :, pl.ds(0, 2 * count)],
+                spill.at[slot, 0],
+            ),
+            pltpu.make_async_copy(
+                wd_full.at[pl.ds(start, count)],
+                wd_buffer.at[slot, pl.ds(0, count)],
+                spill.at[slot, 1],
+            ),
+        ]
+
+    def take(i):
+        g_gu[i].finish()
+        g_wd[i].finish()
+        for copy in chunk_load(i):
+            copy.start()
+
+    def from_output(i):
+        for copy in chunk_load(i):
+            copy.wait()
+        return dot(dy[...], wd_buffer[i % 2, : cfg.chunks[i][1]], NT)
+
+    def from_output_early(i):
+        backs[i] = from_output(i)
+
+    later = range(1, place.bits)
+    agenda = []
+    if place.bits:
+        agenda.append((2, advance, 0, 0))
+    agenda.append((2, begin, 2))
+    if place.bits:
+        agenda.append((cfg.marks[0], advance, 1, 0))
+    agenda += [(cfg.marks[0], begin, 3), (cfg.marks[0], begin, 4)]
+    agenda += [(cfg.marks[1], advance, 0, phase) for phase in later]
+    agenda += [(cfg.marks[1], take, 0), (cfg.marks[2], from_output_early, 0)]
+    agenda += [(cfg.marks[3], advance, 1, phase) for phase in later]
+    agenda += [(cfg.marks[3], take, 1)]
     at = 0
     for mark, action, *rest in agenda:
         line.run(at, mark)
         action(*rest)
         at = mark
     line.run(at, line.rounds)
-    for i in range(2):
-        for phase in range(1, place.bits):
-            advance(i, phase)
     if place.bits:
         advance(2, 0)
     for b in range(2):
@@ -770,38 +809,22 @@
             swap(result.at[b], n2_all, 1 + b, q, QROWS, b * QROWS)
     keep(hidden, hidden_out)
 
-    def chunk_load(i):
-        slot = i % 2
-        return [
-            pltpu.make_async_copy(
-                gu_full.at[:, pl.ds(i * 2 * chunk, 2 * chunk)], gu_buffer.at[slot], spill.at[slot, 0]
-            ),
-            pltpu.make_async_copy(
-                wd_full.at[pl.ds(i * chunk, chunk)], wd_buffer.at[slot], spill.at[slot, 1]
-            ),
-        ]
-
-    def take(i):
-        g_gu[i].finish()
-        g_wd[i].finish()
-        for copy in chunk_load(i):
-            copy.start()
-
     def give(i):
         slot = i % 2
-        act_columns, dgu_columns = pl.ds(i * chunk, chunk), pl.ds(i * 2 * chunk, 2 * chunk)
+        start, count = cfg.chunks[i]
         copies = []
-        for k, (source, target, columns) in enumerate(
-            ((act, act_all, act_columns), (dgu, dgu_all, dgu_columns))
+        for k, (source, target, first, wide) in enumerate(
+            ((act, act_all, start, count), (dgu, dgu_all, 2 * start, 2 * count))
         ):
+            source, columns = source.at[slot, :, pl.ds(0, wide)], pl.ds(first, wide)
             copies.append(
                 pltpu.make_async_copy(
-                    source.at[slot], target.at[pl.ds(0, tokens), columns], spill.at[slot, 2 + k]
+                    source, target.at[pl.ds(0, tokens), columns], spill.at[slot, 2 + k]
                 )
             )
             copies.append(
                 remote(
-                    source.at[slot],
+                    source,
                     target.at[pl.ds(tokens, tokens), columns],
                     chunk_send.at[i, k],
                     chunk_receive.at[i, k],
@@ -811,15 +834,9 @@
         return copies
 
     tile = width // 4
-    n2 = result[...].reshape(tokens, width)
-    take(0)
     for i in range(chunks):
         slot = i % 2
-        for copy in chunk_load(i):
-            copy.wait()
-        if i + 1 < chunks:
-            if i == 0:
-                take(1)
+        count = cfg.chunks[i][1]
         if i >= 2:
             own_act, sent_act, own_dgu, sent_dgu = give(i - 2)
             own_act.wait()
@@ -827,23 +844,23 @@
             sent_act.wait_send()
             sent_dgu.wait_send()
         n2 = result[...].reshape(tokens, width)
-        both = dot(n2, gu_buffer[slot])
-        back = dot(dy[...], wd_buffer[slot], NT)
-        gate, upward = both[:, :chunk], both[:, chunk:]
+        back = backs[0] if i == 0 else from_output(i)
+        both = dot(n2, gu_buffer[slot, :, : 2 * count])
+        gate, upward = both[:, :count], both[:, count:]
         sigmoid = 1.0 / (1.0 + jnp.exp(-gate))
         swish = gate * sigmoid
-        act[slot] = (swish * upward).astype(BF16)
-        dgu[slot, :, :chunk] = (
+        act[slot, :, :count] = (swish * upward).astype(BF16)
+        dgu[slot, :, :count] = (
             back * upward * sigmoid * (1.0 + gate * (1.0 - sigmoid))
         ).astype(BF16)
-        dgu[slot, :, chunk:] = (back * swish).astype(BF16)
+        dgu[slot, :, count : 2 * count] = (back * swish).astype(BF16)
         for copy in give(i):
             copy.start()
 
-        def add(n, carry, i=i, slot=slot):
+        def add(n, carry, i=i, slot=slot, count=count):
             columns = aligned(n, tile)
-            more = dot(dgu[slot], gu_buffer[slot, columns], NT)
-            terms = dot(act[slot], wd_buffer[slot, :, columns])
+            more = dot(dgu[slot, :, : 2 * count], gu_buffer[slot, columns, : 2 * count], NT)
+            terms = dot(act[slot, :, :count], wd_buffer[slot, :count, columns])
             if i:
                 more = more + dn2_sum[:, columns]
                 terms = terms + terms_sum[:, columns]
@@ -859,10 +876,12 @@
         if i + 1 == chunks:
             line.drain()
         lax.fori_loop(0, 4, add, 0)
+        if i == 0 and place.bits:
+            advance(3, 0)
+        if i == 1 and place.bits:
+            advance(4, 0)
         if 2 <= i + 1 < chunks:
-            if i + 2 < chunks and place.bits:
-                advance(i + 2, 0)
-            for phase in range(1, place.bits):
+            for phase in later:
                 advance(i + 1, phase)
             take(i + 1)
     keep(part, dn2_out)
@@ -898,9 +917,11 @@
         self.dp, self.tensor, self.tokens, self.width = dp, tensor, tokens, width
         self.heads, self.groups, self.hidden_units = heads, groups, hidden_units
         self.pieces = 8
-        self.chunks = 4
+        eighth = hidden_units // 8
+        self.chunks = [(2 * n * eighth, 2 * eighth) for n in range(3)]
+        self.chunks += [(6 * eighth, eighth), (7 * eighth, eighth)]
         self.behind = 12
-        self.marks = (4, 4, 11)
+        self.marks = (7, 10, 12, 13)
         self.query_width, self.key_width = heads * HD, groups * HD
         self.qkv_width = self.query_width + 2 * self.key_width
         self.blocks = dp * 2
@@ -908,12 +929,12 @@
         self.window = WINDOW + QROWS
 
 
-def forward_call(cfg, x, dy, lengths, freq, gains, wq, wk, wv, wo, wg, wu, wd):
+def forward_call(cfg, x, dy, lengths, freq, gain_a, gain_m, wq, wk, wv, wo, wg, wu, wd):
     tokens, width, units = cfg.tokens, cfg.width, cfg.hidden_units
     any_spec = pl.BlockSpec(memory_space=pl.ANY)
     shape = jax.ShapeDtypeStruct
     mine = cfg.dp * cfg.block
-    chunk = units // cfg.chunks
+    chunk = max(count for _, count in cfg.chunks)
     outs = [
         shape((width, 2 * units), BF16),
         shape((units, width), BF16),
@@ -934,12 +955,12 @@
         shape((2, QROWS, width), BF16),
     ]
     scratch = [pltpu.VMEM(x.shape, BF16)]
-    scratch += [pltpu.VMEM(w.shape, F32) for w in (wq, wk, wv, wo, wg, wd, gains)]
+    scratch += [pltpu.VMEM(w.shape, F32) for w in (wq, wk, wv, wo, wg, wd, gain_a, gain_m)]
     scratch += [pltpu.VMEM((wq.shape[0], cfg.qkv_width), BF16)]
     scratch += [pltpu.VMEM(wo.shape, BF16)]
     scratch += [pltpu.VMEM((wg.shape[0], 2 * units), BF16)]
     scratch += [pltpu.VMEM(wd.shape, BF16)]
-    scratch += [pltpu.VMEM(gains.shape, BF16)]
+    scratch += [pltpu.VMEM((16, gain_a.shape[1]), BF16)]
     scratch += [
         pltpu.VMEM((width, cfg.qkv_width), BF16),
         pltpu.VMEM((cfg.query_width, width), BF16),
@@ -965,7 +986,8 @@
         pltpu.VMEM((2, tokens, 2 * chunk), BF16),
         pltpu.VMEM((tokens, width), F32),
         pltpu.VMEM((tokens, width), F32),
-        pltpu.SemaphoreType.DMA((10,)),
+        pltpu.VMEM((1, tokens, chunk), F32),
+        pltpu.SemaphoreType.DMA((11,)),
         pltpu.SemaphoreType.DMA((14,)),
         pltpu.SemaphoreType.DMA((1,)),
         pltpu.SemaphoreType.DMA((1,)),
@@ -973,10 +995,10 @@
         pltpu.SemaphoreType.DMA((2, 4)),
         pltpu.SemaphoreType.DMA((3, cfg.dp)),
         pltpu.SemaphoreType.DMA((3, cfg.dp)),
-        pltpu.SemaphoreType.DMA((cfg.chunks, 2)),
-        pltpu.SemaphoreType.DMA((cfg.chunks, 2)),
+        pltpu.SemaphoreType.DMA((len(cfg.chunks), 2)),
+        pltpu.SemaphoreType.DMA((len(cfg.chunks), 2)),
     ]
-    for halves in [1] + [2] * (2 + 2 * cfg.chunks):
+    for halves in [1] + [2] * (2 + 2 * len(cfg.chunks)):
         scratch += Gather.semaphores(cfg.dp, halves)
     scratch += LineSum.semaphores(cfg.pieces)
     return pl.pallas_call(
@@ -988,14 +1010,14 @@
             pl.BlockSpec(memory_space=pltpu.SMEM),
             pl.BlockSpec(memory_space=pltpu.VMEM),
         ]
-        + [any_spec] * 8,
+        + [any_spec] * 9,
         out_specs=[any_spec] * len(outs),
         scratch_shapes=scratch,
         compiler_params=pltpu.CompilerParams(
             collective_id=1, has_side_effects=True, vmem_limit_bytes=VMEM_LIMIT
         ),
         name="attention_forward",
-    )(x, dy, lengths, freq, gains, wq, wk, wv, wo, wg, wu, wd)
+    )(x, dy, lengths, freq, gain_a, gain_m, wq, wk, wv, wo, wg, wu, wd)
 
 
 def backward_kernel(cfg, *refs):
@@ -1016,7 +1038,7 @@
     heads, groups = cfg.heads, cfg.groups
     query_width, key_width, qkv_width = cfg.query_width, cfg.key_width, cfg.qkv_width
     units = act.shape[1]
-    chunk = units // cfg.chunks
+    chunk = units // 4
     block, owners = cfg.block, cfg.dp
     mine = owners * block
     spare = list(sems[3 * 4 + 4 * 3 :])
@@ -1120,8 +1142,16 @@
         down[rows] = dot(act[:, rows], dy_all[...], TN).astype(BF16)
 
     def grad_gate_up(i):
-        target = aligned(lax.rem(i, 2) * cfg.chunks + lax.div(i, 2), chunk)
-        gu_rows[:, target] = dot(n2_all[...], dgu[:, aligned(i, chunk)], TN).astype(BF16)
+        product = dot(n2_all[...], dgu[:, aligned(i, chunk)], TN).astype(BF16)
+
+        @pl.when(i < 6)
+        def _():
+            gu_rows[:, aligned(lax.rem(i, 2) * 4 + lax.div(i, 2), chunk)] = product
+
+        @pl.when(i >= 6)
+        def _():
+            gu_rows[:, aligned(i, chunk // 2)] = product[:, : chunk // 2]
+            gu_rows[:, aligned(8 + i, chunk // 2)] = product[:, chunk // 2 :]
 
     def lines(n):
         line_three.round(n)
@@ -1523,13 +1553,13 @@
             w_key.shape[1] // HD,
             w_gate.shape[1],
         )
-        freq = jnp.tile(frequencies(), (8, 4))
-        gains = jnp.zeros((16, gain_attn.shape[0]), F32).at[0].set(gain_attn).at[1].set(gain_mlp)
+        freq = jnp.asarray(np.tile(frequencies(), (8, 4)), F32)
+        gains = (gain_attn.reshape(1, -1), gain_mlp.reshape(1, -1))
         (
             _, _, wqkv, wo, gains_full, normed, q, k, v, mixed, hidden,
             n2_all, dy_all, act_all, dgu_all, dn2, terms,
         ) = forward_call(
-            cfg, inputs, cotangent, doc_lengths, freq, gains,
+            cfg, inputs, cotangent, doc_lengths, freq, *gains,
             w_query, w_key, w_value, w_out, w_gate, w_up, w_down,
         )
         (

time: 380 us -> 374 us (0.984)
    pallas_call x1, Pallas kernels: 195 us -> 190 us  [backward_call(): pl.pallas_call(functools.partial(backward_kernel, cfg), out_shape=outs, i...]
where the time goes in v5:
time: 374 us; the launch traced here: 369 us
  Pallas kernels  353 us (94%)
  other arithmetic  9.9 us (3%)
  local copies, waits for them, and re-layouts  4.64 us (1%)
    pallas_call x1, Pallas kernels, backward_call(): pl.pallas_call(functools.partial(backward_kernel, cfg), out_shape=outs, i...  190 us
    pallas_call x1, Pallas kernels, forward_call(): pl.pallas_call(functools.partial(forward_kernel, cfg), out_shape=outs, in...  163 us

profile of v5, /device:TPU:0, one launch (start us, length us, event | category | flops | bytes accessed | tf_op | source)
XLA Modules:
  0.0 368.5 jit_solution(3617855492371548168)
XLA Ops:
  0.6 162.8 %attention_forward.1 = (bf16[2048,4096]{1,0:T(8,128)(2,1)}, bf16[2048,2048]{1,0:T(8,128)(2,1)}, bf16[2048,768]{1,0:T(8,128)(2,1)}, bf16[512,2048]{1,0:T(8,128)(2...) custom-call(bf16[512,2048]{1,0:T(8,128)(2,1)} %refs_15_.1, ...), custom_call_target="tpu_custom_call" | custom-call | tf_op jit(solution)/shard_map/attention_forward/pallas_call | solution.py:1004
  163.4 190.3 %backward.1 = (bf16[2,256,2048]{2,1,0:T(8,128)(2,1)}, bf16[2,256,2048]{2,1,0:T(8,128)(2,1)}, bf16[3,2048,256]{2,1,0:T(8,128)(2,1)}, bf16[3,256,4096]{2,1,0:T(8,1...) custom-call(bf16[2,256,2048]{2,1,0:T(8,128)(2,1)} %get-tuple-element.33.refs_0_, ...), custom_call_target="tpu_custom_call" | custom-call | tf_op jit(solution)/shard_map/backward/pallas_call | solution.py:1526
  353.7 0.0 copy-start.3
  353.7 1.4 fusion.1
  355.1 2.1 convert_reduce_fusion.4
  357.2 0.0 copy-done.3
  357.2 0.0 copy-start
  357.2 0.2 convert_reduce_fusion.3
  357.4 0.0 copy-start.1
  357.4 0.7 fusion
  358.1 0.0 slice-start
  358.1 0.9 slice.28
  359.0 0.3 copy-done
  359.3 0.0 slice-start.1
  359.3 1.7 convert_reduce_fusion
  361.0 0.0 copy-done.1
  361.0 2.7 bitcast_convert_fusion
  363.7 0.0 slice-done
  363.7 0.0 slice-done.1
  363.7 0.0 copy-start.2
  363.7 3.2 convert_reduce_fusion.1
  367.0 0.0 copy-done.2
  367.0 1.3 copy.25
  (1 shorter events, 0.0 us)
Async XLA Ops:
  353.7 3.5 copy-start.3
  357.2 2.1 copy-start
  357.4 3.7 copy-start.1
  358.1 5.6 %slice-start = ((s8[6291456]{0:T(1024)(128)(4,1)}), s8[4194304]{0:T(1024)(128)(4,1)S(1)}, s32[]{:S(2)}) async-start(s8[6291456]{0:T(1024)(128)(4,1)} %bitcast.8), calls=%async_computation | async-start | bytes 8388608
  359.3 4.4 %slice-start.1 = ((s8[6291456]{0:T(1024)(128)(4,1)}), s8[2097152]{0:T(1024)(128)(4,1)S(1)}, s32[]{:S(2)}) async-start(s8[6291456]{0:T(1024)(128)(4,1)} %bitcast.8), calls=%async_computation.1 | async-start | bytes 4194304
  363.7 3.2 copy-start.2

commit v6 on v5

--- a/solution.py
+++ b/solution.py
@@ -1157,13 +1157,13 @@
         line_three.round(n)
         line_two.round(n - cfg.behind)
 
-    def between(fill, rounds, fills):
+    def between(fill, rounds, fills, count=4):
         def one(i, carry):
             lines(rounds + i)
             fill(fills + i)
             return carry
 
-        lax.fori_loop(0, 4, one, 0)
+        lax.fori_loop(0, count, one, 0)
 
     for copy in first:
         copy.wait()
@@ -1174,8 +1174,9 @@
     for copy in second + third:
         copy.wait()
     between(grad_gate_up, 4, 0)
-    between(grad_gate_up, 8, 4)
+    between(grad_gate_up, 8, 4, 3)
     line_two.early_start()
+    between(grad_gate_up, 11, 7, 1)
     pl.semaphore_signal(ready, inc=1, device_id=place.core, device_id_type=MESH)
     rest = [
         fetch(wo_in, wo),

time: 374 us -> 373 us (level)
  no operation moved by 1% of the time
where the time goes in v6:
time: 373 us; the launch traced here: 367 us
  Pallas kernels  352 us (94%)
  other arithmetic  9.9 us (3%)
  local copies, waits for them, and re-layouts  4.64 us (1%)
    pallas_call x1, Pallas kernels, backward_call(): pl.pallas_call(functools.partial(backward_kernel, cfg), out_shape=outs, i...  189 us
    pallas_call x1, Pallas kernels, forward_call(): pl.pallas_call(functools.partial(forward_kernel, cfg), out_shape=outs, in...  163 us

profile of v6, /device:TPU:0, one launch (start us, length us, event | category | flops | bytes accessed | tf_op | source)
XLA Modules:
  0.0 367.3 jit_solution(3388907203860927338)
XLA Ops:
  0.6 162.6 %attention_forward.1 = (bf16[2048,4096]{1,0:T(8,128)(2,1)}, bf16[2048,2048]{1,0:T(8,128)(2,1)}, bf16[2048,768]{1,0:T(8,128)(2,1)}, bf16[512,2048]{1,0:T(8,128)(2...) custom-call(bf16[512,2048]{1,0:T(8,128)(2,1)} %refs_15_.1, ...), custom_call_target="tpu_custom_call" | custom-call | tf_op jit(solution)/shard_map/attention_forward/pallas_call | solution.py:1004
  163.2 189.3 %backward.1 = (bf16[2,256,2048]{2,1,0:T(8,128)(2,1)}, bf16[2,256,2048]{2,1,0:T(8,128)(2,1)}, bf16[3,2048,256]{2,1,0:T(8,128)(2,1)}, bf16[3,256,4096]{2,1,0:T(8,1...) custom-call(bf16[2,256,2048]{2,1,0:T(8,128)(2,1)} %get-tuple-element.33.refs_0_, ...), custom_call_target="tpu_custom_call" | custom-call | tf_op jit(solution)/shard_map/backward/pallas_call | solution.py:1527
  352.5 0.0 copy-start.3
  352.5 1.4 fusion.1
  353.9 2.1 convert_reduce_fusion.4
  356.0 0.0 copy-done.3
  356.0 0.0 copy-start
  356.0 0.2 convert_reduce_fusion.3
  356.2 0.0 copy-start.1
  356.2 0.7 fusion
  356.9 0.0 slice-start
  356.9 0.9 slice.28
  357.8 0.3 copy-done
  358.1 0.0 slice-start.1
  358.1 1.7 convert_reduce_fusion
  359.8 0.0 copy-done.1
  359.8 2.7 bitcast_convert_fusion
  362.5 0.0 slice-done
  362.5 0.0 slice-done.1
  362.5 0.0 copy-start.2
  362.5 3.2 convert_reduce_fusion.1
  365.8 0.0 copy-done.2
  365.8 1.3 copy.25
  (1 shorter events, 0.0 us)
Async XLA Ops:
  352.5 3.5 copy-start.3
  356.0 2.1 copy-start
  356.2 3.7 copy-start.1
  356.9 5.6 %slice-start = ((s8[6291456]{0:T(1024)(128)(4,1)}), s8[4194304]{0:T(1024)(128)(4,1)S(1)}, s32[]{:S(2)}) async-start(s8[6291456]{0:T(1024)(128)(4,1)} %bitcast.8), calls=%async_computation | async-start | bytes 8388608
  358.1 4.4 %slice-start.1 = ((s8[6291456]{0:T(1024)(128)(4,1)}), s8[2097152]{0:T(1024)(128)(4,1)S(1)}, s32[]{:S(2)}) async-start(s8[6291456]{0:T(1024)(128)(4,1)} %bitcast.8), calls=%async_computation.1 | async-start | bytes 4194304
  362.5 3.2 copy-start.2
